TPU v7x, 32 devices: a whole 2x2x4 slice. The times are simulated.
32 devices in a mesh: wide: 8 (over y, x, core), narrow: 4 (over z).
Axes of the slice: x: 2, y: 2, z: 4, core: 2. Of those that a mesh axis runs over, the one named last changes fastest.
Arguments:
- tokens: bfloat16 [100352, 384], P(('wide', 'narrow')), may hold values from -6 to 6
- grid_sizes: int32 [128], P('wide'), may hold values from 14 to 24, as said below
- cotangent: bfloat16 [100352, 384], P(('wide', 'narrow')), may hold values from -6 to 6
- attn_weight: float32 [384, 1536], replicated
- attn_first: float32 [384, 1536], replicated, may hold values from -512 to 512
- attn_second: float32 [384, 1536], replicated, may hold values from 9031.68 to 36126.72
- rel_table: float32 [169, 12], replicated, may hold values from -4 to 4
- table_first: float32 [169, 12], replicated, may hold values from -96 to 96
- table_second: float32 [169, 12], replicated, may hold values from 250.88 to 1003.52
- vectors: float32 [8, 384], replicated
- vector_first: float32 [8, 384], replicated, may hold values from -2048 to 2048
- vector_second: float32 [8, 384], replicated, may hold values from 100352 to 401408
- mlp_weight: float32 [2, 1536, 384], P(None, 'narrow')
- mlp_first: float32 [2, 1536, 384], P(None, 'narrow'), may hold values from -512 to 512
- mlp_second: float32 [2, 1536, 384], P(None, 'narrow'), may hold values from 6272 to 25088
- mlp_bias: float32 [1536], P('narrow'), may hold values from -1.5 to 1.5
- bias_first: float32 [1536], P('narrow'), may hold values from -512 to 512
- bias_second: float32 [1536], P('narrow'), may hold values from 6272 to 25088
Outputs:
- outputs: bfloat16 [100352, 384], P(('wide', 'narrow'))
- input_grad: float32 [100352, 384], P(('wide', 'narrow'))
- rms_values: float32 [3], replicated
- attn_new: float32 [384, 1536], replicated
- attn_low: bfloat16 [384, 1536], replicated
- attn_first_new: float32 [384, 1536], replicated
- attn_second_new: float32 [384, 1536], replicated
- table_new: float32 [169, 12], replicated
- table_first_new: float32 [169, 12], replicated
- table_second_new: float32 [169, 12], replicated
- vector_new: float32 [8, 384], replicated
- vector_first_new: float32 [8, 384], replicated
- vector_second_new: float32 [8, 384], replicated
- mlp_new: float32 [2, 1536, 384], P(None, 'narrow')
- mlp_low: bfloat16 [2, 1536, 384], P(None, 'narrow')
- mlp_first_new: float32 [2, 1536, 384], P(None, 'narrow')
- mlp_second_new: float32 [2, 1536, 384], P(None, 'narrow')
- bias_new: float32 [1536], P('narrow')
- bias_first_new: float32 [1536], P('narrow')
- bias_second_new: float32 [1536], P('narrow')
Inputs may be any that keep to these rules, and one draw needn't show every extreme that they name: `grid_sizes`: each entry is 14 or 24; the first image has 14, and the last image of each group of 16 has 24.
All inputs are finite; a program needn't handle non-finite values.
Results may differ from a plain program's by a relative error of at most 0.0055.
The roundings to bfloat16 on the way count: a program that leaves them out, or rounds other values in their place, can miss the bound.
Values may be sent and summed in bfloat16 or wider, within the bound.
A program may use at most 256 MiB of HBM per device.

v0:
```python
import jax
import jax.numpy as jnp
from jax import lax
from jax.sharding import PartitionSpec as P

WIN = 7
PAD_GRID = 28
STEP = 5
IMG_W = 16
WTOK = 49
WPI = 16


norm_eps = 1e-05
mask_fill = -10000.0
beta_one = 0.5
beta_two = 0.5
adam_eps = 1e-08
highest = lax.Precision.HIGHEST


def norm_parts(tensor, gain_row, shift_row):
    centred = tensor - jnp.mean(tensor, -1, keepdims=True)
    inverse = lax.rsqrt(jnp.mean(centred * centred, -1, keepdims=True) + norm_eps)
    normal_x = centred * inverse
    return (normal_x * gain_row + shift_row, normal_x, inverse)


def norm_back(gradient, normal_x, inverse, gain_row):
    scaled = gradient * gain_row
    inner_mean = jnp.mean(scaled * normal_x, -1, keepdims=True)
    result = inverse * (scaled - jnp.mean(scaled, -1, keepdims=True) - normal_x * inner_mean)
    return (result, jnp.sum(gradient * normal_x, 0), jnp.sum(gradient, 0))


def times_trans(left, right):
    return lax.dot_general(
        left, right, (((1,), (1,)), ((), ())), preferred_element_type=jnp.float32
    )


def outer_sum(left, right):
    return lax.dot_general(
        left, right, (((0,), (0,)), ((), ())), preferred_element_type=jnp.float32
    )


def gelu_tanh(tensor):
    return jax.nn.gelu(tensor, approximate=True)


def relative_index():
    position = jnp.arange(WTOK)
    cell_row = position // WIN
    cell_col = position % WIN
    offset = (cell_row[:, None] - cell_row[None, :] + WIN - 1) * (2 * WIN - 1)
    return offset + cell_col[:, None] - cell_col[None, :] + WIN - 1


def window_mask(grid_sizes, first_win, win_total):
    group_windows = IMG_W * WPI
    windows = first_win + jnp.arange(win_total)
    local_win = windows % group_windows
    image_idx = windows // group_windows * IMG_W + local_win % IMG_W
    inner_win = WPI - 1 - local_win // IMG_W
    pick_table = (image_idx[:, None] == jnp.arange(grid_sizes.shape[0])[None, :]).astype(jnp.int32)
    grid_side = jnp.sum(pick_table * grid_sizes[None, :], 1)
    across = PAD_GRID // WIN
    position = jnp.arange(WTOK)
    cell_row = (inner_win // across)[:, None] * WIN + (position // WIN)[None, :]
    cell_col = (inner_win % across)[:, None] * WIN + (position % WIN)[None, :]
    inside = (cell_row < grid_side[:, None]) & (cell_col < grid_side[:, None])
    return inside.astype(jnp.float32).reshape(-1)


def adam_step(weight, gradient, first_old, second_old, rate_value, decay_value):
    first_new = beta_one * first_old + (1.0 - beta_one) * gradient
    second_new = beta_two * second_old + (1.0 - beta_two) * gradient * gradient
    fix_one = 1.0 - beta_one**STEP
    fix_two = 1.0 - beta_two**STEP
    update = rate_value * (first_new / fix_one) / (jnp.sqrt(second_new / fix_two) + adam_eps)
    return (weight - update - rate_value * decay_value * weight, first_new, second_new)


def shards(
    tokens,
    grid_sizes,
    cotangent,
    attn_weight,
    attn_first,
    attn_second,
    rel_table,
    table_first,
    table_second,
    vectors,
    vector_first,
    vector_second,
    mlp_weight,
    mlp_first,
    mlp_second,
    mlp_bias,
    bias_first,
    bias_second,
):
    row_count, model_width = tokens.shape
    head_count = rel_table.shape[1]
    head_size = model_width // head_count
    win_count = row_count // WTOK
    score_scale = head_size ** (-0.5)
    shaped = (win_count, WTOK, head_count, head_size)
    validity = window_mask(grid_sizes, lax.axis_index("narrow") * win_count, win_count)
    token_keep = validity[:, None]
    inputs = tokens.astype(jnp.float32)
    weight_low = attn_weight.astype(jnp.bfloat16)
    normed_one, normal_one, inverse_one = norm_parts(inputs, vectors[0], vectors[1])
    first_low = normed_one.astype(jnp.bfloat16)
    project = jnp.dot(
        first_low, weight_low[:, : 3 * model_width], preferred_element_type=jnp.float32
    )
    queries = (project[:, :model_width] + vectors[2]).astype(jnp.bfloat16).reshape(shaped)
    key_rows = project[:, model_width : 2 * model_width].astype(jnp.bfloat16).reshape(shaped)
    values = (
        (project[:, 2 * model_width : 3 * model_width] + vectors[3])
        .astype(jnp.bfloat16)
        .reshape(shaped)
    )
    one_hot = (
        relative_index()[:, :, None] == jnp.arange(rel_table.shape[0])[None, None, :]
    ).astype(jnp.float32)
    rel_bias = jnp.einsum("qkt,th->hqk", one_hot, rel_table, precision=highest)
    key_fill = ((1.0 - validity) * mask_fill).reshape(win_count, WTOK)

    def score_block():
        raw_scores = jnp.einsum(
            "wqhd,wkhd->whqk", queries, key_rows, preferred_element_type=jnp.float32
        )
        return raw_scores * score_scale + rel_bias[None] + key_fill[:, None, None, :]

    scores = score_block()
    row_top = jnp.max(scores, -1, keepdims=True)
    row_total = jnp.sum(jnp.exp(scores - row_top), -1, keepdims=True)
    attn_probs = jnp.exp(scores - row_top) / row_total
    probs_low = attn_probs.astype(jnp.bfloat16)
    mixed_heads = jnp.einsum(
        "whqk,wkhd->wqhd", probs_low, values, preferred_element_type=jnp.float32
    )
    mixed_low = mixed_heads.reshape(row_count, model_width).astype(jnp.bfloat16)
    attn_out = (
        jnp.dot(mixed_low, weight_low[:, 3 * model_width :], preferred_element_type=jnp.float32)
        + vectors[4]
    )
    attn_branch = attn_out * token_keep
    stream = inputs + attn_branch
    normed_two, normal_two, inverse_two = norm_parts(stream, vectors[5], vectors[6])
    second_low = normed_two.astype(jnp.bfloat16)
    hidden_low = mlp_weight.astype(jnp.bfloat16)
    grad_low = cotangent * validity.astype(jnp.bfloat16)[:, None]
    gathered = lax.all_gather(second_low, "narrow", axis=0, tiled=True)
    pre_act = times_trans(gathered, hidden_low[0]) + mlp_bias
    active = gelu_tanh(pre_act).astype(jnp.bfloat16)
    part_rows = active
    mlp_out = lax.psum_scatter(
        jnp.dot(part_rows, hidden_low[1], preferred_element_type=jnp.float32),
        "narrow",
        scatter_dimension=0,
        tiled=True,
    )
    grad_all = lax.all_gather(grad_low, "narrow", axis=0, tiled=True)
    grad_active = times_trans(grad_all, hidden_low[1])
    grad_pre = jax.vjp(gelu_tanh, pre_act)[1](grad_active)[0].astype(jnp.bfloat16)
    local_weight = jnp.stack([outer_sum(grad_pre, gathered), outer_sum(active, grad_all)])
    local_bias = jnp.sum(grad_pre.astype(jnp.float32), 0)
    part_rows = grad_pre
    grad_second = lax.psum_scatter(
        jnp.dot(part_rows, hidden_low[0], preferred_element_type=jnp.float32),
        "narrow",
        scatter_dimension=0,
        tiled=True,
    )
    mlp_branch = (mlp_out + vectors[7]) * token_keep
    outputs = (stream + mlp_branch).astype(jnp.bfloat16)
    local_stats = jnp.stack(
        [
            jnp.sum(inputs * inputs * token_keep),
            jnp.sum(attn_branch * attn_branch),
            jnp.sum(mlp_branch * mlp_branch),
            jnp.sum(validity),
        ]
    )
    stat_totals = lax.psum(local_stats, ("wide", "narrow"))
    grad_output = cotangent.astype(jnp.float32)
    out_bias_grad = jnp.sum(grad_output * token_keep, 0)
    stream_part, gain_two, shift_two = norm_back(grad_second, normal_two, inverse_two, vectors[5])
    grad_stream = grad_output + stream_part
    grad_attn = grad_stream * token_keep
    attn_bias_grad = jnp.sum(grad_attn, 0)
    grad_attn_low = grad_attn.astype(jnp.bfloat16)
    grad_proj_out = outer_sum(mixed_low, grad_attn_low)
    grad_mixed = (
        times_trans(grad_attn_low, weight_low[:, 3 * model_width :])
        .astype(jnp.bfloat16)
        .reshape(shaped)
    )
    scores = score_block()
    attn_probs = jnp.exp(scores - row_top) / row_total
    probs_low = attn_probs.astype(jnp.bfloat16)
    grad_values = jnp.einsum(
        "whqk,wqhd->wkhd", probs_low, grad_mixed, preferred_element_type=jnp.float32
    )
    grad_probs = jnp.einsum(
        "wqhd,wkhd->whqk", grad_mixed, values, preferred_element_type=jnp.float32
    )
    grad_scores = attn_probs * (grad_probs - jnp.sum(grad_probs * attn_probs, -1, keepdims=True))
    table_grad = jnp.einsum("qkt,hqk->th", one_hot, jnp.sum(grad_scores, 0), precision=highest)
    grad_raw = (grad_scores * score_scale).astype(jnp.bfloat16)
    grad_query = (
        jnp.einsum("whqk,wkhd->wqhd", grad_raw, key_rows, preferred_element_type=jnp.float32)
        .astype(jnp.bfloat16)
        .reshape(row_count, model_width)
    )
    grad_keys = (
        jnp.einsum("whqk,wqhd->wkhd", grad_raw, queries, preferred_element_type=jnp.float32)
        .astype(jnp.bfloat16)
        .reshape(row_count, model_width)
    )
    grad_vals = grad_values.astype(jnp.bfloat16).reshape(row_count, model_width)
    grad_proj = jnp.concatenate([grad_query, grad_keys, grad_vals], 1)
    grad_proj_in = outer_sum(first_low, grad_proj)
    grad_normed = times_trans(grad_proj, weight_low[:, : 3 * model_width])
    input_part, gain_one, shift_one = norm_back(grad_normed, normal_one, inverse_one, vectors[0])
    input_grad = grad_stream + input_part
    attn_grad = jnp.concatenate([grad_proj_in, grad_proj_out], 1)
    vector_grad = jnp.stack(
        [
            gain_one,
            shift_one,
            jnp.sum(grad_query.astype(jnp.float32), 0),
            jnp.sum(grad_vals.astype(jnp.float32), 0),
            attn_bias_grad,
            gain_two,
            shift_two,
            out_bias_grad,
        ]
    )
    attn_grad, table_grad, vector_grad = lax.psum(
        (attn_grad, table_grad, vector_grad), ("wide", "narrow")
    )
    weight_grad, hidden_bias_grad = lax.psum((local_weight, local_bias), "wide")
    rms_values = jnp.sqrt(stat_totals[:3] / (stat_totals[3] * model_width))
    attn_new, attn_first_new, attn_second_new = adam_step(
        attn_weight, attn_grad, attn_first, attn_second, 0.02, 0.05
    )
    table_new, table_first_new, table_second_new = adam_step(
        rel_table, table_grad, table_first, table_second, 0.3, 0.0
    )
    vector_new, vector_first_new, vector_second_new = adam_step(
        vectors, vector_grad, vector_first, vector_second, 0.3, 0.0
    )
    mlp_new, mlp_first_new, mlp_second_new = adam_step(
        mlp_weight, weight_grad, mlp_first, mlp_second, 0.02, 0.05
    )
    bias_new, bias_first_new, bias_second_new = adam_step(
        mlp_bias, hidden_bias_grad, bias_first, bias_second, 0.1, 0.0
    )
    return (
        outputs,
        input_grad,
        rms_values,
        attn_new,
        attn_new.astype(jnp.bfloat16),
        attn_first_new,
        attn_second_new,
        table_new,
        table_first_new,
        table_second_new,
        vector_new,
        vector_first_new,
        vector_second_new,
        mlp_new,
        mlp_new.astype(jnp.bfloat16),
        mlp_first_new,
        mlp_second_new,
        bias_new,
        bias_first_new,
        bias_second_new,
    )


def solution(mesh):
    return jax.shard_map(
        shards,
        mesh=mesh,
        in_specs=(
            P(("wide", "narrow"), None),
            P("wide"),
            P(("wide", "narrow"), None),
            P(),
            P(),
            P(),
            P(),
            P(),
            P(),
            P(),
            P(),
            P(),
            P(None, "narrow", None),
            P(None, "narrow", None),
            P(None, "narrow", None),
            P("narrow"),
            P("narrow"),
            P("narrow"),
        ),
        out_specs=(
            P(("wide", "narrow"), None),
            P(("wide", "narrow"), None),
            P(),
            P(),
            P(),
            P(),
            P(),
            P(),
            P(),
            P(),
            P(),
            P(),
            P(),
            P(None, "narrow", None),
            P(None, "narrow", None),
            P(None, "narrow", None),
            P(None, "narrow", None),
            P("narrow"),
            P("narrow"),
            P("narrow"),
        ),
        check_vma=False,
    )
```

profile of v0, /device:TPU:0, one launch (start us, length us, event | category | flops | bytes accessed | tf_op | source)
XLA Modules:
  0.0 1464.7 jit_solution(15444735954277440856)
XLA Ops:
  41.9 20.1 %reshape.445 = bf16[64,49,12,32]{1,0,3,2:T(8,128)(2,1)} reshape(bf16[3136,384]{0,1:T(8,128)(2,1)} %copy.100) | data formatting | bytes 4816896 | tf_op jit(solution)/shard_map/reshape | solution.py:125
  62.0 20.1 %reshape.447 = bf16[64,49,12,32]{1,0,3,2:T(8,128)(2,1)} reshape(bf16[3136,384]{0,1:T(8,128)(2,1)} %copy.102) | data formatting | bytes 4816896 | tf_op jit(solution)/shard_map/reshape | solution.py:121
  82.1 20.3 %reshape.446 = bf16[64,49,12,32]{1,0,3,2:T(8,128)(2,1)} reshape(bf16[3136,384]{0,1:T(8,128)(2,1)} %copy.101) | data formatting | bytes 4816896 | tf_op jit(solution)/shard_map/reshape | solution.py:120
  102.4 21.8 %fusion.32 = f32[64,12,49,49]{2,3,1,0:T(8,128)} fusion(bf16[64,49,12,32]{1,0,3,2:T(8,128)(2,1)} %reshape.447, bf16[64,49,12,32]{1,0,3,2:T(8,128)(2,1)} %reshape.446), kind=kOutput, calls=%fused_computation.55 | convolution fusion | flops 118013952 | bytes 12192768 | tf_op jit(solution)/shard_map/wqhd,wkhd->whqk/dot_general | solution.py:134
  124.2 31.0 %fusion.107 = (f32[64,12,49]{2,1,0:T(8,128)S(1)}, f32[64,12,49,49]{2,3,1,0:T(8,128)}) fusion(f32[64,12,49,49]{2,3,1,0:T(8,128)} %fusion.32, f32[64,49]{1,0:T(8,128)S(1)} %get-tuple-element.67, f32[12,49,49]{1,2,0:T(8,128)S(1)} %copy.106), kind=kOutput, calls=%fused_computation.197 | output fusion | flops 14751792 | bytes 15030064 | tf_op jit(solution)/shard_map/sub | solution.py:142
  155.2 15.4 %convert_bitcast_fusion.3 = bf16[64,49,12,32]{1,3,2,0:T(8,128)(2,1)} fusion(bf16[64,49,12,32]{1,0,3,2:T(8,128)(2,1)} %reshape.445, f32[64,12,49,49]{2,3,1,0:T(8,128)} %get-tuple-element.69, f32[64,12,49]{2,1,0:T(8,128)S(1)} %get-tuple-element.68), kind=kOutput, calls=%fused_computation.34 | convolution fusion | flops 122906112 | bytes 12343296 | tf_op jit(solution)/shard_map/whqk,wkhd->wqhd/dot_general | solution.py:144
  170.6 9.5 copy.109
  180.2 10.5 convert_element_type.130
  204.2 169.5 %all-gather.3.cloned.1.call-done = bf16[12544,384]{1,0:T(8,128)(2,1)} async-done(((bf16[3136,384]{1,0:T(8,128)(2,1)}), bf16[12544,384]{1,0:T(8,128)(2,1)}) %all-gather.3.cloned.1.call-update) | async-done | bytes 9633808 | tf_op jit(solution)/shard_map/all_gather | solution.py:158
  373.6 14.0 convolution_add_fusion
  387.6 155.8 %all-gather.5.cloned.1.call-done = bf16[12544,384]{1,0:T(8,128)(2,1)} async-done(((bf16[3136,384]{1,0:T(8,128)(2,1)}), bf16[12544,384]{1,0:T(8,128)(2,1)}) %all-gather.5.cloned.1.call-update) | async-done | bytes 9633808 | tf_op jit(solution)/shard_map/all_gather | solution.py:168
  543.4 16.6 %convolution_bitcast_fusion = f32[1,384,384]{2,1,0:T(8,128)} fusion(bf16[12544,384]{1,0:T(8,128)(2,1)} %all-gather.5.cloned.1.call-done, f32[12544,384]{1,0:T(8,128)} %convolution_add_fusion), kind=kOutput, calls=%fused_computation.101 | convolution fusion | flops 3742728192 | bytes 29491200 | tf_op jit(solution)/shard_map/dot_general | solution.py:43
  560.0 22.7 %convert_reduce_fusion = (f32[384]{0:T(512)S(1)}, bf16[12544,384]{1,0:T(8,128)(2,1)S(1)}) fusion(f32[12544,384]{1,0:T(8,128)} %convolution_add_fusion, bf16[12544,384]{1,0:T(8,128)(2,1)} %all-gather.5.cloned.1.call-done, bf16[2,384,384]{2,1,0:T(8,128)(2,1)S(1)} %convert_element_type.134), kind=kOutput, calls=%fused_computation.17 | convolution fusion | flops 3805347328 | bytes 38831616 | tf_op jit(solution)/shard_map/dot_general | solution.py:37
  589.1 12.3 fusion.76
  601.5 15.1 %fusion.78 = f32[12544,384]{1,0:T(8,128)} fusion(bf16[2,384,384]{2,1,0:T(8,128)(2,1)S(1)} %convert_element_type.134, f32[12544,384]{1,0:T(8,128)} %convolution_add_fusion), kind=kOutput, calls=%fused_computation.118 | convolution fusion | flops 3742728192 | bytes 38830080 | tf_op jit(solution)/shard_map/dot_general | solution.py:163
  616.7 14.2 psum.47
  631.5 13.0 all-reduce.6.cloned.1.call-done
  649.4 316.6 %reduce-scatter.5.cloned.1.call-done = f32[3136,384]{1,0:T(8,128)} async-done(((f32[12544,384]{1,0:T(8,128)}), f32[3136,384]{1,0:T(8,128)}) %reduce-scatter.5.cloned.1.call-update) | async-done | bytes 4816912 | tf_op jit(solution)/shard_map/reduce_scatter | solution.py:174
  988.4 19.1 %reshape.448 = bf16[64,49,12,32]{1,0,3,2:T(8,128)(2,1)} reshape(bf16[3136,384]{0,1:T(8,128)(2,1)S(1)} %copy.110) | data formatting | bytes 4816896 | tf_op jit(solution)/shard_map/reshape | solution.py:202
  1007.6 21.1 %convert_reduce_fusion.1 = (f32[12,32]{1,0:T(8,128)S(1)}, bf16[64,49,12,32]{1,3,2,0:T(8,128)(2,1)}) fusion(f32[64,12,49,49]{2,3,1,0:T(8,128)} %get-tuple-element.69, f32[64,12,49]{2,1,0:T(8,128)S(1)} %copy-done.38, bf16[64,49,12,32]{1,0,3,2:T(8,128)(2,1)} %reshape.448), kind=kOutput, calls=%fused_computation.21 | convolution fusion | flops 125314176 | bytes 12344832 | tf_op jit(solution)/shard_map/whqk,wqhd->wkhd/dot_general | solution.py:207
  1038.2 10.7 reshape.451
  1049.0 22.1 %fusion.25 = f32[64,12,49,49]{2,3,1,0:T(8,128)} fusion(bf16[64,49,12,32]{1,0,3,2:T(8,128)(2,1)} %reshape.448, bf16[64,49,12,32]{1,0,3,2:T(8,128)(2,1)} %reshape.445), kind=kOutput, calls=%fused_computation.48 | convolution fusion | flops 118013952 | bytes 12192768 | tf_op jit(solution)/shard_map/wqhd,wkhd->whqk/dot_general | solution.py:210
  1071.1 36.7 %fusion.108 = (f32[12,49,49]{1,2,0:T(8,128)S(1)}, f32[64,12,49,49]{2,3,1,0:T(8,128)}) fusion(f32[64,12,49,49]{2,3,1,0:T(8,128)} %fusion.25, f32[64,12,49,49]{2,3,1,0:T(8,128)} %get-tuple-element.69, f32[64,12,49]{2,1,0:T(8,128)S(1)} %copy-done.39), kind=kOutput, calls=%fused_computation.198 | output fusion | flops 11072676 | bytes 22393392 | tf_op jit(solution)/shard_map/sub | solution.py:213
  1107.7 21.9 %convert_reduce_fusion.2 = (f32[12,32]{1,0:T(8,128)S(1)}, bf16[64,49,12,32]{1,3,2,0:T(8,128)(2,1)}) fusion(f32[64,12,49,49]{2,3,1,0:T(8,128)} %get-tuple-element.72, bf16[64,49,12,32]{1,0,3,2:T(8,128)(2,1)} %reshape.447), kind=kOutput, calls=%fused_computation.22 | convolution fusion | flops 125314176 | bytes 12194304 | tf_op jit(solution)/shard_map/whqk,wkhd->wqhd/dot_general | solution.py:217
  1129.7 15.1 %convert_bitcast_fusion.1 = bf16[64,49,12,32]{1,3,2,0:T(8,128)(2,1)} fusion(f32[64,12,49,49]{2,3,1,0:T(8,128)} %get-tuple-element.72, bf16[64,49,12,32]{1,0,3,2:T(8,128)(2,1)} %reshape.446), kind=kOutput, calls=%fused_computation.32 | convolution fusion | flops 122906112 | bytes 12192768 | tf_op jit(solution)/shard_map/whqk,wqhd->wkhd/dot_general | solution.py:222
  1144.8 9.5 copy.118
  1154.4 10.5 reshape.450
  1174.4 9.6 reshape.449
  1200.8 88.9 %reduce-scatter.3.cloned.1.call-done = f32[3136,384]{1,0:T(8,128)} async-done(((f32[12544,384]{1,0:T(8,128)}), f32[3136,384]{1,0:T(8,128)}) %reduce-scatter.3.cloned.1.call-update) | async-done | bytes 4816912 | tf_op jit(solution)/shard_map/reduce_scatter | solution.py:162
  1289.7 18.5 %fusion.45 = (f32[384]{0:T(512)S(1)}, f32[3136]{0:T(1024)S(1)}, f32[3136]{0:T(1024)S(1)}, f32[384]{0:T(512)S(1)}, f32[]{:T(128)}, /*index=5*/f32[384]{0:T(512)S(...) fusion(bf16[3136,384]{1,0:T(8,128)(2,1)S(1)} %copy-done.4, f32[3136]{0:T(1024)S(1)} %copy-done.18, ...), kind=kOutput, calls=%fused_computation.68 | convolution fusion | flops 2803425280 | bytes 34822408 | tf_op jit(solution)/shard_map/dot_general | solution.py:37
  1312.6 42.0 %all-reduce = (f32[4]{0:T(128)S(1)}, f32[169,12]{0,1:T(8,128)S(1)}, f32[8,384]{1,0:T(8,128)S(1)}) all-reduce(f32[4]{0:T(128)S(1)} %pad_maximum_fusion.2, f32[169,12]{0,1:T(8,128)S(1)} %convolution_bitcast_fusion.2, f32[8,384]{1,0:T(8,128)S(1)} %stack.64), channel_id=1, replica_groups=mesh['wide'=8,'narrow'=4] {'wide','narrow'}, use_global_device_ids=true, to_apply=%region_18.19 | all-reduce | flops 5104 | bytes 40832 | tf_op jit(solution)/shard_map/psum | solution.py:190
  1364.9 84.3 %all-reduce.4.cloned.1.call-done = f32[384,1536]{1,0:T(8,128)} async-done(((f32[384,1536]{1,0:T(8,128)}), f32[384,1536]{1,0:T(8,128)}) %all-reduce.4.cloned.1.call-update) | async-done | bytes 2359312 | tf_op jit(solution)/shard_map/psum | solution.py:245
  (167 shorter events, 140.2 us)
Async XLA Ops:
  7.2 8.4 copy-start.22
  7.2 366.4 %all-gather.3.cloned.1.call-start = ((), (), s32[]{:S(2)}) async-start(), calls=%async_computation.2 | async-start | bytes 12042240 | tf_op jit(solution)/shard_map/all_gather | solution.py:158
  8.2 11.4 copy-start.15
  11.2 8.4 copy-start.13
  14.2 9.9 copy-start.17
  14.9 9.3 copy-start.28
  14.9 9.3 copy-start.33
  155.2 15.4 %copy-start.37 = (f32[64,12,49]{2,1,0:T(8,128)}, f32[64,12,49]{2,1,0:T(8,128)S(1)}, u32[]{:S(2)}) copy-start(f32[64,12,49]{2,1,0:T(8,128)S(1)} %get-tuple-element.68) | copy-start | bytes 451588
  200.8 172.9 %copy-start.21 = (f32[384]{0:T(512)S(1)}, f32[384]{0:T(512)}, u32[]{:S(2)}) copy-start(f32[384]{0:T(512)} %param.33) | copy-start | bytes 4612
  200.8 342.6 %all-gather.5.cloned.1.call-start = ((), (), s32[]{:S(2)}) async-start(), calls=%async_computation.4 | async-start | bytes 12042240 | tf_op jit(solution)/shard_map/all_gather | solution.py:168
  202.8 441.7 %all-reduce.6.cloned.1.call-start = ((), (), s32[]{:S(2)}) async-start(), calls=%async_computation.7 | async-start | bytes 2359296 | tf_op jit(solution)/shard_map/psum | solution.py:248
  543.4 39.3 %slice-start = ((s8[9633792]{0:T(1024)(128)(4,1)}), s8[4194304]{0:T(1024)(128)(4,1)S(1)}, s32[]{:S(2)}) async-start(s8[9633792]{0:T(1024)(128)(4,1)} %bitcast.70), calls=%async_computation.8 | async-start | bytes 8388608
  560.0 22.7 %slice-start.1 = ((s8[9633792]{0:T(1024)(128)(4,1)}), s8[4194304]{0:T(1024)(128)(4,1)S(1)}, s32[]{:S(2)}) async-start(s8[9633792]{0:T(1024)(128)(4,1)} %bitcast.70), calls=%async_computation.9 | async-start | bytes 8388608
  560.0 22.7 %slice-start.2 = ((s8[9633792]{0:T(1024)(128)(4,1)}), s8[1245184]{0:T(1024)(128)(4,1)S(1)}, s32[]{:S(2)}) async-start(s8[9633792]{0:T(1024)(128)(4,1)} %bitcast.70), calls=%async_computation.10 | async-start | bytes 2490368
  589.1 377.0 %reduce-scatter.5.cloned.1.call-start = ((), (), s32[]{:S(2)}) async-start(), calls=%async_computation.5 | async-start | bytes 24084480 | tf_op jit(solution)/shard_map/reduce_scatter | solution.py:174
  601.5 688.2 %reduce-scatter.3.cloned.1.call-start = ((), (), s32[]{:S(2)}) async-start(), calls=%async_computation.3 | async-start | bytes 24084480 | tf_op jit(solution)/shard_map/reduce_scatter | solution.py:162
  616.6 14.3 copy-start.35
  616.6 14.3 copy-start.36
  616.6 832.5 %all-reduce.4.cloned.1.call-start = ((), (), s32[]{:S(2)}) async-start(), calls=%async_computation.6 | async-start | bytes 4718592 | tf_op jit(solution)/shard_map/psum | solution.py:245
  988.4 19.2 %copy-start.38 = (f32[64,12,49]{2,1,0:T(8,128)S(1)}, f32[64,12,49]{2,1,0:T(8,128)}, u32[]{:S(2)}) copy-start(f32[64,12,49]{2,1,0:T(8,128)} %copy-done.37) | copy-start | bytes 451588
  1049.0 22.1 %copy-start.39 = (f32[64,12,49]{2,1,0:T(8,128)S(1)}, f32[64,12,49]{2,1,0:T(8,128)}, u32[]{:S(2)}) copy-start(f32[64,12,49]{2,1,0:T(8,128)} %copy-done.37) | copy-start | bytes 451588
  1174.4 9.7 copy-start.16
  1194.9 94.7 %copy-start.32 = (f32[384]{0:T(512)S(1)}, f32[384]{0:T(512)}, u32[]{:S(2)}) copy-start(f32[384]{0:T(512)} %get-tuple-element.32) | copy-start | bytes 4612
  1289.6 18.6 %copy-start.10 = (f32[384,1152]{1,0:T(8,128)S(1)}, f32[384,1152]{1,0:T(8,128)}, u32[]{:S(2)}) copy-start(f32[384,1152]{1,0:T(8,128)} %fusion.96) | copy-start | bytes 5308420
  1289.6 22.9 %copy-start.30 = (f32[1,384]{1,0:T(1,128)S(1)}, f32[1,384]{1,0:T(1,128)}, u32[]{:S(2)}) copy-start(f32[1,384]{1,0:T(1,128)} %stack.61) | copy-start | bytes 4612
  1289.6 22.9 %copy-start.31 = (f32[1,384]{1,0:T(1,128)S(1)}, f32[1,384]{1,0:T(1,128)}, u32[]{:S(2)}) copy-start(f32[1,384]{1,0:T(1,128)} %stack.62) | copy-start | bytes 4612
  1308.2 48.2 %copy-start.23 = (f32[169,12]{0,1:T(8,128)S(1)}, f32[169,12]{0,1:T(8,128)}, u32[]{:S(2)}) copy-start(f32[169,12]{0,1:T(8,128)} %param.24) | copy-start | bytes 24340
  1308.2 48.2 %copy-start.24 = (f32[169,12]{0,1:T(8,128)S(1)}, f32[169,12]{0,1:T(8,128)}, u32[]{:S(2)}) copy-start(f32[169,12]{0,1:T(8,128)} %param.25) | copy-start | bytes 24340
  1308.2 48.2 %copy-start.25 = (f32[169,12]{0,1:T(8,128)S(1)}, f32[169,12]{0,1:T(8,128)}, u32[]{:S(2)}) copy-start(f32[169,12]{0,1:T(8,128)} %param.26) | copy-start | bytes 24340
  1308.2 48.8 %copy-start.20 = (f32[8,384]{1,0:T(8,128)S(1)}, f32[8,384]{1,0:T(8,128)}, u32[]{:S(2)}) copy-start(f32[8,384]{1,0:T(8,128)} %param.27) | copy-start | bytes 36868
  1308.2 48.8 %copy-start.26 = (f32[8,384]{1,0:T(8,128)S(1)}, f32[8,384]{1,0:T(8,128)}, u32[]{:S(2)}) copy-start(f32[8,384]{1,0:T(8,128)} %param.28) | copy-start | bytes 36868
  1308.2 48.8 %copy-start.27 = (f32[8,384]{1,0:T(8,128)S(1)}, f32[8,384]{1,0:T(8,128)}, u32[]{:S(2)}) copy-start(f32[8,384]{1,0:T(8,128)} %param.29) | copy-start | bytes 36868
  (17 other events, 78.5 us)
Sparse Core Ops, SparseCore 0:
  200.9 172.6 all-gather.2
  375.2 168.1 all-gather.4
  589.2 55.2 all-reduce.5
  646.9 319.1 reduce-scatter.4
  968.4 321.1 reduce-scatter.2
  1312.7 136.4 all-reduce.3
where the time goes:
time: 1480 us; the launch traced here: 1460 us
  waiting for transfers between devices  828 us (56%)
  matrix products  249 us (17%)
  local copies, waits for them, and re-layouts  188 us (13%)
  other arithmetic  127 us (9%)
  blocking collectives  56.1 us (4%)
  between operations  15.9 us (1%)
    reduce_scatter x1, waiting for transfers between devices, shards(): lax.psum_scatter(jnp.dot(part_rows, hidden_low[0], preferred_element_type...  317 us
    all_gather x1, waiting for transfers between devices, shards(): gathered = lax.all_gather(second_low, 'narrow', axis=0, tiled=True)  169 us
    all_gather x1, waiting for transfers between devices, shards(): grad_all = lax.all_gather(grad_low, 'narrow', axis=0, tiled=True)  156 us
    reduce_scatter x1, waiting for transfers between devices, shards(): lax.psum_scatter(jnp.dot(part_rows, hidden_low[1], preferred_element_type...  88.9 us
    psum x1, waiting for transfers between devices, shards(): lax.psum((attn_grad, table_grad, vector_grad), ('wide', 'narrow'))  84.3 us
    dot_general x4, matrix products, times_trans(): lax.dot_general(left, right, (((1,), (1,)), ((), ())), preferred_element_...  59.3 us
    psum x1, blocking collectives, shards(): stat_totals = lax.psum(local_stats, ('wide', 'narrow'))  42 us
    sub x1, other arithmetic, shards(): grad_probs - jnp.sum(grad_probs * attn_probs, -1, keepdims=True)  36.7 us
  transfers between devices with their start and end apart: 6, of which 6 were waited for; matrix products, arithmetic and copies ran while one was open for 20% of the time, Pallas kernels for 0%

commit v1 on v0

v1 whole, which is shorter than its diff:
```python
import jax
import jax.numpy as jnp
import numpy as np
from jax import lax
from jax.sharding import PartitionSpec as P
from jax.experimental import pallas as pl
from jax.experimental.pallas import tpu as pltpu

WIN = 7
WTOK = 49
WPI = 16
IMG_W = 16
STEP = 5
CW = 5
CR = 256
SLOT = 64
KR = 56
HG = 4
LOG2E = 1.4426950408889634

norm_eps = 1e-05
beta_one = 0.5
beta_two = 0.5
adam_eps = 1e-08
highest = lax.Precision.HIGHEST
f32 = jnp.float32
bf16 = jnp.bfloat16


def nn(a, b):
    return lax.dot_general(a, b, (((1,), (0,)), ((), ())), preferred_element_type=f32)


def nt(a, b):
    return lax.dot_general(a, b, (((1,), (1,)), ((), ())), preferred_element_type=f32)


def tn(a, b):
    return lax.dot_general(a, b, (((0,), (0,)), ((), ())), preferred_element_type=f32)


def row_info():
    r = np.arange(CR)
    win = r // WTOK
    p = r % WTOK
    info = np.stack([win, p // WIN, p % WIN]).astype(np.float32)
    info[1, win >= CW] = 1000.0
    return np.ascontiguousarray(np.broadcast_to(info[:, :, None], (3, CR, 128)))


def key_info():
    p = np.arange(KR)
    info = np.stack([p // WIN, p % WIN]).astype(np.float32)
    return np.ascontiguousarray(np.broadcast_to(info[:, :, None], (2, KR, 128)))


def head_mask(head_size):
    row = np.arange(HG * SLOT)
    lane = np.arange(HG * head_size)
    return (((row // SLOT)[:, None] == (lane // head_size)[None, :]) & ((row % SLOT) < WTOK)[:, None]).astype(np.float32)


def fold_rows(t):
    return jnp.sum(t.reshape(t.shape[0] // 8, 8, t.shape[1]), 0)


def rep(v, n):
    return jnp.concatenate([v] * n, 1)


def list_windows(sides, narrow, wins, slots, idx, lim_r, lim_c):
    def one(w, n):
        place = narrow * wins + w
        u = WPI - 1 - place // IMG_W
        side = sides[lax.rem(place, IMG_W)]
        r = side - WIN * (u // 4)
        c = side - WIN * lax.rem(u, 4)
        idx[n] = w
        lim_r[n] = r.astype(f32)
        lim_c[n] = c.astype(f32)
        return jnp.where((r > 0) & (c > 0), n + 1, n)

    n = lax.fori_loop(0, wins, one, 0)

    def blank(s, carry):
        @pl.when(s >= n)
        def _():
            idx[s] = wins
            lim_r[s] = 0.0
            lim_c[s] = 0.0
        return carry

    lax.fori_loop(0, slots, blank, 0)
    return n


def chunk_valid(info, lim_r, lim_c, first):
    win = info[0]
    r = jnp.full_like(win, 0.0)
    c = jnp.full_like(win, 0.0)
    for i in range(CW):
        here = win == float(i)
        r = jnp.where(here, lim_r[first + i], r)
        c = jnp.where(here, lim_c[first + i], c)
    return jnp.where((info[1] < r) & (info[2] < c), 1.0, 0.0)


def norm_stats(x):
    mean = jnp.mean(x, -1, keepdims=True)
    centred = x - mean
    inverse = lax.rsqrt(jnp.mean(centred * centred, -1, keepdims=True) + norm_eps)
    return centred * inverse, inverse


def norm_grad(g, xhat, inverse, gain):
    scaled = g * gain
    m1 = jnp.mean(scaled, -1, keepdims=True)
    m2 = jnp.mean(scaled * xhat, -1, keepdims=True)
    return inverse * (scaled - m1 - xhat * m2)


def spread(src, stage, slots):
    wins = src.shape[0] // WTOK
    part = IMG_W * WTOK
    slots[...] = jnp.zeros_like(slots)

    def one(b, carry):
        stage[...] = src[pl.ds(pl.multiple_of(b * part, part), part), :].astype(f32)
        for i in range(IMG_W):
            slots[b * IMG_W + i, :WTOK, :] = stage[WTOK * i : WTOK * i + WTOK, :]
        return carry

    lax.fori_loop(0, wins // IMG_W, one, 0)


def gather_back(slots, stage, dst):
    wins = dst.shape[0] // WTOK
    part = IMG_W * WTOK

    def one(b, carry):
        for i in range(IMG_W):
            stage[WTOK * i : WTOK * i + WTOK, :] = slots[b * IMG_W + i, :WTOK, :]
        dst[pl.ds(pl.multiple_of(b * part, part), part), :] = stage[...].astype(dst.dtype)
        return carry

    lax.fori_loop(0, wins // IMG_W, one, 0)


def attn_forward(narrow_ref, sides, tok, wq, vec, bias, rinfo, kinfo, hmask,
                 x_out, qkv_out, prob_out, mixed_out, stream_out, stat_out,
                 tok32, stage, xs, pj, mx, idx, lim_r, lim_c, count):
    step = pl.program_id(0)
    wins = tok.shape[0] // WTOK
    width = tok.shape[1]
    groups = width // 128

    @pl.when(step == 0)
    def _():
        count[0] = list_windows(sides, narrow_ref[0], wins, idx.shape[0], idx, lim_r, lim_c)
        spread(tok, stage, tok32)
        xs[...] = jnp.zeros_like(xs)
        pj[...] = jnp.zeros_like(pj)
        mx[...] = jnp.zeros_like(mx)
        stat_out[...] = jnp.zeros_like(stat_out)

    @pl.when(step * CW < count[0])
    def _():
        first = step * CW
        for i in range(CW):
            xs[WTOK * i : WTOK * i + KR, :] = tok32[idx[first + i]]
        x = xs[:CR, :]
        x_out[0] = x.astype(bf16)
        valid = chunk_valid(rinfo, lim_r, lim_c, first)
        keep = rep(valid, groups)
        xhat, _ = norm_stats(x)
        low = (xhat * vec[0:1] + vec[1:2]).astype(bf16)
        pj[:CR, :width] = nn(low, wq[:, :width]) + vec[2:3]
        pj[:CR, width : 2 * width] = nn(low, wq[:, width : 2 * width])
        pj[:CR, 2 * width :] = nn(low, wq[:, 2 * width : 3 * width]) + vec[3:4]
        for i in range(CW):
            rows = slice(WTOK * i, WTOK * i + SLOT)
            qkv = pj[rows, :].astype(bf16)
            qkv_out[0, i] = qkv
            fill = jnp.where((kinfo[0] < lim_r[first + i]) & (kinfo[1] < lim_c[first + i]), 0.0, -10000.0 * LOG2E)
            fill = rep(fill, 2)
            for g in range(groups):
                q = qkv[:, 128 * g : 128 * g + 128]
                k = qkv[:KR, width + 128 * g : width + 128 * g + 128]
                v = qkv[:KR, 2 * width + 128 * g : 2 * width + 128 * g + 128]
                q_bd = jnp.concatenate([q] * HG, 0) * hmask[...]
                s = nt(k, q_bd) * (32 ** (-0.5) * LOG2E) + bias[g] + fill
                e = jnp.exp2(s - jnp.max(s, 0, keepdims=True))
                prob = e / jnp.sum(e, 0, keepdims=True)
                prob_out[0, i, g] = prob
                wide_mix = tn(prob.astype(bf16), v)
                hm = hmask[...].astype(f32)
                o = wide_mix * hm
                o = o[:SLOT] + o[SLOT : 2 * SLOT] + o[2 * SLOT : 3 * SLOT] + o[3 * SLOT :]
                mx[WTOK * i : WTOK * i + KR, 128 * g : 128 * g + 128] = o[:KR]
        mixed = mx[:CR, :].astype(bf16)
        mixed_out[0] = mixed
        branch = (nn(mixed, wq[:, 3 * width :]) + vec[4:5]) * keep
        stream_out[0] = x + branch
        stat_out[0] += fold_rows(x * x * keep)
        stat_out[1] += fold_rows(branch * branch)
        stat_out[2, :, :128] += fold_rows(valid)


def mlp_both(narrow_ref, sides, tok, cot, w1, w2, wo, vec, hidden_bias, rinfo, mixed_in, stream_in,
             out_ref, grad_stream_out, grad_mixed_out, dw1, dw2, dwo, dbias, dvec, stat_out,
             out32, cot32, stage, cs, gm, idx, lim_r, lim_c, count):
    step = pl.program_id(0)
    wins = tok.shape[0] // WTOK
    width = tok.shape[1]
    groups = width // 128
    hidden = w1.shape[0]
    tile = 384

    @pl.when(step == 0)
    def _():
        count[0] = list_windows(sides, narrow_ref[0], wins, idx.shape[0], idx, lim_r, lim_c)
        spread(tok, stage, out32)
        spread(cot, stage, cot32)
        cs[...] = jnp.zeros_like(cs)
        gm[...] = jnp.zeros_like(gm)
        for ref in (dw1, dw2, dwo, dbias, dvec, stat_out):
            ref[...] = jnp.zeros_like(ref)

    @pl.when(step * CW < count[0])
    def _():
        first = step * CW
        for i in range(CW):
            cs[WTOK * i : WTOK * i + KR, :] = cot32[idx[first + i]]
        cotan = cs[:CR, :]
        keep = rep(chunk_valid(rinfo, lim_r, lim_c, first), groups)
        stream = stream_in[0]
        xhat, inverse = norm_stats(stream)
        second = (xhat * vec[5:6] + vec[6:7]).astype(bf16)
        kept_cot = cotan * keep
        grad_low = kept_cot.astype(bf16)
        mlp_out = jnp.zeros((CR, width), f32)
        grad_second = jnp.zeros((CR, width), f32)
        for t in range(hidden // tile):
            cols = slice(tile * t, tile * t + tile)
            pre = nt(second, w1[cols, :]) + hidden_bias[0:1, cols]
            inner = 0.7978845608028654 * (pre + 0.044715 * (pre * pre * pre))
            th = jnp.tanh(inner)
            active = (0.5 * pre * (1.0 + th)).astype(bf16)
            slope = 0.5 * (1.0 + th) + (0.5 * pre) * (1.0 - th * th) * (
                0.7978845608028654 * (1.0 + 3 * 0.044715 * (pre * pre)))
            grad_pre32 = nt(grad_low, w2[cols, :]) * slope
            grad_pre = grad_pre32.astype(bf16)
            mlp_out += nn(active, w2[cols, :])
            grad_second += nn(grad_pre, w1[cols, :])
            dw1[:, cols] += tn(second, grad_pre)
            dw2[:, cols] += tn(grad_low, active)
            dbias[:, cols] += fold_rows(grad_pre.astype(f32))
        branch = (mlp_out + vec[7:8]) * keep
        result = stream + branch
        stat_out[...] += fold_rows(branch * branch)
        grad_stream = cotan + norm_grad(grad_second, xhat, inverse, vec[5:6])
        grad_stream_out[0] = grad_stream
        dvec[0] += fold_rows(grad_second * xhat)
        dvec[1] += fold_rows(grad_second)
        dvec[2] += fold_rows(kept_cot)
        grad_attn = grad_stream * keep
        dvec[3] += fold_rows(grad_attn)
        grad_attn_low = grad_attn.astype(bf16)
        dwo[...] += tn(mixed_in[0], grad_attn_low)
        gm[:CR, :] = nt(grad_attn_low, wo[...])
        cs[:CR, :] = result
        for i in range(CW):
            rows = slice(WTOK * i, WTOK * i + SLOT)
            grad_mixed_out[0, i] = gm[rows, :].astype(bf16)

            @pl.when(first + i < count[0])
            def _():
                out32[idx[first + i], :WTOK, :] = cs[WTOK * i : WTOK * i + WTOK, :]

    @pl.when(step == pl.num_programs(0) - 1)
    def _():
        gather_back(out32, stage, out_ref)


def attn_backward(narrow_ref, sides, cot, wq, vec, rinfo, hmask, x_in, qkv_in, prob_in, grad_mixed_in, grad_stream_in,
                  input_grad, dwq, dbias, dvec, dtable,
                  ig32, stage, dp, gs, idx, lim_r, lim_c, count):
    step = pl.program_id(0)
    wins = cot.shape[0] // WTOK
    width = cot.shape[1]
    groups = width // 128

    @pl.when(step == 0)
    def _():
        count[0] = list_windows(sides, narrow_ref[0], wins, idx.shape[0], idx, lim_r, lim_c)
        spread(cot, stage, ig32)
        dp[...] = jnp.zeros_like(dp)
        for ref in (dwq, dbias, dvec, dtable):
            ref[...] = jnp.zeros_like(ref)

    @pl.when(step * CW < count[0])
    def _():
        first = step * CW
        for i in range(CW):
            rows = slice(WTOK * i, WTOK * i + KR)
            for g in range(groups):
                q = qkv_in[0, i, :, 128 * g : 128 * g + 128]
                k = qkv_in[0, i, :KR, width + 128 * g : width + 128 * g + 128]
                v = qkv_in[0, i, :KR, 2 * width + 128 * g : 2 * width + 128 * g + 128]
                do = grad_mixed_in[0, i, :, 128 * g : 128 * g + 128]
                q_bd = jnp.concatenate([q] * HG, 0) * hmask[...]
                do_bd = jnp.concatenate([do] * HG, 0) * hmask[...]
                prob = prob_in[0, i, g]
                gp = nt(v, do_bd)
                ds = prob * (gp - jnp.sum(gp * prob, 0, keepdims=True))
                dtable[g] += ds
                raw = (ds * 32 ** (-0.5)).astype(bf16)
                hm = hmask[...].astype(f32)
                o = tn(raw, k) * hm
                dq = o[:SLOT] + o[SLOT : 2 * SLOT] + o[2 * SLOT : 3 * SLOT] + o[3 * SLOT :]
                dp[rows, 128 * g : 128 * g + 128] = dq[:KR]
                dp[rows, width + 128 * g : width + 128 * g + 128] = nn(raw, q_bd)
                dp[rows, 2 * width + 128 * g : 2 * width + 128 * g + 128] = nn(prob.astype(bf16), do_bd)
        dproj = dp[:CR, :].astype(bf16)
        x = x_in[0].astype(f32)
        xhat, inverse = norm_stats(x)
        low = (xhat * vec[0:1] + vec[1:2]).astype(bf16)
        for j in range(3):
            cols = slice(width * j, width * j + width)
            dwq[:, cols] += tn(low, dproj[:, cols])
        dbias[0] += fold_rows(dproj[:, :width].astype(f32))
        dbias[1] += fold_rows(dproj[:, 2 * width :].astype(f32))
        grad_normed = nt(dproj, wq[:, : 3 * width])
        dvec[0] += fold_rows(grad_normed * xhat)
        dvec[1] += fold_rows(grad_normed)
        gs[:CR, :] = grad_stream_in[0] + norm_grad(grad_normed, xhat, inverse, vec[0:1])
        for i in range(CW):
            @pl.when(first + i < count[0])
            def _():
                ig32[idx[first + i], :WTOK, :] = gs[WTOK * i : WTOK * i + WTOK, :]

    @pl.when(step == pl.num_programs(0) - 1)
    def _():
        gather_back(ig32, stage, input_grad)


def whole(a):
    nd = len(a.shape)
    return pl.BlockSpec(a.shape, lambda *_: (0,) * nd)


def per_chunk(shape):
    nd = len(shape)
    return pl.BlockSpec((1,) + tuple(shape[1:]), lambda c, *_: (c,) + (0,) * (nd - 1))


def sds(shape, dt):
    return jax.ShapeDtypeStruct(shape, dt)


def call(body, scalars, wholes, chunked, out_wholes, out_chunked, order_out, scratch, steps, cost):
    in_specs = [whole(a) for a in wholes] + [per_chunk(a.shape) for a in chunked]
    outs = [sds(s, d) for _, s, d in order_out]
    out_specs = [whole(sds(s, d)) if kind == "w" else per_chunk(s) for kind, s, d in order_out]
    slots = steps * CW
    return pl.pallas_call(
        body,
        grid_spec=pltpu.PrefetchScalarGridSpec(
            num_scalar_prefetch=len(scalars),
            grid=(steps,),
            in_specs=in_specs,
            out_specs=out_specs,
            scratch_shapes=list(scratch) + [
                pltpu.SMEM((slots + 1,), jnp.int32),
                pltpu.SMEM((slots + 1,), f32),
                pltpu.SMEM((slots + 1,), f32),
                pltpu.SMEM((1,), jnp.int32),
            ],
        ),
        out_shape=outs,
        compiler_params=pltpu.CompilerParams(vmem_limit_bytes=60 * 1024 * 1024, dimension_semantics=("arbitrary",)),
        cost_estimate=pl.CostEstimate(flops=cost, bytes_accessed=20000000, transcendentals=0),
    )(*scalars, *wholes, *chunked)


def bias_layout(rel_table):
    pos = np.arange(WTOK)
    row, col = pos // WIN, pos % WIN
    off = (row[:, None] - row[None, :] + WIN - 1) * (2 * WIN - 1) + col[:, None] - col[None, :] + WIN - 1
    full = np.full((KR, SLOT), -1, np.int32)
    full[:WTOK, :WTOK] = off.T
    return full


def expand_bias(rel_table):
    full = bias_layout(rel_table)
    heads = rel_table.shape[1]
    hot = (jnp.asarray(full)[:, :, None] == jnp.arange(rel_table.shape[0])).astype(f32)
    b = jnp.einsum("kqt,th->khq", hot, rel_table * LOG2E, precision=highest)
    b = b.reshape(KR, heads // HG, HG * SLOT).transpose(1, 0, 2)
    dead = (np.arange(KR) >= WTOK)[None, :, None]
    return jnp.where(dead, -1e30, b), hot


def block(tokens, grid_sizes, cotangent, attn_weight, rel_table, vectors, w1, w2, mlp_bias, narrow):
    rows, width = tokens.shape
    wins = rows // WTOK
    heads = rel_table.shape[1]
    groups = heads // HG
    steps = -(-wins // CW)
    weight_low = attn_weight.astype(bf16)
    bias, hot = expand_bias(rel_table)
    rinfo = jnp.asarray(row_info())
    kinfo = jnp.asarray(key_info())
    hmask = jnp.asarray(head_mask(width // heads), bf16)
    slots32 = pltpu.VMEM((wins + 1, KR, width), f32)
    stage = pltpu.VMEM((IMG_W * WTOK, width), f32)
    scal = (narrow.reshape(1).astype(jnp.int32), grid_sizes)
    x, qkv, prob, mixed, stream, stat0 = call(
        attn_forward, scal, (tokens, weight_low, vectors, bias, rinfo, kinfo, hmask), (), None, None,
        [("c", (steps, CR, width), bf16), ("c", (steps, CW, SLOT, 3 * width), bf16),
         ("c", (steps, CW, groups, KR, HG * SLOT), f32), ("c", (steps, CR, width), bf16),
         ("c", (steps, CR, width), f32), ("w", (3, 8, width), f32)],
        [slots32, stage, pltpu.VMEM((CR + 16, width), f32),
         pltpu.VMEM((CR + 16, 3 * width), f32), pltpu.VMEM((CR + 16, width), f32)],
        steps, 8 * rows * width * width)
    outputs, grad_stream, grad_mixed, dw1, dw2, dwo, dhid, dvec2, stat1 = call(
        mlp_both, scal, (tokens, cotangent, w1, w2, weight_low[:, 3 * width :], vectors, mlp_bias.reshape(1, -1), rinfo),
        (mixed, stream), None, None,
        [("w", (rows, width), bf16), ("c", (steps, CR, width), f32), ("c", (steps, CW, SLOT, width), bf16),
         ("w", (width, w1.shape[0]), f32), ("w", (width, w1.shape[0]), f32), ("w", (width, width), f32),
         ("w", (8, w1.shape[0]), f32), ("w", (4, 8, width), f32), ("w", (8, width), f32)],
        [slots32, slots32, stage,
         pltpu.VMEM((CR + 16, width), f32), pltpu.VMEM((CR + 16, width), f32)],
        steps, 52 * rows * width * width)
    input_grad, dwq, dqv, dvec1, dtab = call(
        attn_backward, scal, (cotangent, weight_low, vectors, rinfo, hmask),
        (x, qkv, prob, grad_mixed, grad_stream), None, None,
        [("w", (rows, width), f32), ("w", (width, 3 * width), f32), ("w", (2, 8, width), f32), ("w", (2, 8, width), f32),
         ("w", (groups, KR, HG * SLOT), f32)],
        [slots32, stage, pltpu.VMEM((CR + 16, 3 * width), f32), pltpu.VMEM((CR + 16, width), f32)],
        steps, 16 * rows * width * width)
    dt = dtab.transpose(1, 0, 2).reshape(KR, heads, SLOT)
    table_grad = jnp.einsum("kqt,khq->th", hot, dt, precision=highest)
    dqv = jnp.sum(dqv, 1)
    dvec1 = jnp.sum(dvec1, 1)
    dvec2 = jnp.sum(dvec2, 1)
    vector_grad = jnp.stack([dvec1[0], dvec1[1], dqv[0], dqv[1], dvec2[3], dvec2[0], dvec2[1], dvec2[2]])
    stats = jnp.stack([jnp.sum(stat0[0]), jnp.sum(stat0[1]), jnp.sum(stat1), jnp.sum(stat0[2, :, 0])])
    attn_grad = jnp.concatenate([dwq, dwo], 1)
    return outputs, input_grad, stats, attn_grad, table_grad, vector_grad, dw1, dw2, jnp.sum(dhid, 0)


def adam_step(weight, gradient, first_old, second_old, rate_value, decay_value):
    first_new = beta_one * first_old + (1.0 - beta_one) * gradient
    second_new = beta_two * second_old + (1.0 - beta_two) * gradient * gradient
    fix_one = 1.0 - beta_one**STEP
    fix_two = 1.0 - beta_two**STEP
    update = rate_value * (first_new / fix_one) / (jnp.sqrt(second_new / fix_two) + adam_eps)
    return (weight - update - rate_value * decay_value * weight, first_new, second_new)


def shards(tokens, grid_sizes, cotangent, attn_weight, attn_first, attn_second, rel_table, table_first, table_second,
           vectors, vector_first, vector_second, mlp_weight, mlp_first, mlp_second, mlp_bias, bias_first, bias_second):
    width = tokens.shape[1]
    hidden_low = lax.all_gather(mlp_weight.astype(bf16), "narrow", axis=1, tiled=True)
    hidden_bias = lax.all_gather(mlp_bias, "narrow", axis=0, tiled=True)
    outputs, input_grad, stats, attn_grad, table_grad, vector_grad, dw1, dw2, dhid = block(
        tokens, grid_sizes, cotangent, attn_weight, rel_table, vectors, hidden_low[0], hidden_low[1], hidden_bias,
        lax.axis_index("narrow"))
    both = ("wide", "narrow")
    stat_totals = lax.psum(stats, both)
    weight_grad = lax.psum(lax.psum_scatter(jnp.stack([dw1, dw2]), "narrow", scatter_dimension=2, tiled=True), "wide")
    weight_grad = weight_grad.transpose(0, 2, 1)
    hidden_bias_grad = lax.psum(lax.psum_scatter(dhid, "narrow", scatter_dimension=0, tiled=True), "wide")
    attn_grad, table_grad, vector_grad = lax.psum((attn_grad, table_grad, vector_grad), both)
    rms_values = jnp.sqrt(stat_totals[:3] / (stat_totals[3] * width))
    attn_new, attn_first_new, attn_second_new = adam_step(attn_weight, attn_grad, attn_first, attn_second, 0.02, 0.05)
    table_new, table_first_new, table_second_new = adam_step(rel_table, table_grad, table_first, table_second, 0.3, 0.0)
    vector_new, vector_first_new, vector_second_new = adam_step(vectors, vector_grad, vector_first, vector_second, 0.3, 0.0)
    mlp_new, mlp_first_new, mlp_second_new = adam_step(mlp_weight, weight_grad, mlp_first, mlp_second, 0.02, 0.05)
    bias_new, bias_first_new, bias_second_new = adam_step(mlp_bias, hidden_bias_grad, bias_first, bias_second, 0.1, 0.0)
    return (outputs, input_grad, rms_values, attn_new, attn_new.astype(bf16), attn_first_new, attn_second_new,
            table_new, table_first_new, table_second_new, vector_new, vector_first_new, vector_second_new,
            mlp_new, mlp_new.astype(bf16), mlp_first_new, mlp_second_new, bias_new, bias_first_new, bias_second_new)


def solution(mesh):
    rows = P(("wide", "narrow"), None)
    split = P(None, "narrow", None)
    return jax.shard_map(
        shards, mesh=mesh,
        in_specs=(rows, P("wide"), rows) + (P(),) * 9 + (split,) * 3 + (P("narrow"),) * 3,
        out_specs=(rows, rows) + (P(),) * 11 + (split,) * 4 + (P("narrow"),) * 3,
        check_vma=False)
```

time: 1480 us -> 458 us (0.31)
  waiting for transfers between devices: 828 us -> 120 us
  matrix products: 249 us -> 6.89 us
  local copies, waits for them, and re-layouts: 188 us -> 27.9 us
  blocking collectives: 56.1 us -> 152 us
  Pallas kernels: 0 us -> 92.1 us
  other arithmetic: 127 us -> 42 us
    reduce_scatter x2 -> x1, waiting for transfers between devices: 405 us -> 0.01 us  [shards(): lax.psum_scatter(jnp.stack([dw1, dw2]), 'narrow', scatter_dimension=2, ti...]
    all_gather x2 -> x1, waiting for transfers between devices: 325 us -> 5.86 us  [shards(): lax.all_gather(mlp_weight.astype(bf16), 'narrow', axis=1, tiled=True)]
    dot_general x20 -> x2, matrix products: 249 us -> 6.89 us  [the longest x1 3.95 us: expand_bias(): b = jnp.einsum('kqt,th->khq', hot, rel_table * LOG2E, precision=highest)]
    reshape x7 -> x2, local copies, waits for them, and re-layouts: 111 us -> 3.77 us  [the longest x1 1.89 us: block(): dt = dtab.transpose(1, 0, 2).reshape(KR, heads, SLOT)]
    pallas_call x0 -> x3, Pallas kernels: none -> 92.1 us  [call(): pl.pallas_call(body, grid_spec=pltpu.PrefetchScalarGridSpec(num_scalar_pr...]
    psum x2, blocking collectives: 56.1 us -> 127 us  [the longest x1 114 us: shards(): stat_totals = lax.psum(stats, both)]
    sub x3 -> x0, other arithmetic: 67.8 us -> none  [the longest x1 36.7 us: shards(): grad_probs - jnp.sum(grad_probs * attn_probs, -1, keepdims=True)]
    convert_element_type x9 -> x0, local copies, waits for them, and re-layouts: 60.6 us -> none  [the longest x2 20.1 us: shards(): mixed_low = mixed_heads.reshape(row_count, model_width).astype(jnp.bfloat16)]
  transfers between devices with their start and end apart: 6 -> 4, of which waited for: 6 -> 3; matrix products, arithmetic and copies ran while one was open for 20% -> 12% of each run, Pallas kernels for 0% -> 12%
where the time goes in v1:
time: 458 us; the launch traced here: 457 us
  blocking collectives  152 us (33%)
  waiting for transfers between devices  120 us (26%)
  Pallas kernels  92.1 us (20%)
  other arithmetic  42 us (9%)
  local copies, waits for them, and re-layouts  27.9 us (6%)
  between operations  15.2 us (3%)
  matrix products  6.89 us (2%)
    psum x1, blocking collectives, shards(): stat_totals = lax.psum(stats, both)  114 us
    pallas_call x3, Pallas kernels, call(): pl.pallas_call(body, grid_spec=pltpu.PrefetchScalarGridSpec(num_scalar_pr...  92.1 us
    psum x1, waiting for transfers between devices, shards(): lax.psum((attn_grad, table_grad, vector_grad), both)  62.6 us
    psum x1, waiting for transfers between devices, shards(): lax.psum(lax.psum_scatter(jnp.stack([dw1, dw2]), 'narrow', scatter_dimens...  51.9 us
    unnamed x26, local copies, waits for them, and re-layouts  16.6 us
    all_gather x1, blocking collectives, shards(): hidden_bias = lax.all_gather(mlp_bias, 'narrow', axis=0, tiled=True)  14.2 us
    psum x1, blocking collectives, shards(): lax.psum(lax.psum_scatter(dhid, 'narrow', scatter_dimension=0, tiled=True...  12.9 us
    unnamed x1, blocking collectives  11 us
  transfers between devices with their start and end apart: 4, of which 3 were waited for; matrix products, arithmetic and copies ran while one was open for 12% of the time, Pallas kernels for 12%

profile of v1, /device:TPU:0, one launch (start us, length us, event | category | flops | bytes accessed | tf_op | source)
XLA Modules:
  0.0 456.6 jit_solution(17906052321771446640)
XLA Ops:
  7.2 2.3 convert_element_type.13
  10.3 3.9 fusion.5
  14.2 1.9 reshape.57
  17.5 14.2 %all-gather = f32[4,1,384]{2,1,0:T(1,128)} all-gather(f32[1,1,384]{2,1,0:T(1,128)S(1)} %reshape.59), channel_id=1, replica_groups=mesh['wide'=8,'narrow'=4] {'narrow'}, dimensions={0}, use_global_device_ids=true | all-gather | bytes 7680 | tf_op jit(solution)/shard_map/all_gather | solution.py:467
  31.7 1.7 fusion.8.bias
  33.4 24.1 %shard_map.374 = (bf16[13,256,384]{2,1,0:T(8,128)(2,1)}, bf16[13,5,64,1152]{3,2,1,0:T(8,128)(2,1)}, f32[13,5,3,56,256]{4,3,2,1,0:T(8,128)}, bf16[13,256,384]{2,1...) custom-call(s32[1]{0:T(128)} %bitcast.narrow_ref, s32[16]{0:T(128)} %sides.5, bf16[3136,384]{1,0:T(8,128)(2,1)} %tok.3, ...), custom_call_target="tpu_custom_call" | custom-call | flops 3699376128 | bytes 20000000 | tf_op jit(solution)/shard_map/pallas_call | solution.py:366
  57.6 5.9 %all-gather.3.cloned.1.call-done = bf16[2,1536,384]{2,1,0:T(8,128)(2,1)} async-done(((bf16[2,384,384]{2,1,0:T(8,128)(2,1)}), bf16[2,1536,384]{2,1,0:T(8,128)(2,1)}) %all-gather.3.cloned.1.call-update) | async-done | bytes 2359312 | tf_op jit(solution)/shard_map/all_gather | solution.py:466
  63.4 3.3 slice_bitcast_fusion
  66.7 35.4 %shard_map.375 = (bf16[3136,384]{1,0:T(8,128)(2,1)}, f32[13,256,384]{2,1,0:T(8,128)}, bf16[13,5,64,384]{3,2,1,0:T(8,128)(2,1)}, f32[384,1536]{1,0:T(8,128)}, f32...) custom-call(s32[1]{0:T(128)} %bitcast.narrow_ref, ...), custom_call_target="tpu_custom_call" | custom-call | flops 24045944832 | bytes 20000000 | tf_op jit(solution)/shard_map/pallas_call | solution.py:366
  102.1 4.9 %pad_maximum_fusion = f32[2,384,1536]{2,1,0:T(8,128)} fusion(f32[1,384,1536]{2,1,0:T(8,128)} %bitcast.28, f32[1,384,1536]{2,1,0:T(8,128)} %bitcast.27), kind=kLoop, calls=%fused_computation | loop fusion | flops 1179648 | bytes 9437184 | tf_op jit(solution)/shard_map/stack | solution.py:473
  107.3 1.6 copy.65
  109.0 2.7 copy.63
  111.7 2.7 copy.64
  118.1 32.5 %shard_map.376 = (f32[3136,384]{1,0:T(8,128)}, f32[384,1152]{1,0:T(8,128)}, f32[2,8,384]{2,1,0:T(8,128)}, f32[2,8,384]{2,1,0:T(8,128)}, f32[3,56,256]{2,1,0:T(8,128)}) custom-call(s32[1]{0:T(128)} %bitcast.narrow_ref, s32[16]{0:T(128)} %sides.5, bf16[3136,384]{1,0:T(8,128)(2,1)} %cot.3, bf16[384,1536]{1,0:T(8,128)(2,1)} %copy-done.1, f32[8,384]{1,0:T(8,128)} %vec.5, ...), custom_call_target="tpu_custom_call" | custom-call | flops 7398752256 | bytes 20000000 | tf_op jit(solution)/shard_map/pallas_call | solution.py:366
  150.7 3.4 pad_maximum_fusion.1
  154.1 3.2 pad_maximum_fusion.3
  159.4 1.4 reduce_sum.78
  162.0 1.7 copy.62
  163.7 1.9 reshape.58
  166.9 2.9 fusion.7
  170.5 113.9 %all-reduce.1 = (f32[4]{0:T(128)S(1)}, f32[169,12]{0,1:T(8,128)}, f32[8,384]{1,0:T(8,128)}) all-reduce(f32[4]{0:T(128)} %pad_maximum_fusion.3, f32[169,12]{0,1:T(8,128)} %fusion.7, f32[8,384]{1,0:T(8,128)} %pad_maximum_fusion.2), channel_id=1, replica_groups=mesh['wide'=8,'narrow'=4] {'wide','narrow'}, use_global_device_ids=true, to_apply=%region_4.5 | all-reduce | flops 5104 | bytes 40832 | tf_op jit(solution)/shard_map/psum | solution.py:472
  285.0 1.4 reduce_sum.79
  287.0 11.0 %all-reduce = f32[1536]{0:T(1024)} all-reduce(f32[1536]{0:T(1024)} %reduce_sum.79), channel_id=3, replica_groups=mesh['wide'=8,'narrow'=4] {'narrow'}, use_global_device_ids=true, to_apply=%region_14.15.clone | all-reduce | flops 1536 | bytes 12288
  299.4 12.9 %psum.47 = f32[384]{0:T(512)S(1)} all-reduce(f32[384]{0:T(512)} %dynamic-slice.1), channel_id=1, replica_groups=mesh['wide'=8,'narrow'=4] {'wide'}, use_global_device_ids=true, to_apply=%region_15.16 | all-reduce | flops 384 | bytes 3072 | tf_op jit(solution)/shard_map/psum | solution.py:475
  316.1 1.4 multiply_subtract_fusion.2
  317.5 62.6 %all-reduce.5.cloned.1.call-done = f32[384,1536]{1,0:T(8,128)} async-done(((f32[384,1536]{1,0:T(8,128)}), f32[384,1536]{1,0:T(8,128)}) %all-reduce.5.cloned.1.call-update) | async-done | bytes 2359312 | tf_op jit(solution)/shard_map/psum | solution.py:476
  380.1 7.6 %fusion.21 = (bf16[384,1536]{1,0:T(8,128)(2,1)}, f32[384,1536]{1,0:T(8,128)}, f32[384,1536]{1,0:T(8,128)}, f32[384,1536]{1,0:T(8,128)}) fusion(f32[384,1536]{1,0:T(8,128)S(1)} %copy-done, f32[384,1536]{1,0:T(8,128)} %all-reduce.5.cloned.1.call-done, f32[384,1536]{1,0:T(8,128)} %param.27, f32[384,1536]{1,0:T(8,128)} %param.28), kind=kLoop, calls=%fused_computation.44 | loop fusion | flops 8257536 | bytes 17694720 | tf_op jit(solution)/shard_map/convert_element_type | solution.py:483
  387.7 51.9 %all-reduce.7.cloned.1.call-done = f32[2,384,384]{1,2,0:T(8,128)} async-done(((f32[2,384,384]{1,2,0:T(8,128)}), f32[2,384,384]{1,2,0:T(8,128)}) %all-reduce.7.cloned.1.call-update) | async-done | bytes 1179664 | tf_op jit(solution)/shard_map/psum | solution.py:473
  439.6 4.0 fusion.17
  443.6 2.7 copy.67
  446.3 1.4 copy.69
  447.6 1.4 copy.70
  (42 shorter events, 17.8 us)
Async XLA Ops:
  7.2 2.4 copy-start
  7.2 56.2 %all-gather.3.cloned.1.call-start = ((), (), s32[]{:S(2)}) async-start(), calls=%async_computation.1 | async-start | bytes 2949120 | tf_op jit(solution)/shard_map/all_gather | solution.py:466
  9.5 0.7 copy-start.4
  9.6 307.9 %reduce-scatter.2.cloned.1.call-start = ((), (), s32[]{:S(2)}) async-start(), calls=%async_computation.3 | async-start | bytes 5898240 | tf_op jit(solution)/shard_map/reduce_scatter | solution.py:473
  9.8 23.7 %copy-start.1 = (bf16[384,1536]{1,0:T(8,128)(2,1)}, bf16[384,1536]{1,0:T(8,128)(2,1)S(1)}, u32[]{:S(2)}) copy-start(bf16[384,1536]{1,0:T(8,128)(2,1)S(1)} %convert_element_type.14.wq) | copy-start | bytes 3538948
  107.1 273.0 %all-reduce.5.cloned.1.call-start = ((), (), s32[]{:S(2)}) async-start(), calls=%async_computation.2 | async-start | bytes 4718592 | tf_op jit(solution)/shard_map/psum | solution.py:476
  109.0 5.3 %copy-start.7 = (u32[32]{0:T(128)S(1)}, u32[32]{0:T(128)}, u32[]{:S(2)}) copy-start(u32[32]{0:T(128)} %constant.78) | copy-start | bytes 388
  109.0 8.5 %copy-start.5 = (f32[8,384]{1,0:T(8,128)S(1)}, f32[8,384]{1,0:T(8,128)}, u32[]{:S(2)}) copy-start(f32[8,384]{1,0:T(8,128)} %get-tuple-element.50) | copy-start | bytes 36868
  154.0 160.7 %copy-start.3 = (f32[8,384]{1,0:T(8,128)S(1)}, f32[8,384]{1,0:T(8,128)}, u32[]{:S(2)}) copy-start(f32[8,384]{1,0:T(8,128)} %vec.5) | copy-start | bytes 36868
  154.0 285.5 %all-reduce.7.cloned.1.call-start = ((), (), s32[]{:S(2)}) async-start(), calls=%async_computation.4 | async-start | bytes 2359296 | tf_op jit(solution)/shard_map/psum | solution.py:473
  284.4 13.6 %copy-start.6 = (f32[4]{0:T(128)}, f32[4]{0:T(128)S(1)}, u32[]{:S(2)}) copy-start(f32[4]{0:T(128)S(1)} %get-tuple-element.122) | copy-start | bytes 52
  446.3 2.8 copy-start.2
Sparse Core Ops, SparseCore 0:
  10.2 53.2 all-gather.2
  107.2 130.4 reduce-scatter.1
  243.8 136.2 all-reduce.4
  383.5 56.0 all-reduce.6

commit v2 on v1

--- a/solution.py
+++ b/solution.py
@@ -1,3 +1,5 @@
+import functools
+
 import jax
 import jax.numpy as jnp
 import numpy as np
@@ -207,8 +209,8 @@
 
 
 def mlp_both(narrow_ref, sides, tok, cot, w1, w2, wo, vec, hidden_bias, rinfo, mixed_in, stream_in,
-             out_ref, grad_stream_out, grad_mixed_out, dw1, dw2, dwo, dbias, dvec, stat_out,
-             out32, cot32, stage, cs, gm, idx, lim_r, lim_c, count):
+             out_ref, grad_stream_out, grad_mixed_out, dmlp, dwo, dbias, dvec, stat_out,
+             dw1, dw2, out32, cot32, stage, cs, gm, idx, lim_r, lim_c, count):
     step = pl.program_id(0)
     wins = tok.shape[0] // WTOK
     width = tok.shape[1]
@@ -280,11 +282,19 @@
     @pl.when(step == pl.num_programs(0) - 1)
     def _():
         gather_back(out32, stage, out_ref)
-
-
-def attn_backward(narrow_ref, sides, cot, wq, vec, rinfo, hmask, x_in, qkv_in, prob_in, grad_mixed_in, grad_stream_in,
-                  input_grad, dwq, dbias, dvec, dtable,
-                  ig32, stage, dp, gs, idx, lim_r, lim_c, count):
+        parts, twice, _ = dmlp.shape
+        share = twice // 2
+        for j, ref in enumerate((dw1, dw2)):
+            for t in range(hidden // tile):
+                turned = ref[:, tile * t : tile * t + tile].T
+                for piece in range(tile // share):
+                    n = (tile * t) // share + piece
+                    dmlp[n, share * j : share * j + share, :] = turned[share * piece : share * piece + share, :]
+
+
+def attn_backward(narrow_ref, sides, cot, wq, vec, hmask, hot, dvec2, dhid, stat0, stat1, x_in, qkv_in, prob_in, grad_mixed_in, grad_stream_in,
+                  input_grad, dwq, misc,
+                  dbias, dvec, dtable, flat, ig32, stage, dp, gs, idx, lim_r, lim_c, count):
     step = pl.program_id(0)
     wins = cot.shape[0] // WTOK
     width = cot.shape[1]
@@ -327,7 +337,7 @@
         low = (xhat * vec[0:1] + vec[1:2]).astype(bf16)
         for j in range(3):
             cols = slice(width * j, width * j + width)
-            dwq[:, cols] += tn(low, dproj[:, cols])
+            dwq[j] += tn(low, dproj[:, cols])
         dbias[0] += fold_rows(dproj[:, :width].astype(f32))
         dbias[1] += fold_rows(dproj[:, 2 * width :].astype(f32))
         grad_normed = nt(dproj, wq[:, : 3 * width])
@@ -342,6 +352,32 @@
     @pl.when(step == pl.num_programs(0) - 1)
     def _():
         gather_back(ig32, stage, input_grad)
+        rows = [dvec[0], dvec[1], dbias[0], dbias[1], dvec2[3], dvec2[0], dvec2[1], dvec2[2]]
+        for i, part in enumerate(rows):
+            misc[i : i + 1, :] = jnp.sum(part, 0, keepdims=True)
+        hid = jnp.sum(dhid[...], 0, keepdims=True)
+        for i in range(hid.shape[1] // width):
+            misc[8 + i : 9 + i, :] = hid[:, width * i : width * i + width]
+        lane = lax.broadcasted_iota(jnp.int32, (1, width), 1)
+        line = jnp.zeros((1, width), f32)
+        for i, part in enumerate((stat0[0], stat0[1], stat1[...])):
+            line = jnp.where(lane == i, jnp.sum(part), line)
+        misc[12:13, :] = jnp.where(lane == 3, jnp.sum(stat0[2]) / 128.0, line)
+        misc[13:16, :] = jnp.zeros((3, width), f32)
+        flat[...] = jnp.zeros_like(flat)
+        for g in range(groups):
+            for k in range(WTOK):
+                line = dtable[g, k : k + 1, :]
+                for h in range(HG):
+                    flat[HG * g + h : HG * g + h + 1, SLOT * k : SLOT * k + SLOT] = line[:, SLOT * h : SLOT * h + SLOT]
+        rest = flat[...]
+        misc[16:32, :] = jnp.zeros((16, width), f32)
+        total = jnp.zeros((16, 256), f32)
+        for _ in range(3):
+            part = rest.astype(bf16)
+            total += nn(part, hot[...])
+            rest = rest - part.astype(f32)
+        misc[16:32, :256] = total
 
 
 def whole(a):
@@ -383,6 +419,303 @@
     )(*scalars, *wholes, *chunked)
 
 
+def loop_rows(total, body):
+    size = next(n for n in (96, 64, 48, 32, 16) if total % n == 0)
+    lax.fori_loop(0, total // size, lambda i, c: (body(pl.multiple_of(i * size, size), size), c)[1], 0)
+
+
+def reduce_all(wide_n, narrow_n, share, m_ref, q_ref, o_ref, s_ref, gm_out, gt_out, s_out,
+               send0, recv0, accm, acct, zsend, zrecv, gm, gt, sbuf, srecv, szrecv, *rest):
+    send_sem, recv_sem = rest[-2:]
+    bufs = rest[:-2]
+    me_w = lax.axis_index("wide")
+    me_n = lax.axis_index("narrow")
+    width = accm.shape[2]
+    n_bits = wide_n.bit_length() - 1
+    bit = [lax.rem(me_w // (1 << b), 2) for b in range(n_bits)]
+    mate = [me_w + (1 - 2 * bit[b]) * (1 << b) for b in range(n_bits)]
+    peer = [lax.rem(me_n + s, narrow_n) for s in range(1, narrow_n)]
+    sems = [0]
+
+    def copy(src, dst, dev):
+        k = sems[0]
+        sems[0] += 1
+        return pltpu.make_async_remote_copy(src_ref=src, dst_ref=dst, send_sem=send_sem.at[k], recv_sem=recv_sem.at[k],
+                                            device_id=dev, device_id_type=pl.DeviceIdType.MESH)
+
+    def at_wide(b):
+        return (mate[b], me_n)
+
+    barrier = pltpu.get_barrier_semaphore()
+    for b in range(n_bits):
+        pl.semaphore_signal(barrier, inc=1, device_id=at_wide(b), device_id_type=pl.DeviceIdType.MESH)
+    for n in peer:
+        pl.semaphore_signal(barrier, inc=1, device_id=(me_w, n), device_id_type=pl.DeviceIdType.MESH)
+    pl.semaphore_wait(barrier, n_bits + narrow_n - 1)
+
+    hm, ht = accm.shape[1], acct.shape[1]
+
+    def attn_rows(n, start, size):
+        flat = n * share
+        if flat < q_ref.shape[0]:
+            return q_ref[pl.ds(flat + start, size), :]
+        return o_ref[pl.ds(flat - q_ref.shape[0] + start, size), :]
+
+    away_m, away_t = (1 - bit[0]) * hm, (1 - bit[0]) * ht
+    keep_m, keep_t = bit[0] * hm, bit[0] * ht
+    sbuf[0] = s_ref[...]
+    first = [copy(sbuf.at[0], srecv.at[0], at_wide(0))]
+    first[0].start()
+    for n in range(narrow_n):
+        def pack_m(i, size):
+            send0[n, pl.ds(i, size), :] = m_ref[n, pl.ds(pl.multiple_of(away_m + i, 16), size), :]
+        def pack_t(i, size):
+            send0[n, pl.ds(hm + i, size), :] = attn_rows(n, pl.multiple_of(away_t + i, 16), size)
+        loop_rows(hm, pack_m)
+        loop_rows(ht, pack_t)
+        c = copy(send0.at[n], recv0.at[n], at_wide(0))
+        c.start()
+        first.append(c)
+    first[0].wait()
+    sbuf[1] = sbuf[0] + srecv[0]
+    for n in range(narrow_n):
+        first[n + 1].wait()
+        def add_m(i, size):
+            accm[n, pl.ds(i, size), :] = m_ref[n, pl.ds(pl.multiple_of(keep_m + i, 16), size), :] + recv0[n, pl.ds(i, size), :]
+        def add_t(i, size):
+            acct[n, pl.ds(i, size), :] = attn_rows(n, pl.multiple_of(keep_t + i, 16), size) + recv0[n, pl.ds(hm + i, size), :]
+        loop_rows(hm, add_m)
+        loop_rows(ht, add_t)
+
+    streams, plan = plan_streams(n_bits, hm, ht)
+    place = {st: streams[st][0] for st in streams}
+    steps = n_bits - 1
+    at = 0
+    trail = []
+    for s in range(steps):
+        copies = []
+        c = copy(sbuf.at[1 + s], srecv.at[1 + s], at_wide(plan["A"][s]))
+        c.start()
+        copies.append((None, None, None, None, None, None, c))
+        for st in streams:
+            start, size0, acc_name, name = streams[st]
+            acc = accm if acc_name == "m" else acct
+            b = plan[name][s]
+            rows = plan[st][s]
+            halves = plan[st][s + 1] < rows
+            size = plan[st][s + 1]
+            send, recv = bufs[2 * at], bufs[2 * at + 1]
+            at += 1
+            here = place[st]
+            if halves:
+                out_at, in_at = here + (1 - bit[b]) * size, here + bit[b] * size
+            else:
+                out_at, in_at = here, here
+            for n in range(narrow_n):
+                def pack(i, k):
+                    send[n, pl.ds(i, k), :] = acc[n, pl.ds(pl.multiple_of(out_at + i, 16), k), :].astype(bf16)
+                loop_rows(size, pack)
+            c = copy(send, recv, at_wide(b))
+            c.start()
+            copies.append((acc, send, recv, in_at, size, halves, c))
+            trail.append((st, s, b, in_at, size, halves))
+            place[st] = in_at
+        for acc, send, recv, in_at, size, halves, c in copies:
+            c.wait()
+            if acc is None:
+                sbuf[2 + s] = sbuf[1 + s] + srecv[1 + s]
+                continue
+            for n in range(narrow_n):
+                def add(i, k):
+                    here = pl.ds(pl.multiple_of(in_at + i, 16), k)
+                    mine = acc[n, here, :] if halves else send[n, pl.ds(i, k), :].astype(f32)
+                    acc[n, here, :] = mine + recv[n, pl.ds(i, k), :].astype(f32)
+                loop_rows(size, add)
+
+    base = {}
+    total = 0
+    for st in streams:
+        base[st] = total
+        total += plan[st][steps]
+    copies = []
+    for i, n in enumerate(peer):
+        c = copy(sbuf.at[n_bits], szrecv.at[i], (me_w, n))
+        c.start()
+        copies.append(c)
+    for i, n in enumerate(peer):
+        for st in streams:
+            acc = accm if streams[st][2] == "m" else acct
+            def pack(r, k):
+                zsend[i, pl.ds(base[st] + r, k), :] = acc[n, pl.ds(pl.multiple_of(place[st] + r, 16), k), :].astype(bf16)
+            loop_rows(plan[st][steps], pack)
+        c = copy(zsend.at[i], zrecv.at[i], (me_w, n))
+        c.start()
+        copies.append(c)
+    for c in copies:
+        c.wait()
+    for st in streams:
+        is_m = streams[st][2] == "m"
+        acc = accm if is_m else acct
+        top = (keep_m if is_m else keep_t) + place[st]
+        def add(r, k):
+            value = acc[me_n, pl.ds(pl.multiple_of(place[st] + r, 16), k), :]
+            for i in range(narrow_n - 1):
+                value = value + zrecv[i, pl.ds(base[st] + r, k), :].astype(f32)
+            if is_m:
+                gm[pl.ds(pl.multiple_of(top + r, 16), k), :] = value.astype(bf16)
+            else:
+                gt[me_n, pl.ds(pl.multiple_of(top + r, 16), k), :] = value.astype(bf16)
+        loop_rows(plan[st][steps], add)
+
+    copies = []
+    for st in streams:
+        if streams[st][2] == "t":
+            where = pl.ds(pl.multiple_of(keep_t + place[st], 16), plan[st][steps])
+            for n in peer:
+                c = copy(gt.at[me_n, where, :], gt.at[me_n, where, :], (me_w, n))
+                c.start()
+                copies.append(c)
+    szero = sbuf[n_bits]
+    total_s = jnp.zeros_like(szero)
+    for n in range(narrow_n):
+        behind = lax.rem(me_n + narrow_n - n, narrow_n)
+        value = szero
+        for i in range(1, narrow_n):
+            value = jnp.where(behind == i, szrecv[i - 1], value)
+        total_s = total_s + value
+    s_out[...] = total_s
+    pending = copies
+    for s in reversed(range(steps)):
+        for c in pending:
+            c.wait()
+        pending = []
+        for st, s2, b, in_at, size, halves in trail:
+            if s2 != s or not halves:
+                continue
+            is_m = streams[st][2] == "m"
+            where = pl.ds(pl.multiple_of((keep_m if is_m else keep_t) + in_at, 16), size)
+            if is_m:
+                c = copy(gm.at[where, :], gm.at[where, :], at_wide(b))
+            else:
+                c = copy(gt.at[:, where, :], gt.at[:, where, :], at_wide(b))
+            c.start()
+            pending.append(c)
+    for c in pending:
+        c.wait()
+    wm, wt = pl.ds(pl.multiple_of(keep_m, 16), hm), pl.ds(pl.multiple_of(keep_t, 16), ht)
+    last = [copy(gm.at[wm, :], gm.at[wm, :], at_wide(0)), copy(gt.at[:, wt, :], gt.at[:, wt, :], at_wide(0))]
+    for c in last:
+        c.start()
+    for c in last:
+        c.wait()
+    gm_out[...] = gm[...]
+    gt_out[...] = gt[...]
+
+
+def plan_streams(n_bits, hm, ht):
+    rest = list(range(1, n_bits))
+    half = len(rest) // 2
+    plan = {"A": rest, "B": rest[half:] + rest[:half]}
+    cut_m, cut_t = hm // 2, ht * 2 // 3
+    streams = {"mA": (0, cut_m, "m", "A"), "mB": (cut_m, hm - cut_m, "m", "B"),
+               "tA": (0, cut_t, "t", "A"), "tB": (cut_t, ht - cut_t, "t", "B")}
+    for st, (_, size, _, _) in streams.items():
+        sizes = [size]
+        for _ in rest:
+            sizes.append(sizes[-1] // 2 if sizes[-1] % 32 == 0 else sizes[-1])
+        plan[st] = sizes
+    return streams, plan
+
+
+def reduce_call(wide_n, narrow_n, dmlp, dq, do, misc):
+    parts, twice, width = dmlp.shape
+    share = twice // 2
+    hm, ht = share, share // 2
+    n_bits = wide_n.bit_length() - 1
+    streams, plan = plan_streams(n_bits, hm, ht)
+    scratch = [
+        pltpu.VMEM((narrow_n, hm + ht, width), f32), pltpu.VMEM((narrow_n, hm + ht, width), f32),
+        pltpu.VMEM((narrow_n, hm, width), f32), pltpu.VMEM((narrow_n, ht, width), f32)]
+    last = sum(plan[st][-1] for st in streams)
+    scratch += [pltpu.VMEM((narrow_n - 1, last, width), bf16)] * 2
+    scratch += [pltpu.VMEM((twice, width), bf16), pltpu.VMEM((narrow_n, share, width), bf16)]
+    scratch += [pltpu.VMEM((n_bits + 1,) + misc.shape, f32), pltpu.VMEM((n_bits,) + misc.shape, f32),
+                pltpu.VMEM((narrow_n - 1,) + misc.shape, f32)]
+    for s in range(n_bits - 1):
+        for st in streams:
+            scratch += [pltpu.VMEM((narrow_n, plan[st][s + 1], width), bf16)] * 2
+    copies = 1 + narrow_n + (n_bits - 1) * 5 + 2 * (narrow_n - 1) + 2 * (narrow_n - 1) + (n_bits - 1) * 4 + 2
+    scratch += [pltpu.SemaphoreType.DMA((copies,)), pltpu.SemaphoreType.DMA((copies,))]
+    vmem = pl.BlockSpec(memory_space=pltpu.VMEM)
+    return pl.pallas_call(
+        functools.partial(reduce_all, wide_n, narrow_n, share),
+        out_shape=[sds((twice, width), bf16), sds((narrow_n, share, width), bf16), sds(misc.shape, f32)],
+        in_specs=[vmem] * 4, out_specs=[vmem] * 3, scratch_shapes=scratch,
+        compiler_params=pltpu.CompilerParams(collective_id=0, has_side_effects=True, vmem_limit_bytes=60 * 1024 * 1024),
+    )(dmlp, dq, do, misc)
+
+
+def adam_kernel(narrow_ref, gt, gm, misc, aw, af, as_, mw, mf, ms, tw, tf, ts, vw, vf, vs, bw, bf, bs,
+                rms, an, al, afn, asn, mn, ml, mfn, msn, tn_, tfn, tsn, vn, vfn, vsn, bn, bfn, bsn):
+    def put(new, w, g, m, v, rate, decay, low=None):
+        out = adam_step(w, g, m, v, rate, decay)
+        for ref, value in zip(new, out):
+            ref[...] = value.reshape(ref.shape)
+        if low is not None:
+            low[...] = out[0].astype(bf16).reshape(low.shape)
+
+    put((an, afn, asn), aw[...], gt[0].astype(f32), af[...], as_[...], 0.02, 0.05, al)
+    put((mn, mfn, msn), mw[0], gm[0].astype(f32), mf[0], ms[0], 0.02, 0.05, ml)
+
+    @pl.when(pl.program_id(0) == 0)
+    def _():
+        put((vn, vfn, vsn), vw[...], misc[0:8, :], vf[...], vs[...], 0.3, 0.0)
+        stats = misc[12:13, :]
+        for i in range(3):
+            ratio = jnp.sqrt(stats[:, i : i + 1] / (stats[:, 3:4] * misc.shape[1]))
+            rms[i] = ratio[0, 0]
+        n = narrow_ref[0]
+        share = bw.shape[1]
+        grad = jnp.zeros((1, share), f32)
+        per = misc.shape[1] // share
+        for i in range(4):
+            for k in range(per):
+                grad = jnp.where(n == per * i + k, misc[8 + i : 9 + i, share * k : share * k + share], grad)
+        put((bn, bfn, bsn), bw[...], grad, bf[...], bs[...], 0.1, 0.0)
+        turned = jnp.concatenate([misc[16:32, :256], jnp.zeros((112, 256), f32)], 0).T
+        count, heads = tw.shape
+        put((tn_, tfn, tsn), tw[...], turned[:count, :heads], tf[...], ts[...], 0.3, 0.0)
+
+
+def adam_call(narrow, gt, gm, misc, attn, mlp, table, vec, bias):
+    width = gm.shape[1]
+    share = mlp[0].shape[1]
+    gt = gt.reshape(4, width, width)
+    quarter = share // 2
+    gm = gm.reshape(4, quarter, width)
+    mlp = [a.reshape(4, quarter, width) for a in mlp]
+    bias = [a.reshape(1, -1) for a in bias]
+    col = pl.BlockSpec((width, width), lambda j, *_: (0, j))
+    lead = lambda r: pl.BlockSpec((1, r, width), lambda j, *_: (j, 0, 0))
+    smalls = list(table) + list(vec) + list(bias)
+    args = [gt, gm, misc] + list(attn) + mlp + smalls
+    in_specs = [lead(width), lead(quarter), whole(misc)] + [col] * 3 + [lead(quarter)] * 3 + [whole(a) for a in smalls]
+    three = lambda a: [sds(a.shape, f32)] * 3
+    outs = [sds((3,), f32), sds(attn[0].shape, f32), sds(attn[0].shape, bf16)] + [sds(attn[0].shape, f32)] * 2
+    outs += [sds(mlp[0].shape, f32), sds(mlp[0].shape, bf16)] + [sds(mlp[0].shape, f32)] * 2
+    outs += three(table[0]) + three(vec[0]) + three(bias[0])
+    out_specs = [pl.BlockSpec(memory_space=pltpu.SMEM)] + [col] * 4 + [lead(quarter)] * 4
+    out_specs += [whole(a) for a in smalls]
+    r = pl.pallas_call(
+        adam_kernel,
+        grid_spec=pltpu.PrefetchScalarGridSpec(num_scalar_prefetch=1, grid=(4,), in_specs=in_specs, out_specs=out_specs),
+        out_shape=outs,
+        compiler_params=pltpu.CompilerParams(vmem_limit_bytes=60 * 1024 * 1024),
+    )(narrow, *args)
+    full = (2, share, width)
+    return [r[0], *r[1:5], *r[9:12], *r[12:15], *[a.reshape(full) for a in r[5:9]], *[a.reshape(-1) for a in r[15:18]]]
+
+
 def bias_layout(rel_table):
     pos = np.arange(WTOK)
     row, col = pos // WIN, pos % WIN
@@ -402,7 +735,7 @@
     return jnp.where(dead, -1e30, b), hot
 
 
-def block(tokens, grid_sizes, cotangent, attn_weight, rel_table, vectors, w1, w2, mlp_bias, narrow):
+def block(tokens, grid_sizes, cotangent, attn_weight, rel_table, vectors, w1, w2, mlp_bias, narrow, parts):
     rows, width = tokens.shape
     wins = rows // WTOK
     heads = rel_table.shape[1]
@@ -424,31 +757,27 @@
         [slots32, stage, pltpu.VMEM((CR + 16, width), f32),
          pltpu.VMEM((CR + 16, 3 * width), f32), pltpu.VMEM((CR + 16, width), f32)],
         steps, 8 * rows * width * width)
-    outputs, grad_stream, grad_mixed, dw1, dw2, dwo, dhid, dvec2, stat1 = call(
+    outputs, grad_stream, grad_mixed, dmlp, dwo, dhid, dvec2, stat1 = call(
         mlp_both, scal, (tokens, cotangent, w1, w2, weight_low[:, 3 * width :], vectors, mlp_bias.reshape(1, -1), rinfo),
         (mixed, stream), None, None,
         [("w", (rows, width), bf16), ("c", (steps, CR, width), f32), ("c", (steps, CW, SLOT, width), bf16),
-         ("w", (width, w1.shape[0]), f32), ("w", (width, w1.shape[0]), f32), ("w", (width, width), f32),
+         ("w", (parts, 2 * w1.shape[0] // parts, width), f32), ("w", (width, width), f32),
          ("w", (8, w1.shape[0]), f32), ("w", (4, 8, width), f32), ("w", (8, width), f32)],
-        [slots32, slots32, stage,
+        [pltpu.VMEM((width, w1.shape[0]), f32), pltpu.VMEM((width, w1.shape[0]), f32), slots32, slots32, stage,
          pltpu.VMEM((CR + 16, width), f32), pltpu.VMEM((CR + 16, width), f32)],
         steps, 52 * rows * width * width)
-    input_grad, dwq, dqv, dvec1, dtab = call(
-        attn_backward, scal, (cotangent, weight_low, vectors, rinfo, hmask),
+    hot2 = np.zeros((KR * SLOT, 256), np.float32)
+    lay = bias_layout(rel_table).reshape(-1)
+    hot2[np.arange(KR * SLOT)[lay >= 0], lay[lay >= 0]] = 1.0
+    input_grad, dwq, misc = call(
+        attn_backward, scal, (cotangent, weight_low, vectors, hmask, jnp.asarray(hot2, bf16), dvec2, dhid, stat0, stat1),
         (x, qkv, prob, grad_mixed, grad_stream), None, None,
-        [("w", (rows, width), f32), ("w", (width, 3 * width), f32), ("w", (2, 8, width), f32), ("w", (2, 8, width), f32),
-         ("w", (groups, KR, HG * SLOT), f32)],
-        [slots32, stage, pltpu.VMEM((CR + 16, 3 * width), f32), pltpu.VMEM((CR + 16, width), f32)],
+        [("w", (rows, width), f32), ("w", (3, width, width), f32), ("w", (32, width), f32)],
+        [pltpu.VMEM((2, 8, width), f32), pltpu.VMEM((2, 8, width), f32), pltpu.VMEM((groups, KR, HG * SLOT), f32),
+         pltpu.VMEM((16, KR * SLOT), f32),
+         slots32, stage, pltpu.VMEM((CR + 16, 3 * width), f32), pltpu.VMEM((CR + 16, width), f32)],
         steps, 16 * rows * width * width)
-    dt = dtab.transpose(1, 0, 2).reshape(KR, heads, SLOT)
-    table_grad = jnp.einsum("kqt,khq->th", hot, dt, precision=highest)
-    dqv = jnp.sum(dqv, 1)
-    dvec1 = jnp.sum(dvec1, 1)
-    dvec2 = jnp.sum(dvec2, 1)
-    vector_grad = jnp.stack([dvec1[0], dvec1[1], dqv[0], dqv[1], dvec2[3], dvec2[0], dvec2[1], dvec2[2]])
-    stats = jnp.stack([jnp.sum(stat0[0]), jnp.sum(stat0[1]), jnp.sum(stat1), jnp.sum(stat0[2, :, 0])])
-    attn_grad = jnp.concatenate([dwq, dwo], 1)
-    return outputs, input_grad, stats, attn_grad, table_grad, vector_grad, dw1, dw2, jnp.sum(dhid, 0)
+    return outputs, input_grad, dmlp, dwq, dwo, misc
 
 
 def adam_step(weight, gradient, first_old, second_old, rate_value, decay_value):
@@ -460,36 +789,28 @@
     return (weight - update - rate_value * decay_value * weight, first_new, second_new)
 
 
-def shards(tokens, grid_sizes, cotangent, attn_weight, attn_first, attn_second, rel_table, table_first, table_second,
-           vectors, vector_first, vector_second, mlp_weight, mlp_first, mlp_second, mlp_bias, bias_first, bias_second):
+def shards(wide_n, narrow_n, tokens, grid_sizes, cotangent, attn_weight, attn_first, attn_second, rel_table, table_first,
+           table_second, vectors, vector_first, vector_second, mlp_weight, mlp_first, mlp_second, mlp_bias, bias_first,
+           bias_second):
     width = tokens.shape[1]
     hidden_low = lax.all_gather(mlp_weight.astype(bf16), "narrow", axis=1, tiled=True)
     hidden_bias = lax.all_gather(mlp_bias, "narrow", axis=0, tiled=True)
-    outputs, input_grad, stats, attn_grad, table_grad, vector_grad, dw1, dw2, dhid = block(
+    narrow = lax.axis_index("narrow").reshape(1).astype(jnp.int32)
+    outputs, input_grad, dmlp, dwq, dwo, misc = block(
         tokens, grid_sizes, cotangent, attn_weight, rel_table, vectors, hidden_low[0], hidden_low[1], hidden_bias,
-        lax.axis_index("narrow"))
-    both = ("wide", "narrow")
-    stat_totals = lax.psum(stats, both)
-    weight_grad = lax.psum(lax.psum_scatter(jnp.stack([dw1, dw2]), "narrow", scatter_dimension=2, tiled=True), "wide")
-    weight_grad = weight_grad.transpose(0, 2, 1)
-    hidden_bias_grad = lax.psum(lax.psum_scatter(dhid, "narrow", scatter_dimension=0, tiled=True), "wide")
-    attn_grad, table_grad, vector_grad = lax.psum((attn_grad, table_grad, vector_grad), both)
-    rms_values = jnp.sqrt(stat_totals[:3] / (stat_totals[3] * width))
-    attn_new, attn_first_new, attn_second_new = adam_step(attn_weight, attn_grad, attn_first, attn_second, 0.02, 0.05)
-    table_new, table_first_new, table_second_new = adam_step(rel_table, table_grad, table_first, table_second, 0.3, 0.0)
-    vector_new, vector_first_new, vector_second_new = adam_step(vectors, vector_grad, vector_first, vector_second, 0.3, 0.0)
-    mlp_new, mlp_first_new, mlp_second_new = adam_step(mlp_weight, weight_grad, mlp_first, mlp_second, 0.02, 0.05)
-    bias_new, bias_first_new, bias_second_new = adam_step(mlp_bias, hidden_bias_grad, bias_first, bias_second, 0.1, 0.0)
-    return (outputs, input_grad, rms_values, attn_new, attn_new.astype(bf16), attn_first_new, attn_second_new,
-            table_new, table_first_new, table_second_new, vector_new, vector_first_new, vector_second_new,
-            mlp_new, mlp_new.astype(bf16), mlp_first_new, mlp_second_new, bias_new, bias_first_new, bias_second_new)
+        narrow, narrow_n)
+    gm, gt, misc = reduce_call(wide_n, narrow_n, dmlp, dwq.reshape(3 * width, width), dwo, misc)
+    new = adam_call(narrow, gt, gm, misc, (attn_weight, attn_first, attn_second), (mlp_weight, mlp_first, mlp_second),
+                    (rel_table, table_first, table_second), (vectors, vector_first, vector_second),
+                    (mlp_bias, bias_first, bias_second))
+    return (outputs, input_grad, *new)
 
 
 def solution(mesh):
     rows = P(("wide", "narrow"), None)
     split = P(None, "narrow", None)
     return jax.shard_map(
-        shards, mesh=mesh,
+        functools.partial(shards, mesh.shape["wide"], mesh.shape["narrow"]), mesh=mesh,
         in_specs=(rows, P("wide"), rows) + (P(),) * 9 + (split,) * 3 + (P("narrow"),) * 3,
         out_specs=(rows, rows) + (P(),) * 11 + (split,) * 4 + (P("narrow"),) * 3,
         check_vma=False)

time: 458 us -> 308 us (0.67)
  Pallas kernels: 92.1 us -> 249 us
  blocking collectives: 152 us -> 14.4 us
  waiting for transfers between devices: 120 us -> 5.74 us
  other arithmetic: 42 us -> 7 us
  local copies, waits for them, and re-layouts: 27.9 us -> 13.4 us
    pallas_call x0 -> x2, Pallas kernels: none -> 153 us  [the longest x1 141 us: reduce_call(): pl.pallas_call(functools.partial(reduce_all, wide_n, narrow_n, share), ou...]
    psum x2 -> x0, blocking collectives: 127 us -> none  [the longest x1 114 us: shards(): stat_totals = lax.psum(stats, both)]
    psum x2 -> x0, waiting for transfers between devices: 114 us -> none  [the longest x1 62.6 us: shards(): lax.psum((attn_grad, table_grad, vector_grad), both)]
    convert_element_type x2 -> x0, other arithmetic: 11.6 us -> none  [the longest x1 7.6 us: shards(): attn_new.astype(bf16)]
    unnamed x1 -> x0, blocking collectives: 11 us -> none
    another operation x3 -> x0, other arithmetic: 9.44 us -> none  [the longest x1 4.94 us: shards(): jnp.stack([dw1, dw2])]
    unnamed x26 -> x27, local copies, waits for them, and re-layouts: 16.6 us -> 7.57 us
    reduce_sum x7 -> x0, other arithmetic: 8.14 us -> none  [the longest x1 1.41 us: block(): dvec2 = jnp.sum(dvec2, 1)]
  transfers between devices with their start and end apart: 4 -> 1, of which waited for: 3 -> 1; matrix products, arithmetic and copies ran while one was open for 12% -> 3% of each run, Pallas kernels for 12% -> 8%
where the time goes in v2:
time: 308 us; the launch traced here: 307 us
  Pallas kernels  249 us (81%)
  blocking collectives  14.4 us (5%)
  between operations  14.2 us (5%)
  local copies, waits for them, and re-layouts  13.4 us (4%)
  other arithmetic  7 us (2%)
  waiting for transfers between devices  5.74 us (2%)
    pallas_call x1, Pallas kernels, reduce_call(): pl.pallas_call(functools.partial(reduce_all, wide_n, narrow_n, share), ou...  141 us
    pallas_call x3, Pallas kernels, call(): pl.pallas_call(body, grid_spec=pltpu.PrefetchScalarGridSpec(num_scalar_pr...  96.4 us
    all_gather x1, blocking collectives, shards(): hidden_bias = lax.all_gather(mlp_bias, 'narrow', axis=0, tiled=True)  14.4 us
    pallas_call x1, Pallas kernels, adam_call(): pl.pallas_call(adam_kernel, grid_spec=pltpu.PrefetchScalarGridSpec(num_sc...  11.3 us
    unnamed x27, local copies, waits for them, and re-layouts  7.57 us
  transfers between devices with their start and end apart: 1, of which 1 were waited for; matrix products, arithmetic and copies ran while one was open for 3% of the time, Pallas kernels for 8%

profile of v2, /device:TPU:0, one launch (start us, length us, event | category | flops | bytes accessed | tf_op | source)
XLA Modules:
  0.0 307.0 jit_solution(1853896076296150609)
XLA Ops:
  7.2 0.0 all-gather.3.cloned.1.call-start
  7.3 2.3 convert_element_type.7
  9.6 0.0 all-gather.3.cloned.1.call-update
  9.6 0.6 reshape.113
  10.2 0.6 reshape.103.bw
  10.7 0.1 convert_element_type.8.wq
  10.9 0.0 copy-start.1
  10.9 0.0 copy-start.7
  10.9 0.0 copy-start.9
  11.0 0.7 copy.58.tw
  11.7 3.1 fusion.2
  14.8 0.2 reshape.97
  15.0 0.7 slice.14.wo
  15.7 0.7 copy.59.tf
  16.4 0.7 copy.60.ts
  17.2 0.6 reshape.104.bf
  17.8 0.6 reshape.105.bs
  18.3 14.4 %all-gather = f32[4,1,384]{2,1,0:T(1,128)} all-gather(f32[1,1,384]{2,1,0:T(1,128)S(1)} %copy-done.6), channel_id=1, replica_groups=mesh['wide'=8,'narrow'=4] {'narrow'}, dimensions={0}, use_global_device_ids=true | all-gather | bytes 7680 | tf_op jit(solution)/shard_map/all_gather | solution.py:797
  32.7 0.8 fusion.3.bias
  33.5 24.3 %shard_map.383 = (bf16[13,256,384]{2,1,0:T(8,128)(2,1)}, bf16[13,5,64,1152]{3,2,1,0:T(8,128)(2,1)}, f32[13,5,3,56,256]{4,3,2,1,0:T(8,128)}, bf16[13,256,384]{2,1...) custom-call(s32[1]{0:T(128)} %bitcast.narrow_ref, s32[16]{0:T(128)} %sides.5, bf16[3136,384]{1,0:T(8,128)(2,1)} %tok.3, ...), custom_call_target="tpu_custom_call" | custom-call | flops 3699376128 | bytes 20000000 | tf_op jit(solution)/shard_map/pallas_call | solution.py:402
  57.7 5.7 %all-gather.3.cloned.1.call-done = bf16[2,1536,384]{2,1,0:T(8,128)(2,1)} async-done(((bf16[2,384,384]{2,1,0:T(8,128)(2,1)}), bf16[2,1536,384]{2,1,0:T(8,128)(2,1)}) %all-gather.3.cloned.1.call-update) | async-done | bytes 2359312 | tf_op jit(solution)/shard_map/all_gather | solution.py:796
  63.5 3.3 %slice_bitcast_fusion = (bf16[1536,384]{1,0:T(8,128)(2,1)}, bf16[1536,384]{1,0:T(8,128)(2,1)}) fusion(bf16[2,1536,384]{2,1,0:T(8,128)(2,1)} %all-gather.3.cloned.1.call-done), kind=kLoop, calls=%fused_computation.4 | loop fusion | bytes 4718592 | tf_op jit(solution)/shard_map/squeeze | solution.py:800
  66.7 36.7 %shard_map.384 = (bf16[3136,384]{1,0:T(8,128)(2,1)}, f32[13,256,384]{2,1,0:T(8,128)}, bf16[13,5,64,384]{3,2,1,0:T(8,128)(2,1)}, f32[4,768,384]{2,1,0:T(8,128)}, ...) custom-call(s32[1]{0:T(128)} %bitcast.narrow_ref, s32[16]{0:T(128)} %sides.5, ...), custom_call_target="tpu_custom_call" | custom-call | flops 24045944832 | bytes 20000000 | tf_op jit(solution)/shard_map/pallas_call | solution.py:402
  103.4 35.5 %shard_map.385 = (f32[3136,384]{1,0:T(8,128)}, f32[3,384,384]{2,1,0:T(8,128)}, f32[32,384]{1,0:T(8,128)}) custom-call(s32[1]{0:T(128)} %bitcast.narrow_ref, s32[16]{0:T(128)} %sides.5, bf16[3136,384]{1,0:T(8,128)(2,1)} %cot.3, bf16[384,1536]{1,0:T(8,128)(2,1)} %copy-done.1, f32[8,384]{1,0:T(8,128)} %vw.1, bf16[256,128]{1,0:T(8,128)(2,1)} %constant.24.clone.hmask, ...), custom_call_target="tpu_custom_call" | custom-call | flops 7398752256 | bytes 20000000 | tf_op jit(solution)/shard_map/pallas_call | solution.py:402
  138.9 141.5 %shard_map.386 = (bf16[768,384]{1,0:T(8,128)(2,1)}, bf16[4,384,384]{2,1,0:T(8,128)(2,1)}, f32[32,384]{1,0:T(8,128)}) custom-call(f32[4,768,384]{2,1,0:T(8,128)} %get-tuple-element.71.m_ref, f32[1152,384]{1,0:T(8,128)} %bitcast.23, f32[384,384]{1,0:T(8,128)} %get-tuple-element.73.o_ref, f32[32,384]{1,0:T(8,128)} %get-tuple-element.74.s_ref), custom_call_target="tpu_custom_call" | custom-call | tf_op jit(solution)/shard_map/pallas_call | solution.py:650
  280.4 11.3 %shard_map.387 = (f32[3]{0:T(128)}, f32[384,1536]{1,0:T(8,128)}, bf16[384,1536]{1,0:T(8,128)(2,1)}, f32[384,1536]{1,0:T(8,128)}, f32[384,1536]{1,0:T(8,128)}, /*...) custom-call(s32[1]{0:T(128)} %bitcast.narrow_ref, ...), custom_call_target="tpu_custom_call" | custom-call | tf_op jit(solution)/shard_map/pallas_call | solution.py:709
  291.6 1.6 copy.61
  293.2 1.6 copy.62
  294.8 1.6 copy.63
  296.4 1.3 reduce
  297.6 1.3 reduce.1
  298.9 1.3 reduce.2
  (17 shorter events, 0.0 us)
Async XLA Ops:
  7.2 2.4 copy-start.5
  7.2 3.5 %copy-start = (f32[384,1536]{1,0:T(8,128)S(1)}, f32[384,1536]{1,0:T(8,128)}, u32[]{:S(2)}) copy-start(f32[384,1536]{1,0:T(8,128)} %aw.1) | copy-start | bytes 7077892
  7.2 56.3 %all-gather.3.cloned.1.call-start = ((), (), s32[]{:S(2)}) async-start(), calls=%async_computation | async-start | bytes 2949120 | tf_op jit(solution)/shard_map/all_gather | solution.py:796
  9.6 1.3 copy-start.2
  10.9 22.6 %copy-start.1 = (bf16[384,1536]{1,0:T(8,128)(2,1)}, bf16[384,1536]{1,0:T(8,128)(2,1)S(1)}, u32[]{:S(2)}) copy-start(bf16[384,1536]{1,0:T(8,128)(2,1)S(1)} %convert_element_type.8.wq) | copy-start | bytes 3538948
  10.9 4.8 %copy-start.3 = (f32[169,12]{0,1:T(8,128)S(1)}, f32[169,12]{0,1:T(8,128)}, u32[]{:S(2)}) copy-start(f32[169,12]{0,1:T(8,128)} %param.31) | copy-start | bytes 24340
  10.9 5.5 %copy-start.4 = (f32[169,12]{0,1:T(8,128)S(1)}, f32[169,12]{0,1:T(8,128)}, u32[]{:S(2)}) copy-start(f32[169,12]{0,1:T(8,128)} %param.32) | copy-start | bytes 24340
  10.9 6.3 %copy-start.7 = (f32[384]{0:T(512)S(1)}, f32[384]{0:T(512)}, u32[]{:S(2)}) copy-start(f32[384]{0:T(512)} %param.40) | copy-start | bytes 4612
  10.9 6.8 %copy-start.8 = (f32[384]{0:T(512)S(1)}, f32[384]{0:T(512)}, u32[]{:S(2)}) copy-start(f32[384]{0:T(512)} %param.41) | copy-start | bytes 4612
  10.9 7.4 %copy-start.6 = (f32[1,1,384]{2,1,0:T(1,128)S(1)}, f32[1,1,384]{2,1,0:T(1,128)}, u32[]{:S(2)}) copy-start(f32[1,1,384]{2,1,0:T(1,128)} %reshape.113) | copy-start | bytes 4612
  10.9 21.8 %copy-start.9 = (pred[56]{0:T(512)(128)(4,1)S(1)}, pred[56]{0:T(512)(128)(4,1)}, u32[]{:S(2)}) copy-start(pred[56]{0:T(512)(128)(4,1)} %constant.26) | copy-start | bytes 172
Sparse Core Ops, SparseCore 0:
  10.2 53.2 all-gather.2

commit v3 on v2

v3 whole, which is shorter than its diff:
```python
import functools

import jax
import jax.numpy as jnp
import numpy as np
from jax import lax
from jax.sharding import PartitionSpec as P
from jax.experimental import pallas as pl
from jax.experimental.pallas import tpu as pltpu

WIN = 7
WTOK = 49
WPI = 16
IMG_W = 16
STEP = 5
CW = 16
CR = CW * WTOK
SLOT = 64
KR = 56
HG = 4
LOG2E = 1.4426950408889634

norm_eps = 1e-05
beta_one = 0.5
beta_two = 0.5
adam_eps = 1e-08
highest = lax.Precision.HIGHEST
f32 = jnp.float32
bf16 = jnp.bfloat16


def nn(a, b):
    return lax.dot_general(a, b, (((1,), (0,)), ((), ())), preferred_element_type=f32)


def nt(a, b):
    return lax.dot_general(a, b, (((1,), (1,)), ((), ())), preferred_element_type=f32)


def tn(a, b):
    return lax.dot_general(a, b, (((0,), (0,)), ((), ())), preferred_element_type=f32)


def row_info():
    r = np.arange(CR)
    win = r // WTOK
    p = r % WTOK
    info = np.stack([win, p // WIN, p % WIN]).astype(np.float32)
    info[1, win >= CW] = 1000.0
    return np.ascontiguousarray(np.broadcast_to(info[:, :, None], (3, CR, 128)))


def key_info():
    p = np.arange(KR)
    info = np.stack([p // WIN, p % WIN]).astype(np.float32)
    return np.ascontiguousarray(np.broadcast_to(info[:, :, None], (2, KR, 128)))


def head_mask(head_size):
    row = np.arange(HG * SLOT)
    lane = np.arange(HG * head_size)
    return (((row // SLOT)[:, None] == (lane // head_size)[None, :]) & ((row % SLOT) < WTOK)[:, None]).astype(np.float32)


def fold_rows(t):
    return jnp.sum(t.reshape(t.shape[0] // 8, 8, t.shape[1]), 0)


def rep(v, n):
    return jnp.concatenate([v] * n, 1)


def fill_sides(sides, info, side_s):
    win = info[0]
    value = jnp.zeros_like(win)
    for i in range(CW):
        value = jnp.where(win == float(i), sides[i].astype(f32), value)
    side_s[...] = value


def corner(narrow, step, steps):
    u = WPI - 1 - (narrow * steps + step)
    return (WIN * (u // 4)).astype(f32), (WIN * lax.rem(u, 4)).astype(f32)


def chunk_valid(info, side_s, top, left):
    side = side_s[...]
    return jnp.where((info[1] + top < side) & (info[2] + left < side), 1.0, 0.0)


def norm_stats(x):
    mean = jnp.mean(x, -1, keepdims=True)
    centred = x - mean
    inverse = lax.rsqrt(jnp.mean(centred * centred, -1, keepdims=True) + norm_eps)
    return centred * inverse, inverse


def norm_grad(g, xhat, inverse, gain):
    scaled = g * gain
    m1 = jnp.mean(scaled, -1, keepdims=True)
    m2 = jnp.mean(scaled * xhat, -1, keepdims=True)
    return inverse * (scaled - m1 - xhat * m2)


class Links:
    def __init__(self, wide_n, narrow_n, send_sem, recv_sem):
        self.w = lax.axis_index("wide")
        self.n = lax.axis_index("narrow")
        self.bits = wide_n.bit_length() - 1
        self.bit = [lax.rem(self.w // (1 << b), 2) for b in range(self.bits)]
        self.mate = [self.w + (1 - 2 * self.bit[b]) * (1 << b) for b in range(self.bits)]
        self.peer = [lax.rem(self.n + s, narrow_n) for s in range(1, narrow_n)]
        self.send_sem, self.recv_sem = send_sem, recv_sem
        self.used = 0

    def copy(self, src, dst, device):
        k = self.used
        self.used += 1
        return pltpu.make_async_remote_copy(
            src_ref=src, dst_ref=dst, send_sem=self.send_sem.at[k], recv_sem=self.recv_sem.at[k],
            device_id=device, device_id_type=pl.DeviceIdType.MESH)

    def along(self, b):
        return (self.mate[b], self.n)

    def over(self, n):
        return (self.w, n)

    def barrier(self):
        sem = pltpu.get_barrier_semaphore()
        for b in range(self.bits):
            pl.semaphore_signal(sem, inc=1, device_id=self.along(b), device_id_type=pl.DeviceIdType.MESH)
        for n in self.peer:
            pl.semaphore_signal(sem, inc=1, device_id=self.over(n), device_id_type=pl.DeviceIdType.MESH)
        pl.semaphore_wait(sem, self.bits + len(self.peer))


def gather_cuts(wide_n, rows):
    bits = list(range(min(3, wide_n.bit_length() - 1)))
    first = rows // 256 * 128
    return [(0, first, bits[1:] + bits[:1]), (first, rows - first, bits[1:][::-1] + bits[:1])]


def gather_plan(links, wide_n, own, tail_own, all_w, all_tail):
    narrow_n, rows, _ = all_w.shape
    streams = gather_cuts(wide_n, rows)
    stages = [[]]
    place, sizes = [], []
    for start, size, order in streams:
        piece = size >> len(order)
        off = 0
        for k, b in enumerate(order):
            off = off + links.bit[b] * (piece << k)
        place.append(start + off)
        sizes.append(piece)
    for n in links.peer:
        stages[0].append(links.copy(tail_own, all_tail.at[links.n], links.over(n)))
        for at, size in zip(place, sizes):
            here = pl.ds(pl.multiple_of(at, 16), size)
            stages[0].append(links.copy(own.at[here, :], all_w.at[links.n, here, :], links.over(n)))
    for k in range(len(streams[0][2])):
        stage = []
        for s, (start, size, order) in enumerate(streams):
            here = pl.ds(pl.multiple_of(place[s], 16), sizes[s])
            for n in links.peer:
                part = all_w.at[n, here, :]
                stage.append(links.copy(part, part, links.along(order[k])))
            place[s] = place[s] - links.bit[order[k]] * sizes[s]
            sizes[s] = sizes[s] * 2
        stages.append(stage)
    return stages


def run_stages(stages, step, steps):
    for k, stage in enumerate(stages):
        @pl.when(step == min(k, steps - 1))
        def _():
            if k:
                for c in stages[k - 1]:
                    c.wait()
            for c in stage:
                c.start()


def expand_table(table, hot, wide_t, flat, bias):
    count, heads = table.shape
    wide_t[...] = jnp.zeros_like(wide_t)
    wide_t[:count, :heads] = table[...] * LOG2E
    rest = wide_t[...].T[:16, :]
    total = jnp.zeros((16, hot.shape[0]), f32)
    for _ in range(3):
        part = rest.astype(bf16)
        total += nt(part, hot[...])
        rest = rest - part.astype(f32)
    flat[...] = total
    bias[...] = jnp.full(bias.shape, -1e30, f32)
    for g in range(heads // HG):
        for k in range(WTOK):
            for h in range(HG):
                bias[g, k : k + 1, SLOT * h : SLOT * h + SLOT] = flat[HG * g + h : HG * g + h + 1, SLOT * k : SLOT * k + SLOT]


def turn(t):
    t = jnp.concatenate([t[:, :128], t[:, 128:]], 0).T
    return jnp.concatenate([t[:SLOT], t[SLOT:]], 1)


def padded(t):
    return jnp.concatenate([t, jnp.zeros((SLOT - KR, t.shape[1]), f32)], 0)


def four(t, mask):
    return jnp.concatenate([t] * HG, 0) * mask


BATCH = 8


def attn_forward(wide_n, narrow_n, comm, narrow_ref, sides, tok, attn_w, mlp_w, mlp_b, vec, table, hot, rinfo, kinfo, hmask, hmask2,
                 qkv_s, prob_out, mixed_out, stream_out, stats, gw_out, tail_out,
                 wq, pj, mx, turn_s, bias, wide_t, flat, side_s, own, tail_own, gw, tails, *sems):
    step = pl.program_id(0)
    steps = pl.num_programs(0)
    static_steps = comm[1]
    width = tok.shape[1]
    groups = width // 128
    scale = 32 ** (-0.5)
    narrow = narrow_ref[0]
    share = mlp_w.shape[1]

    @pl.when(step == 0)
    def _():
        for j in range(2):
            own[share * j : share * j + share, :] = mlp_w[j].astype(bf16)
        tail_own[...] = jnp.zeros_like(tail_own)
        rest = mlp_b[...]
        for i in range(3):
            part = rest.astype(bf16).astype(f32)
            tail_own[i : i + 1, :share] = part
            rest = rest - part
        if comm[0]:
            gw[lax.axis_index("narrow")] = own[...]
            tails[lax.axis_index("narrow")] = tail_own[...]
        else:
            for n in range(narrow_n):
                gw[n] = own[...]
                tails[n] = tail_own[...]

    if comm[0]:
        links = Links(wide_n, narrow_n, *sems)

        @pl.when(step == 0)
        def _():
            links.barrier()

        stages = gather_plan(links, wide_n, own, tail_own, gw, tails)
        run_stages(stages, step, static_steps)

    @pl.when(step == 0)
    def _():
        wq[...] = attn_w[...].astype(bf16)
        fill_sides(sides, rinfo, side_s)
        expand_table(table, hot, wide_t, flat, bias)
        for ref in (pj, mx, stats):
            ref[...] = jnp.zeros_like(ref)

    top, left = corner(narrow, step, static_steps)
    x = tok[...].astype(f32)
    valid = chunk_valid(rinfo, side_s, top, left)
    keep = rep(valid, groups)
    xhat, _ = norm_stats(x)
    low = (xhat * vec[0:1] + vec[1:2]).astype(bf16)
    pj[:CR, :width] = nn(low, wq[:, :width]) + vec[2:3]
    pj[:CR, width : 2 * width] = nn(low, wq[:, width : 2 * width])
    pj[:CR, 2 * width :] = nn(low, wq[:, 2 * width : 3 * width]) + vec[3:4]
    for i in range(CW):
        qkv_s[i] = pj[WTOK * i : WTOK * i + SLOT, :].astype(bf16)

    def score(b, carry):
        for k in range(BATCH):
            i = b * BATCH + k
            for g in range(groups):
                q_bd = four(qkv_s[i, :, 128 * g : 128 * g + 128], hmask[...])
                prob_out[i, g] = nt(qkv_s[i, :KR, width + 128 * g : width + 128 * g + 128], q_bd)
        return carry

    def soft(b, carry):
        for k in range(BATCH):
            i = b * BATCH + k
            side = sides[i].astype(f32)
            fill = jnp.where((kinfo[0] < side - top) & (kinfo[1] < side - left), 0.0, -10000.0 * LOG2E)
            fill = rep(fill, 2)
            for g in range(groups):
                s = prob_out[i, g] * (scale * LOG2E) + bias[g] + fill
                e = jnp.exp2(s - jnp.max(s, 0, keepdims=True))
                prob = e * (1.0 / jnp.sum(e, 0, keepdims=True))
                prob_out[i, g] = prob
                turn_s[i, g] = turn(padded(prob).astype(bf16))
        return carry

    lax.fori_loop(0, CW // BATCH, score, 0)
    lax.fori_loop(0, CW // BATCH, soft, 0)
    for i in range(CW):
        for g in range(groups):
            v_bd = four(qkv_s[i, :, 2 * width + 128 * g : 2 * width + 128 * g + 128], hmask2[...])
            mx[WTOK * i : WTOK * i + SLOT, 128 * g : 128 * g + 128] = nn(turn_s[i, g], v_bd)
    mixed = mx[:CR, :].astype(bf16)
    mixed_out[...] = mixed
    branch = (nn(mixed, wq[:, 3 * width :]) + vec[4:5]) * keep
    stream_out[...] = x + branch
    stats[0] += fold_rows(x * x * keep)
    stats[1] += fold_rows(branch * branch)
    stats[2, :, :128] += fold_rows(valid)

    @pl.when(step == steps - 1)
    def _():
        if comm[0]:
            for c in stages[-1]:
                c.wait()
        gw_out[...] = gw[...]
        tail_out[...] = tails[...]


def feed_forward(tile, narrow_ref, sides, cot, mixed_in, stream_in, attn_w, gw, tails, vec, rinfo,
                 out_ref, grad_stream_out, gm_s, dmlp, dwo, dhid, dvec,
                 wo, w1, w2, hb, dw1, dw2, mx, side_s):
    step = pl.program_id(0)
    steps = pl.num_programs(0)
    width = cot.shape[1]
    groups = width // 128
    hidden = w1.shape[0]
    shards_n, twice, _ = gw.shape
    share = twice // 2

    @pl.when(step == 0)
    def _():
        wo[...] = attn_w[...].astype(bf16)
        for n in range(shards_n):
            w1[share * n : share * n + share, :] = gw[n, :share, :]
            w2[share * n : share * n + share, :] = gw[n, share:, :]
            three = tails[n]
            hb[:, share * n : share * n + share] = (three[0:1] + three[1:2] + three[2:3])[:, :share]
        fill_sides(sides, rinfo, side_s)
        for ref in (mx, dw1, dw2, dwo, dhid, dvec):
            ref[...] = jnp.zeros_like(ref)

    top, left = corner(narrow_ref[0], step, steps)
    keep = rep(chunk_valid(rinfo, side_s, top, left), groups)
    cotan = cot[...].astype(f32)
    stream = stream_in[...]
    xhat2, inverse2 = norm_stats(stream)
    second = (xhat2 * vec[5:6] + vec[6:7]).astype(bf16)
    kept_cot = cotan * keep
    grad_low = kept_cot.astype(bf16)
    second_t = jnp.concatenate([second.T, jnp.ones((16, CR), bf16)], 0)
    grad_t = grad_low.T
    mlp_out = jnp.zeros((CR, width), f32)
    grad_second = jnp.zeros((CR, width), f32)
    for t in range(hidden // tile):
        cols = slice(tile * t, tile * t + tile)
        pre = nt(second, w1[cols, :]) + hb[0:1, cols]
        square = pre * pre
        half = 0.5 * jnp.tanh(pre * (square * (0.7978845608028654 * 0.044715) + 0.7978845608028654)) + 0.5
        active = (pre * half).astype(bf16)
        slope = half + (pre * (half - half * half)) * (square * (6 * 0.7978845608028654 * 0.044715) + 2 * 0.7978845608028654)
        grad_pre = (nt(grad_low, w2[cols, :]) * slope).astype(bf16)
        mlp_out += nn(active, w2[cols, :])
        grad_second += nn(grad_pre, w1[cols, :])
        outer = nn(second_t, grad_pre)
        dw1[:, cols] += outer[:width]
        dhid[:, cols] += outer[width : width + 8]
        dw2[:, cols] += nn(grad_t, active)
    branch = (mlp_out + vec[7:8]) * keep
    out_ref[...] = (stream + branch).astype(bf16)
    dvec[4] += fold_rows(branch * branch)
    dvec[0] += fold_rows(grad_second * xhat2)
    dvec[1] += fold_rows(grad_second)
    dvec[2] += fold_rows(kept_cot)
    grad_stream = cotan + norm_grad(grad_second, xhat2, inverse2, vec[5:6])
    grad_stream_out[...] = grad_stream
    grad_attn = grad_stream * keep
    dvec[3] += fold_rows(grad_attn)
    grad_attn_low = grad_attn.astype(bf16)
    dwo[...] += nn(mixed_in[...].T, grad_attn_low)
    mx[:CR, :] = nt(grad_attn_low, wo[...])
    for i in range(CW):
        gm_s[i] = mx[WTOK * i : WTOK * i + SLOT, :].astype(bf16)

    @pl.when(step == steps - 1)
    def _():
        for j, ref in enumerate((dw1, dw2)):
            for t in range(hidden // width):
                turned = ref[:, width * t : width * t + width].T
                for k in range(width // share):
                    n = (width * t) // share + k
                    dmlp[n, share * j : share * j + share, :] = turned[share * k : share * k + share, :]


def scatter_sizes(wide_n, share):
    n_bits = wide_n.bit_length() - 1
    rest = list(range(1, n_bits))
    half = len(rest) // 2
    plan = {"A": rest, "B": rest[half:] + rest[:half]}
    cut = share // 2
    streams = {"A": (0, cut), "B": (cut, share - cut)}
    sizes = {}
    for st, (_, size) in streams.items():
        sizes[st] = [size]
        for _ in rest:
            sizes[st].append(sizes[st][-1] // 2 if sizes[st][-1] % 32 == 0 else sizes[st][-1])
    return plan, streams, sizes


def scatter_stages(links, wide_n, narrow_n, share, dmlp, mine_out, send0, recv0, acc, zsend, zrecv, bufs):
    plan, streams, sizes = scatter_sizes(wide_n, share)
    bit = links.bit
    keep0, away0 = bit[0] * share, (1 - bit[0]) * share
    stages = []

    def pack0():
        for n in range(narrow_n):
            def one(i, size):
                send0[n, pl.ds(i, size), :] = dmlp[n, pl.ds(pl.multiple_of(away0 + i, 16), size), :].astype(send0.dtype)
            loop_rows(share, one)

    def add0():
        for n in range(narrow_n):
            def one(i, size):
                acc[n, pl.ds(i, size), :] = (dmlp[n, pl.ds(pl.multiple_of(keep0 + i, 16), size), :]
                                             + recv0[n, pl.ds(i, size), :].astype(f32))
            loop_rows(share, one)

    stages.append((pack0, [links.copy(send0, recv0, links.along(0))], add0))
    place = {st: streams[st][0] for st in streams}
    trail = []
    for s in range(links.bits - 1):
        work = []
        for k, st in enumerate(streams):
            b = plan[st][s]
            size = sizes[st][s + 1]
            halves = size < sizes[st][s]
            send, recv = bufs[2 * (2 * s + k)], bufs[2 * (2 * s + k) + 1]
            here = place[st]
            out_at, in_at = (here + (1 - bit[b]) * size, here + bit[b] * size) if halves else (here, here)
            place[st] = in_at
            work.append((send, recv, out_at, in_at, size, halves, links.copy(send, recv, links.along(b))))
            trail.append((st, s, b, in_at, size, halves))

        def pack(work=work):
            for send, recv, out_at, in_at, size, halves, _ in work:
                for n in range(narrow_n):
                    def one(i, k):
                        send[n, pl.ds(i, k), :] = acc[n, pl.ds(pl.multiple_of(out_at + i, 16), k), :].astype(send.dtype)
                    loop_rows(size, one)

        def add(work=work):
            for send, recv, out_at, in_at, size, halves, _ in work:
                for n in range(narrow_n):
                    def one(i, k):
                        here = pl.ds(pl.multiple_of(in_at + i, 16), k)
                        mine = acc[n, here, :] if halves else send[n, pl.ds(i, k), :].astype(f32)
                        acc[n, here, :] = mine + recv[n, pl.ds(i, k), :].astype(f32)
                    loop_rows(size, one)

        stages.append((pack, [w[-1] for w in work], add))
    base, total = {}, 0
    for st in streams:
        base[st] = total
        total += sizes[st][-1]

    def packz():
        for i, n in enumerate(links.peer):
            for st in streams:
                def one(r, k):
                    zsend[i, pl.ds(base[st] + r, k), :] = acc[n, pl.ds(pl.multiple_of(place[st] + r, 16), k), :].astype(zsend.dtype)
                loop_rows(sizes[st][-1], one)

    def addz():
        for st in streams:
            def one(r, k):
                value = acc[links.n, pl.ds(pl.multiple_of(place[st] + r, 16), k), :]
                for i in range(narrow_n - 1):
                    value = value + zrecv[i, pl.ds(base[st] + r, k), :].astype(f32)
                mine_out[pl.ds(base[st] + r, k), :] = value.astype(bf16)
            loop_rows(sizes[st][-1], one)

    stages.append((packz, [links.copy(zsend.at[i], zrecv.at[i], links.over(n)) for i, n in enumerate(links.peer)], addz))
    return stages


def attn_backward(wide_n, narrow_n, comm, tok, qkv_s, prob_in, gm_s, grad_stream_in, attn_w, vec, hot, hmask, hmask2,
                  dmlp, dhid, dvec2, stats,
                  input_grad, dwq, misc, mine_out,
                  wq, pj, gp_s, low_s, turn_s, dext, dvec, dtable, flat, send0, recv0, acc, zsend, zrecv, *rest):
    step = pl.program_id(0)
    steps = pl.num_programs(0)
    static_steps = comm[1]
    width = tok.shape[1]
    groups = width // 128
    scale = 32 ** (-0.5)
    share = dmlp.shape[1] // 2

    if comm[0]:
        links = Links(wide_n, narrow_n, *rest[-2:])

        @pl.when(step == 0)
        def _():
            links.barrier()

        stages = scatter_stages(links, wide_n, narrow_n, share, dmlp, mine_out, send0, recv0, acc, zsend, zrecv, rest[:-2])
        for k, (pack, copies, add) in enumerate(stages):
            @pl.when(step == min(k, static_steps - 1))
            def _():
                if k:
                    for c in stages[k - 1][1]:
                        c.wait()
                    stages[k - 1][2]()
                pack()
                for c in copies:
                    c.start()

    @pl.when(step == 0)
    def _():
        wq[...] = attn_w[:, : 3 * width].astype(bf16)
        for ref in (dwq, dext, dvec, dtable):
            ref[...] = jnp.zeros_like(ref)

    def first(b, carry):
        for k in range(BATCH):
            i = b * BATCH + k
            for g in range(groups):
                do_bd = four(gm_s[i, :, 128 * g : 128 * g + 128], hmask[...])
                gp_s[i, g] = nt(qkv_s[i, :KR, 2 * width + 128 * g : 2 * width + 128 * g + 128], do_bd)
        return carry

    def second(b, carry):
        for g in range(groups):
            total = dtable[g]
            for k in range(BATCH):
                i = b * BATCH + k
                gp = gp_s[i, g]
                prob = prob_in[i, g]
                ds = prob * (gp - jnp.sum(gp * prob, 0, keepdims=True))
                total = total + ds
                raw = padded(ds * scale).astype(bf16)
                low_s[i, g] = raw
                turn_s[i, g] = turn(raw)
            dtable[g] = total
        return carry

    lax.fori_loop(0, CW // BATCH, first, 0)
    lax.fori_loop(0, CW // BATCH, second, 0)
    for i in range(CW):
        rows = slice(WTOK * i, WTOK * i + SLOT)
        for g in range(groups):
            q_bd = four(qkv_s[i, :, 128 * g : 128 * g + 128], hmask[...])
            k_bd = four(qkv_s[i, :, width + 128 * g : width + 128 * g + 128], hmask2[...])
            do_bd = four(gm_s[i, :, 128 * g : 128 * g + 128], hmask[...])
            pj[rows, 128 * g : 128 * g + 128] = nn(turn_s[i, g], k_bd)
            pj[rows, width + 128 * g : width + 128 * g + 128] = nn(low_s[i, g], q_bd)
            pj[rows, 2 * width + 128 * g : 2 * width + 128 * g + 128] = nn(padded(prob_in[i, g]).astype(bf16), do_bd)
    dproj = pj[:CR, :].astype(bf16)
    x = tok[...].astype(f32)
    xhat, inverse = norm_stats(x)
    low = (xhat * vec[0:1] + vec[1:2]).astype(bf16)
    low_t = jnp.concatenate([low.T, jnp.ones((16, CR), bf16)], 0)
    for j in range(3):
        outer = nn(low_t, dproj[:, width * j : width * j + width])
        dwq[j] += outer[:width]
        dext[j] += outer[width : width + 8]
    grad_normed = nt(dproj, wq[...])
    dvec[0] += fold_rows(grad_normed * xhat)
    dvec[1] += fold_rows(grad_normed)
    input_grad[...] = grad_stream_in[...] + norm_grad(grad_normed, xhat, inverse, vec[0:1])

    @pl.when(step == steps - 1)
    def _():
        rows = [dvec[0], dvec[1], None, None, dvec2[3], dvec2[0], dvec2[1], dvec2[2]]
        for i, part in enumerate(rows):
            if part is not None:
                misc[i : i + 1, :] = jnp.sum(part, 0, keepdims=True)
        misc[2:3, :] = dext[0, 0:1, :]
        misc[3:4, :] = dext[2, 0:1, :]
        for i in range(dhid.shape[1] // width):
            misc[8 + i : 9 + i, :] = dhid[0:1, width * i : width * i + width]
        lane = lax.broadcasted_iota(jnp.int32, (1, width), 1)
        line = jnp.zeros((1, width), f32)
        for i, part in enumerate((stats[0], stats[1], dvec2[4])):
            line = jnp.where(lane == i, jnp.sum(part), line)
        misc[12:13, :] = jnp.where(lane == 3, jnp.sum(stats[2]) / 128.0, line)
        misc[13:16, :] = jnp.zeros((3, width), f32)
        flat[...] = jnp.zeros_like(flat)
        for g in range(groups):
            for k in range(WTOK):
                line = dtable[g, k : k + 1, :]
                for h in range(HG):
                    flat[HG * g + h : HG * g + h + 1, SLOT * k : SLOT * k + SLOT] = line[:, SLOT * h : SLOT * h + SLOT]
        rest_f = flat[...]
        total = jnp.zeros((16, 256), f32)
        for _ in range(3):
            part = rest_f.astype(bf16)
            total += nn(part, hot[...])
            rest_f = rest_f - part.astype(f32)
        misc[16:32, :] = jnp.zeros((16, width), f32)
        misc[16:32, :256] = total
        if comm[0]:
            for c in stages[-1][1]:
                c.wait()
            stages[-1][2]()


def sds(shape, dt):
    return jax.ShapeDtypeStruct(shape, dt)


def whole(a):
    nd = len(a.shape)
    return pl.BlockSpec(a.shape, lambda *_: (0,) * nd, pipeline_mode=pl.Buffered(1))


def whole_out(a):
    nd = len(a.shape)
    return pl.BlockSpec(a.shape, lambda *_: (0,) * nd)


def by_step(a, steps):
    nd = len(a.shape)
    return pl.BlockSpec((a.shape[0] // steps,) + tuple(a.shape[1:]), lambda c: (c,) + (0,) * (nd - 1))


def run(body, steps, scalars, stepped, wholes, out_stepped, out_wholes, scratch, flops, collective_id=None):
    smem = pl.BlockSpec(memory_space=pltpu.SMEM)
    params = dict(vmem_limit_bytes=62 * 1024 * 1024)
    if collective_id is not None:
        params.update(collective_id=collective_id, has_side_effects=True)
    return pl.pallas_call(
        body, grid=(steps,),
        in_specs=[smem] * len(scalars) + [by_step(a, steps) for a in stepped] + wholes[1],
        out_specs=[by_step(a, steps) for a in out_stepped] + [whole_out(a) for a in out_wholes],
        out_shape=list(out_stepped) + list(out_wholes), scratch_shapes=scratch,
        compiler_params=pltpu.CompilerParams(**params),
        cost_estimate=pl.CostEstimate(flops=flops, bytes_accessed=20000000, transcendentals=0),
    )(*scalars, *stepped, *wholes[0])


def wholes_of(*arrays):
    return (arrays, [whole(a) for a in arrays])


def loop_rows(total, body):
    size = next(n for n in (96, 64, 48, 32, 16) if total % n == 0)
    lax.fori_loop(0, total // size, lambda i, c: (body(pl.multiple_of(i * size, size), size), c)[1], 0)


def reduce_all(wide_n, narrow_n, share, mine_ref, q_ref, o_ref, s_ref, gm_out, gt_out, s_out,
               send0, recv0, acct, zsend, zrecv, gm, gt, sbuf, srecv, szrecv, *rest):
    bufs = rest[:-2]
    links = Links(wide_n, narrow_n, *rest[-2:])
    bit, me_n, peer, n_bits = links.bit, links.n, links.peer, links.bits
    plan, m_streams, m_sizes = scatter_sizes(wide_n, share)
    links.barrier()
    ht = acct.shape[1]
    steps = n_bits - 1

    def attn_rows(n, start, size):
        flat = n * share
        if flat < q_ref.shape[0]:
            return q_ref[pl.ds(flat + start, size), :]
        return o_ref[pl.ds(flat - q_ref.shape[0] + start, size), :]

    m_trail = []
    m_place = {}
    for st, (start, _) in m_streams.items():
        here = start
        for s in range(steps):
            b = plan[st][s]
            size = m_sizes[st][s + 1]
            halves = size < m_sizes[st][s]
            here = here + bit[b] * size if halves else here
            m_trail.append((st, s, b, here, size, halves))
        m_place[st] = here
    base = 0
    for st in m_streams:
        size = m_sizes[st][-1]
        gm[pl.ds(pl.multiple_of(bit[0] * share + m_place[st], 16), size), :] = mine_ref[base : base + size, :]
        base += size
    m_back = []
    for s in reversed(range(steps)):
        stage = []
        for st, s2, b, at, size, halves in m_trail:
            if s2 == s and halves:
                part = gm.at[pl.ds(pl.multiple_of(bit[0] * share + at, 16), size), :]
                stage.append(links.copy(part, part, links.along(b)))
        m_back.append(stage)
    part = gm.at[pl.ds(pl.multiple_of(bit[0] * share, 16), share), :]
    m_back.append([links.copy(part, part, links.along(0))])
    m_back.append([])

    def back(k):
        if 0 < k <= len(m_back) - 1:
            for c in m_back[k - 1]:
                c.wait()
        if k < len(m_back):
            for c in m_back[k]:
                c.start()

    away_t, keep_t = (1 - bit[0]) * ht, bit[0] * ht
    sbuf[0] = s_ref[...]
    copies = [links.copy(sbuf.at[0], srecv.at[0], links.along(0))]
    copies[0].start()
    for n in range(narrow_n):
        def pack_t(i, size):
            send0[n, pl.ds(i, size), :] = attn_rows(n, pl.multiple_of(away_t + i, 16), size)
        loop_rows(ht, pack_t)
        c = links.copy(send0.at[n], recv0.at[n], links.along(0))
        c.start()
        copies.append(c)
    back(0)
    copies[0].wait()
    sbuf[1] = sbuf[0] + srecv[0]
    for n in range(narrow_n):
        copies[n + 1].wait()
        def add_t(i, size):
            acct[n, pl.ds(i, size), :] = attn_rows(n, pl.multiple_of(keep_t + i, 16), size) + recv0[n, pl.ds(i, size), :]
        loop_rows(ht, add_t)

    streams, sizes = t_streams(wide_n, ht)
    place = {st: streams[st][0] for st in streams}
    trail = []
    for s in range(steps):
        work = []
        small = links.copy(sbuf.at[1 + s], srecv.at[1 + s], links.along(plan["A"][s]))
        small.start()
        for k, st in enumerate(streams):
            b = plan[st][s]
            size = sizes[st][s + 1]
            halves = size < sizes[st][s]
            send, recv = bufs[2 * (2 * s + k)], bufs[2 * (2 * s + k) + 1]
            here = place[st]
            out_at, in_at = (here + (1 - bit[b]) * size, here + bit[b] * size) if halves else (here, here)
            for n in range(narrow_n):
                def pack(i, k2):
                    send[n, pl.ds(i, k2), :] = acct[n, pl.ds(pl.multiple_of(out_at + i, 16), k2), :].astype(send.dtype)
                loop_rows(size, pack)
            c = links.copy(send, recv, links.along(b))
            c.start()
            work.append((send, recv, in_at, size, halves, c))
            trail.append((st, s, b, in_at, size, halves))
            place[st] = in_at
        back(1 + s)
        small.wait()
        sbuf[2 + s] = sbuf[1 + s] + srecv[1 + s]
        for send, recv, in_at, size, halves, c in work:
            c.wait()
            for n in range(narrow_n):
                def add(i, k2):
                    here = pl.ds(pl.multiple_of(in_at + i, 16), k2)
                    mine = acct[n, here, :] if halves else send[n, pl.ds(i, k2), :].astype(f32)
                    acct[n, here, :] = mine + recv[n, pl.ds(i, k2), :].astype(f32)
                loop_rows(size, add)

    z_base, total = {}, 0
    for st in streams:
        z_base[st] = total
        total += sizes[st][-1]
    copies = []
    for i, n in enumerate(peer):
        c = links.copy(sbuf.at[n_bits], szrecv.at[i], links.over(n))
        c.start()
        copies.append(c)
    for i, n in enumerate(peer):
        for st in streams:
            def pack(r, k):
                zsend[i, pl.ds(z_base[st] + r, k), :] = acct[n, pl.ds(pl.multiple_of(place[st] + r, 16), k), :].astype(bf16)
            loop_rows(sizes[st][-1], pack)
        c = links.copy(zsend.at[i], zrecv.at[i], links.over(n))
        c.start()
        copies.append(c)
    for k in range(1 + steps, len(m_back)):
        back(k)
    for c in copies:
        c.wait()
    for st in streams:
        top = keep_t + place[st]
        def add(r, k):
            value = acct[me_n, pl.ds(pl.multiple_of(place[st] + r, 16), k), :]
            for i in range(narrow_n - 1):
                value = value + zrecv[i, pl.ds(z_base[st] + r, k), :].astype(f32)
            gt[me_n, pl.ds(pl.multiple_of(top + r, 16), k), :] = value.astype(bf16)
        loop_rows(sizes[st][-1], add)

    pending = []
    for st in streams:
        where = pl.ds(pl.multiple_of(keep_t + place[st], 16), sizes[st][-1])
        for n in peer:
            part = gt.at[me_n, where, :]
            c = links.copy(part, part, links.over(n))
            c.start()
            pending.append(c)
    zero = sbuf[n_bits]
    total_s = jnp.zeros_like(zero)
    for n in range(narrow_n):
        behind = lax.rem(me_n + narrow_n - n, narrow_n)
        value = zero
        for i in range(1, narrow_n):
            value = jnp.where(behind == i, szrecv[i - 1], value)
        total_s = total_s + value
    s_out[...] = total_s
    gm_out[...] = gm[...]
    for s in reversed(range(steps)):
        for c in pending:
            c.wait()
        pending = []
        for st, s2, b, at, size, halves in trail:
            if s2 == s and halves:
                part = gt.at[:, pl.ds(pl.multiple_of(keep_t + at, 16), size), :]
                c = links.copy(part, part, links.along(b))
                c.start()
                pending.append(c)
    for c in pending:
        c.wait()
    part = gt.at[:, pl.ds(pl.multiple_of(keep_t, 16), ht), :]
    c = links.copy(part, part, links.along(0))
    c.start()
    c.wait()
    gt_out[...] = gt[...]


def t_streams(wide_n, ht):
    rest = range(1, wide_n.bit_length() - 1)
    cut = ht * 2 // 3
    streams = {"A": (0, cut), "B": (cut, ht - cut)}
    sizes = {}
    for st, (_, size) in streams.items():
        sizes[st] = [size]
        for _ in rest:
            sizes[st].append(sizes[st][-1] // 2 if sizes[st][-1] % 32 == 0 else sizes[st][-1])
    return streams, sizes


def reduce_call(wide_n, narrow_n, share, mine, dq, do, misc):
    width = mine.shape[1]
    ht = share // 2
    n_bits = wide_n.bit_length() - 1
    streams, sizes = t_streams(wide_n, ht)
    last = sum(sizes[st][-1] for st in streams)
    scratch = [
        pltpu.VMEM((narrow_n, ht, width), f32), pltpu.VMEM((narrow_n, ht, width), f32), pltpu.VMEM((narrow_n, ht, width), f32),
        pltpu.VMEM((narrow_n - 1, last, width), bf16), pltpu.VMEM((narrow_n - 1, last, width), bf16),
        pltpu.VMEM((2 * share, width), bf16), pltpu.VMEM((narrow_n, share, width), bf16),
        pltpu.VMEM((n_bits + 1,) + misc.shape, f32), pltpu.VMEM((n_bits,) + misc.shape, f32),
        pltpu.VMEM((narrow_n - 1,) + misc.shape, f32)]
    for s in range(n_bits - 1):
        for st in streams:
            scratch += [pltpu.VMEM((narrow_n, sizes[st][s + 1], width), bf16)] * 2
    copies = 2 + narrow_n + 7 * n_bits + 4 * narrow_n
    scratch += [pltpu.SemaphoreType.DMA((copies,)), pltpu.SemaphoreType.DMA((copies,))]
    vmem = pl.BlockSpec(memory_space=pltpu.VMEM)
    return pl.pallas_call(
        functools.partial(reduce_all, wide_n, narrow_n, share),
        out_shape=[sds((2 * share, width), bf16), sds((narrow_n, share, width), bf16), sds(misc.shape, f32)],
        in_specs=[vmem] * 4, out_specs=[vmem] * 3, scratch_shapes=scratch,
        compiler_params=pltpu.CompilerParams(collective_id=0, has_side_effects=True, vmem_limit_bytes=60 * 1024 * 1024),
    )(mine, dq, do, misc)


def adam_kernel(narrow_ref, gt, gm, misc, aw, af, as_, mw, mf, ms, tw, tf, ts, vw, vf, vs, bw, bf, bs,
                rms, an, al, afn, asn, mn, ml, mfn, msn, tn_, tfn, tsn, vn, vfn, vsn, bn, bfn, bsn):
    def put(new, w, g, m, v, rate, decay, low=None):
        out = adam_step(w, g, m, v, rate, decay)
        for ref, value in zip(new, out):
            ref[...] = value.reshape(ref.shape)
        if low is not None:
            low[...] = out[0].astype(bf16).reshape(low.shape)

    put((an, afn, asn), aw[...], gt[0].astype(f32), af[...], as_[...], 0.02, 0.05, al)
    put((mn, mfn, msn), mw[0], gm[0].astype(f32), mf[0], ms[0], 0.02, 0.05, ml)

    @pl.when(pl.program_id(0) == 0)
    def _():
        put((vn, vfn, vsn), vw[...], misc[0:8, :], vf[...], vs[...], 0.3, 0.0)
        stats = misc[12:13, :]
        for i in range(3):
            ratio = jnp.sqrt(stats[:, i : i + 1] / (stats[:, 3:4] * misc.shape[1]))
            rms[i] = ratio[0, 0]
        n = narrow_ref[0]
        share = bw.shape[1]
        grad = jnp.zeros((1, share), f32)
        per = misc.shape[1] // share
        for i in range(4):
            for k in range(per):
                grad = jnp.where(n == per * i + k, misc[8 + i : 9 + i, share * k : share * k + share], grad)
        put((bn, bfn, bsn), bw[...], grad, bf[...], bs[...], 0.1, 0.0)
        turned = jnp.concatenate([misc[16:32, :256], jnp.zeros((112, 256), f32)], 0).T
        count, heads = tw.shape
        put((tn_, tfn, tsn), tw[...], turned[:count, :heads], tf[...], ts[...], 0.3, 0.0)


def adam_call(narrow, gt, gm, misc, attn, mlp, table, vec, bias):
    width = gm.shape[1]
    share = mlp[0].shape[1]
    gt = gt.reshape(4, width, width)
    quarter = share // 2
    gm = gm.reshape(4, quarter, width)
    mlp = [a.reshape(4, quarter, width) for a in mlp]
    bias = [a.reshape(1, -1) for a in bias]
    col = pl.BlockSpec((width, width), lambda j, *_: (0, j))
    lead = lambda r: pl.BlockSpec((1, r, width), lambda j, *_: (j, 0, 0))
    smalls = list(table) + list(vec) + list(bias)
    args = [gt, gm, misc] + list(attn) + mlp + smalls
    in_specs = [lead(width), lead(quarter), whole(misc)] + [col] * 3 + [lead(quarter)] * 3 + [whole(a) for a in smalls]
    three = lambda a: [sds(a.shape, f32)] * 3
    outs = [sds((3,), f32), sds(attn[0].shape, f32), sds(attn[0].shape, bf16)] + [sds(attn[0].shape, f32)] * 2
    outs += [sds(mlp[0].shape, f32), sds(mlp[0].shape, bf16)] + [sds(mlp[0].shape, f32)] * 2
    outs += three(table[0]) + three(vec[0]) + three(bias[0])
    out_specs = [pl.BlockSpec(memory_space=pltpu.SMEM)] + [col] * 4 + [lead(quarter)] * 4
    out_specs += [whole_out(a) for a in smalls]
    r = pl.pallas_call(
        adam_kernel,
        grid_spec=pltpu.PrefetchScalarGridSpec(num_scalar_prefetch=1, grid=(4,), in_specs=in_specs, out_specs=out_specs),
        out_shape=outs,
        compiler_params=pltpu.CompilerParams(vmem_limit_bytes=60 * 1024 * 1024),
    )(narrow, *args)
    full = (2, share, width)
    return [r[0], *r[1:5], *r[9:12], *r[12:15], *[a.reshape(full) for a in r[5:9]], *[a.reshape(-1) for a in r[15:18]]]


def bias_layout(rel_table):
    pos = np.arange(WTOK)
    row, col = pos // WIN, pos % WIN
    off = (row[:, None] - row[None, :] + WIN - 1) * (2 * WIN - 1) + col[:, None] - col[None, :] + WIN - 1
    full = np.full((KR, SLOT), -1, np.int32)
    full[:WTOK, :WTOK] = off.T
    return full


def block(tokens, grid_sizes, cotangent, attn_weight, rel_table, vectors, mlp_weight, mlp_bias, narrow, wide_n, narrow_n, linked=True):
    rows, width = tokens.shape
    wins = rows // WTOK
    steps = wins // CW
    heads = rel_table.shape[1]
    groups = heads // HG
    share = mlp_weight.shape[1]
    hidden = share * narrow_n
    n_bits = wide_n.bit_length() - 1
    comm = (linked, steps)
    unit = rows * width * width
    hot = np.zeros((KR * SLOT, 256), np.float32)
    lay = bias_layout(rel_table).reshape(-1)
    hot[np.arange(KR * SLOT)[lay >= 0], lay[lay >= 0]] = 1.0
    hot = jnp.asarray(hot, bf16)
    mask = head_mask(width // heads)
    mask2 = mask.reshape(HG, SLOT, -1)[np.array([0, 2, 1, 3])].reshape(mask.shape)
    mask, mask2 = jnp.asarray(mask, bf16), jnp.asarray(mask2, bf16)
    rinfo, kinfo = jnp.asarray(row_info()), jnp.asarray(key_info())
    scal = (narrow, grid_sizes)
    pad = CR + 16
    copies = 3 * (narrow_n - 1) + 3 * 2 * (narrow_n - 1) + 4
    sem = [pltpu.SemaphoreType.DMA((copies,)), pltpu.SemaphoreType.DMA((copies,))] if linked else []
    sides = pltpu.VMEM((CR, 128), f32)
    table_s = pltpu.VMEM((groups, KR, HG * SLOT), f32)
    flat = pltpu.VMEM((16, KR * SLOT), f32)
    turned = pltpu.VMEM((CW, groups, SLOT, HG * SLOT), bf16)
    qkv, prob, mixed, stream, stats, gw, tails = run(
        functools.partial(attn_forward, wide_n, narrow_n, comm), steps, scal, (tokens,),
        wholes_of(attn_weight, mlp_weight, mlp_bias.reshape(1, -1), vectors, rel_table, hot, rinfo, kinfo, mask, mask2),
        [sds((wins, SLOT, 3 * width), bf16), sds((wins, groups, KR, HG * SLOT), f32), sds((rows, width), bf16), sds((rows, width), f32)],
        [sds((3, 8, width), f32), sds((narrow_n, 2 * share, width), bf16), sds((narrow_n, 8, width), f32)],
        [pltpu.VMEM((width, 4 * width), bf16), pltpu.VMEM((pad, 3 * width), f32), pltpu.VMEM((pad, width), f32), turned,
         table_s, pltpu.VMEM((256, 128), f32), flat, sides,
         pltpu.VMEM((2 * share, width), bf16), pltpu.VMEM((8, width), f32),
         pltpu.VMEM((narrow_n, 2 * share, width), bf16), pltpu.VMEM((narrow_n, 8, width), f32)] + sem,
        12 * unit, 1 if linked else None)
    out_proj = pl.BlockSpec((width, width), lambda *_: (0, 3), pipeline_mode=pl.Buffered(1))
    fixed = (attn_weight, gw, tails, vectors, rinfo)
    outputs, grad_stream, gm, dmlp, dwo, dhid, dvec2 = run(
        functools.partial(feed_forward, TILE), steps, scal, (cotangent, mixed, stream),
        (fixed, [out_proj] + [whole(a) for a in fixed[1:]]),
        [sds((rows, width), bf16), sds((rows, width), f32), sds((wins, SLOT, width), bf16)],
        [sds((narrow_n, 2 * share, width), f32), sds((width, width), f32), sds((8, hidden), f32), sds((5, 8, width), f32)],
        [pltpu.VMEM((width, width), bf16), pltpu.VMEM((hidden, width), bf16), pltpu.VMEM((hidden, width), bf16),
         pltpu.VMEM((1, hidden), f32), pltpu.VMEM((width, hidden), f32), pltpu.VMEM((width, hidden), f32),
         pltpu.VMEM((pad, width), f32), sides],
        52 * unit)
    _, streams, sizes = scatter_sizes(wide_n, share)
    last = sum(sizes[st][-1] for st in streams)
    bufs = []
    for s in range(n_bits - 1):
        for st in streams:
            bufs += [pltpu.VMEM((narrow_n, sizes[st][s + 1], width), bf16)] * 2
    copies = 1 + 2 * n_bits + narrow_n
    sem = [pltpu.SemaphoreType.DMA((copies,)), pltpu.SemaphoreType.DMA((copies,))] if linked else []
    input_grad, dwq, misc, mine = run(
        functools.partial(attn_backward, wide_n, narrow_n, comm), steps, (), (tokens, qkv, prob, gm, grad_stream),
        wholes_of(attn_weight, vectors, hot, mask, mask2, dmlp, dhid, dvec2, stats),
        [sds((rows, width), f32)],
        [sds((3, width, width), f32), sds((32, width), f32), sds((last, width), bf16)],
        [pltpu.VMEM((width, 3 * width), bf16), pltpu.VMEM((pad, 3 * width), f32),
         pltpu.VMEM((CW, groups, KR, HG * SLOT), f32), turned, turned, pltpu.VMEM((3, 8, width), f32),
         pltpu.VMEM((2, 8, width), f32), table_s, flat,
         pltpu.VMEM((narrow_n, share, width), bf16), pltpu.VMEM((narrow_n, share, width), bf16),
         pltpu.VMEM((narrow_n, share, width), f32), pltpu.VMEM((narrow_n - 1, last, width), bf16),
         pltpu.VMEM((narrow_n - 1, last, width), bf16)] + bufs + sem,
        20 * unit, 2 if linked else None)
    return outputs, input_grad, dmlp, dwq, dwo, misc, mine


TILE = 768


def adam_step(weight, gradient, first_old, second_old, rate_value, decay_value):
    first_new = beta_one * first_old + (1.0 - beta_one) * gradient
    second_new = beta_two * second_old + (1.0 - beta_two) * gradient * gradient
    fix_one = 1.0 - beta_one**STEP
    fix_two = 1.0 - beta_two**STEP
    update = rate_value * (first_new / fix_one) / (jnp.sqrt(second_new / fix_two) + adam_eps)
    return (weight - update - rate_value * decay_value * weight, first_new, second_new)


def shards(wide_n, narrow_n, tokens, grid_sizes, cotangent, attn_weight, attn_first, attn_second, rel_table, table_first,
           table_second, vectors, vector_first, vector_second, mlp_weight, mlp_first, mlp_second, mlp_bias, bias_first,
           bias_second):
    width = tokens.shape[1]
    narrow = lax.axis_index("narrow").reshape(1).astype(jnp.int32)
    outputs, input_grad, _, dwq, dwo, misc, mine = block(
        tokens, grid_sizes, cotangent, attn_weight, rel_table, vectors, mlp_weight, mlp_bias, narrow, wide_n, narrow_n)
    gm, gt, misc = reduce_call(wide_n, narrow_n, mlp_weight.shape[1], mine, dwq.reshape(3 * width, width), dwo, misc)
    new = adam_call(narrow, gt, gm, misc, (attn_weight, attn_first, attn_second), (mlp_weight, mlp_first, mlp_second),
                    (rel_table, table_first, table_second), (vectors, vector_first, vector_second),
                    (mlp_bias, bias_first, bias_second))
    return (outputs, input_grad, *new)


def solution(mesh):
    rows = P(("wide", "narrow"), None)
    split = P(None, "narrow", None)
    return jax.shard_map(
        functools.partial(shards, mesh.shape["wide"], mesh.shape["narrow"]), mesh=mesh,
        in_specs=(rows, P("wide"), rows) + (P(),) * 9 + (split,) * 3 + (P("narrow"),) * 3,
        out_specs=(rows, rows) + (P(),) * 11 + (split,) * 4 + (P("narrow"),) * 3,
        check_vma=False)
```

time: 308 us -> 205 us (0.67)
  Pallas kernels: 249 us -> 185 us
  blocking collectives: 14.4 us -> 0 us
  between operations: 14.2 us -> 0.75 us
  waiting for transfers between devices: 5.74 us -> 0 us
  other arithmetic: 7 us -> 3.75 us
    pallas_call x1, Pallas kernels: 141 us -> 43.6 us  [reduce_call(): pl.pallas_call(functools.partial(reduce_all, wide_n, narrow_n, share), ou...]
    pallas_call x3, Pallas kernels: 96.4 us -> 130 us  [run(): pl.pallas_call(body, grid=(steps,), in_specs=[smem] * len(scalars) + [by_...]
    all_gather x1 -> x0, blocking collectives: 14.4 us -> none  [shards(): hidden_bias = lax.all_gather(mlp_bias, 'narrow', axis=0, tiled=True)]
    all_gather x1 -> x0, waiting for transfers between devices: 5.72 us -> none  [shards(): lax.all_gather(mlp_weight.astype(bf16), 'narrow', axis=1, tiled=True)]
    unnamed x27 -> x15, local copies, waits for them, and re-layouts: 7.57 us -> 12.6 us
    squeeze x1 -> x0, local copies, waits for them, and re-layouts: 3.26 us -> none  [shards(): hidden_low[1]]
  transfers between devices with their start and end apart: 1 -> 0, of which waited for: 1 -> 0; matrix products, arithmetic and copies ran while one was open for 3% -> 0% of each run, Pallas kernels for 8% -> 0%
where the time goes in v3:
time: 205 us
  Pallas kernels  185 us (90%)
  local copies, waits for them, and re-layouts  15 us (7%)
  other arithmetic  3.75 us (2%)
    pallas_call x3, Pallas kernels, run(): pl.pallas_call(body, grid=(steps,), in_specs=[smem] * len(scalars) + [by_...  130 us
    pallas_call x1, Pallas kernels, reduce_call(): pl.pallas_call(functools.partial(reduce_all, wide_n, narrow_n, share), ou...  43.6 us
    unnamed x15, local copies, waits for them, and re-layouts  12.6 us
    pallas_call x1, Pallas kernels, adam_call(): pl.pallas_call(adam_kernel, grid_spec=pltpu.PrefetchScalarGridSpec(num_sc...  11.2 us

profile of v3, /device:TPU:0, one launch (start us, length us, event | category | flops | bytes accessed | tf_op | source)
XLA Modules:
  0.0 204.6 jit_solution(11231186537699048497)
XLA Ops:
  0.7 1.5 copy.43.table.tw
  2.1 1.2 reshape.90.mlp_b.bw
  3.4 40.1 %shard_map.374 = (bf16[64,64,1152]{2,1,0:T(8,128)(2,1)}, f32[64,3,56,256]{3,2,1,0:T(8,128)}, bf16[3136,384]{1,0:T(8,128)(2,1)}, f32[3136,384]{1,0:T(8,128)}, f32...) custom-call(s32[1]{0:T(128)} %bitcast.narrow_ref, s32[16]{0:T(128)} %sides.3, ...), custom_call_target="tpu_custom_call" | custom-call | flops 5549064192 | bytes 20000000 | tf_op jit(solution)/shard_map/pallas_call | solution.py:636
  43.4 48.7 %shard_map.375 = (bf16[3136,384]{1,0:T(8,128)(2,1)}, f32[3136,384]{1,0:T(8,128)}, bf16[64,64,384]{2,1,0:T(8,128)(2,1)}, f32[4,768,384]{2,1,0:T(8,128)}, f32[384,...) custom-call(s32[1]{0:T(128)} %bitcast.narrow_ref, s32[16]{0:T(128)} %sides.3, bf16[3136,384]{1,0:T(8,128)(2,1)} %cot.1, ...), custom_call_target="tpu_custom_call" | custom-call | flops 24045944832 | bytes 20000000 | tf_op jit(solution)/shard_map/pallas_call | solution.py:636
  92.2 41.6 %shard_map.376 = (f32[3136,384]{1,0:T(8,128)}, f32[3,384,384]{2,1,0:T(8,128)}, f32[32,384]{1,0:T(8,128)}, bf16[96,384]{1,0:T(8,128)(2,1)}) custom-call(bf16[3136,384]{1,0:T(8,128)(2,1)} %tok.3, bf16[64,64,1152]{2,1,0:T(8,128)(2,1)} %get-tuple-element.64.qkv_s, f32[64,3,56,256]{3,2,1,0:T(8,128)} %get-tuple-element.65.prob_in, ...), custom_call_target="tpu_custom_call" | custom-call | flops 9248440320 | bytes 20000000 | tf_op jit(solution)/shard_map/pallas_call | solution.py:636
  133.8 0.0 copy-start
  133.8 0.0 copy-start.1
  133.8 0.0 copy-start.2
  133.8 0.0 copy-start.3
  133.8 43.6 %shard_map.377 = (bf16[768,384]{1,0:T(8,128)(2,1)}, bf16[4,384,384]{2,1,0:T(8,128)(2,1)}, f32[32,384]{1,0:T(8,128)}) custom-call(bf16[96,384]{1,0:T(8,128)(2,1)} %get-tuple-element.73.mine_ref, f32[1152,384]{1,0:T(8,128)} %bitcast.10, f32[384,384]{1,0:T(8,128)} %get-tuple-element.75.o_ref, f32[32,384]{1,0:T(8,128)} %get-tuple-element.76.s_ref), custom_call_target="tpu_custom_call" | custom-call | tf_op jit(solution)/shard_map/pallas_call | solution.py:859
  177.4 0.0 copy-done
  177.4 0.7 copy.45.tf
  178.2 0.0 copy-done.1
  178.2 0.7 copy.46.ts
  178.9 0.0 copy-done.2
  178.9 0.6 reshape.96.bf
  179.5 0.0 copy-done.3
  179.5 0.6 reshape.97.bs
  180.1 11.2 %shard_map.378 = (f32[3]{0:T(128)}, f32[384,1536]{1,0:T(8,128)}, bf16[384,1536]{1,0:T(8,128)(2,1)}, f32[384,1536]{1,0:T(8,128)}, f32[384,1536]{1,0:T(8,128)}, /*...) custom-call(s32[1]{0:T(128)} %bitcast.narrow_ref, ...), custom_call_target="tpu_custom_call" | custom-call | tf_op jit(solution)/shard_map/pallas_call | solution.py:918
  191.2 1.6 copy.47
  192.8 1.6 copy.48
  194.4 1.6 copy.49
  196.0 1.2 reduce
  197.2 1.3 reduce.1
  198.5 1.3 reduce.2
  199.7 4.9 %copy.51 = f32[3136,384]{1,0:T(8,128)} copy(f32[3136,384]{1,0:T(8,128)} %get-tuple-element.139) | data formatting | bytes 9633792
Async XLA Ops:
  133.8 43.6 %copy-start = (f32[169,12]{0,1:T(8,128)S(1)}, f32[169,12]{0,1:T(8,128)}, u32[]{:S(2)}) copy-start(f32[169,12]{0,1:T(8,128)} %param.30) | copy-start | bytes 24340
  133.8 44.4 %copy-start.1 = (f32[169,12]{0,1:T(8,128)S(1)}, f32[169,12]{0,1:T(8,128)}, u32[]{:S(2)}) copy-start(f32[169,12]{0,1:T(8,128)} %param.31) | copy-start | bytes 24340
  133.8 45.1 %copy-start.2 = (f32[384]{0:T(512)S(1)}, f32[384]{0:T(512)}, u32[]{:S(2)}) copy-start(f32[384]{0:T(512)} %param.39) | copy-start | bytes 4612
  133.8 45.7 %copy-start.3 = (f32[384]{0:T(512)S(1)}, f32[384]{0:T(512)}, u32[]{:S(2)}) copy-start(f32[384]{0:T(512)} %param.40) | copy-start | bytes 4612

commit v4 on v3

--- a/solution.py
+++ b/solution.py
@@ -112,13 +112,16 @@
         self.peer = [lax.rem(self.n + s, narrow_n) for s in range(1, narrow_n)]
         self.send_sem, self.recv_sem = send_sem, recv_sem
         self.used = 0
+        self.all = []
 
     def copy(self, src, dst, device):
         k = self.used
         self.used += 1
-        return pltpu.make_async_remote_copy(
+        c = pltpu.make_async_remote_copy(
             src_ref=src, dst_ref=dst, send_sem=self.send_sem.at[k], recv_sem=self.recv_sem.at[k],
             device_id=device, device_id_type=pl.DeviceIdType.MESH)
+        self.all.append(c)
+        return c
 
     def along(self, b):
         return (self.mate[b], self.n)
@@ -183,10 +186,10 @@
 
 
 def expand_table(table, hot, wide_t, flat, bias):
-    count, heads = table.shape
+    heads, count = table.shape
     wide_t[...] = jnp.zeros_like(wide_t)
-    wide_t[:count, :heads] = table[...] * LOG2E
-    rest = wide_t[...].T[:16, :]
+    wide_t[:heads, :count] = table[...] * LOG2E
+    rest = wide_t[...]
     total = jnp.zeros((16, hot.shape[0]), f32)
     for _ in range(3):
         part = rest.astype(bf16)
@@ -213,7 +216,7 @@
     return jnp.concatenate([t] * HG, 0) * mask
 
 
-BATCH = 8
+BATCH = 16
 
 
 def attn_forward(wide_n, narrow_n, comm, narrow_ref, sides, tok, attn_w, mlp_w, mlp_b, vec, table, hot, rinfo, kinfo, hmask, hmask2,
@@ -233,7 +236,7 @@
         for j in range(2):
             own[share * j : share * j + share, :] = mlp_w[j].astype(bf16)
         tail_own[...] = jnp.zeros_like(tail_own)
-        rest = mlp_b[...]
+        rest = mlp_b[...].reshape(1, share)
         for i in range(3):
             part = rest.astype(bf16).astype(f32)
             tail_own[i : i + 1, :share] = part
@@ -653,7 +656,7 @@
 
 
 def reduce_all(wide_n, narrow_n, share, mine_ref, q_ref, o_ref, s_ref, gm_out, gt_out, s_out,
-               send0, recv0, acct, zsend, zrecv, gm, gt, sbuf, srecv, szrecv, *rest):
+               recv0, acct, zsend, zrecv, gm, gt, sbuf, srecv, szrecv, *rest):
     bufs = rest[:-2]
     links = Links(wide_n, narrow_n, *rest[-2:])
     bit, me_n, peer, n_bits = links.bit, links.n, links.peer, links.bits
@@ -699,7 +702,7 @@
     def back(k):
         if 0 < k <= len(m_back) - 1:
             for c in m_back[k - 1]:
-                c.wait()
+                c.wait_recv()
         if k < len(m_back):
             for c in m_back[k]:
                 c.start()
@@ -709,17 +712,16 @@
     copies = [links.copy(sbuf.at[0], srecv.at[0], links.along(0))]
     copies[0].start()
     for n in range(narrow_n):
-        def pack_t(i, size):
-            send0[n, pl.ds(i, size), :] = attn_rows(n, pl.multiple_of(away_t + i, 16), size)
-        loop_rows(ht, pack_t)
-        c = links.copy(send0.at[n], recv0.at[n], links.along(0))
+        flat = n * share
+        src, off = (q_ref, flat) if flat < q_ref.shape[0] else (o_ref, flat - q_ref.shape[0])
+        c = links.copy(src.at[pl.ds(pl.multiple_of(off + away_t, 16), ht), :], recv0.at[n], links.along(0))
         c.start()
         copies.append(c)
     back(0)
-    copies[0].wait()
+    copies[0].wait_recv()
     sbuf[1] = sbuf[0] + srecv[0]
     for n in range(narrow_n):
-        copies[n + 1].wait()
+        copies[n + 1].wait_recv()
         def add_t(i, size):
             acct[n, pl.ds(i, size), :] = attn_rows(n, pl.multiple_of(keep_t + i, 16), size) + recv0[n, pl.ds(i, size), :]
         loop_rows(ht, add_t)
@@ -748,10 +750,10 @@
             trail.append((st, s, b, in_at, size, halves))
             place[st] = in_at
         back(1 + s)
-        small.wait()
+        small.wait_recv()
         sbuf[2 + s] = sbuf[1 + s] + srecv[1 + s]
         for send, recv, in_at, size, halves, c in work:
-            c.wait()
+            c.wait_recv()
             for n in range(narrow_n):
                 def add(i, k2):
                     here = pl.ds(pl.multiple_of(in_at + i, 16), k2)
@@ -779,7 +781,7 @@
     for k in range(1 + steps, len(m_back)):
         back(k)
     for c in copies:
-        c.wait()
+        c.wait_recv()
     for st in streams:
         top = keep_t + place[st]
         def add(r, k):
@@ -809,7 +811,7 @@
     gm_out[...] = gm[...]
     for s in reversed(range(steps)):
         for c in pending:
-            c.wait()
+            c.wait_recv()
         pending = []
         for st, s2, b, at, size, halves in trail:
             if s2 == s and halves:
@@ -818,12 +820,14 @@
                 c.start()
                 pending.append(c)
     for c in pending:
-        c.wait()
+        c.wait_recv()
     part = gt.at[:, pl.ds(pl.multiple_of(keep_t, 16), ht), :]
     c = links.copy(part, part, links.along(0))
     c.start()
-    c.wait()
+    c.wait_recv()
     gt_out[...] = gt[...]
+    for c in links.all:
+        c.wait_send()
 
 
 def t_streams(wide_n, ht):
@@ -845,7 +849,7 @@
     streams, sizes = t_streams(wide_n, ht)
     last = sum(sizes[st][-1] for st in streams)
     scratch = [
-        pltpu.VMEM((narrow_n, ht, width), f32), pltpu.VMEM((narrow_n, ht, width), f32), pltpu.VMEM((narrow_n, ht, width), f32),
+        pltpu.VMEM((narrow_n, ht, width), f32), pltpu.VMEM((narrow_n, ht, width), f32),
         pltpu.VMEM((narrow_n - 1, last, width), bf16), pltpu.VMEM((narrow_n - 1, last, width), bf16),
         pltpu.VMEM((2 * share, width), bf16), pltpu.VMEM((narrow_n, share, width), bf16),
         pltpu.VMEM((n_bits + 1,) + misc.shape, f32), pltpu.VMEM((n_bits,) + misc.shape, f32),
@@ -873,7 +877,7 @@
         if low is not None:
             low[...] = out[0].astype(bf16).reshape(low.shape)
 
-    put((an, afn, asn), aw[...], gt[0].astype(f32), af[...], as_[...], 0.02, 0.05, al)
+    put((an, afn, asn), aw[...], jnp.concatenate([gt[j].astype(f32) for j in range(4)], 1), af[...], as_[...], 0.02, 0.05, al)
     put((mn, mfn, msn), mw[0], gm[0].astype(f32), mf[0], ms[0], 0.02, 0.05, ml)
 
     @pl.when(pl.program_id(0) == 0)
@@ -884,45 +888,46 @@
             ratio = jnp.sqrt(stats[:, i : i + 1] / (stats[:, 3:4] * misc.shape[1]))
             rms[i] = ratio[0, 0]
         n = narrow_ref[0]
-        share = bw.shape[1]
+        share = bw.shape[0]
         grad = jnp.zeros((1, share), f32)
         per = misc.shape[1] // share
         for i in range(4):
             for k in range(per):
                 grad = jnp.where(n == per * i + k, misc[8 + i : 9 + i, share * k : share * k + share], grad)
-        put((bn, bfn, bsn), bw[...], grad, bf[...], bs[...], 0.1, 0.0)
-        turned = jnp.concatenate([misc[16:32, :256], jnp.zeros((112, 256), f32)], 0).T
-        count, heads = tw.shape
-        put((tn_, tfn, tsn), tw[...], turned[:count, :heads], tf[...], ts[...], 0.3, 0.0)
+        put((bn, bfn, bsn), bw[...], grad.reshape(share), bf[...], bs[...], 0.1, 0.0)
+        heads, count = tw.shape
+        put((tn_, tfn, tsn), tw[...], misc[16 : 16 + heads, :count], tf[...], ts[...], 0.3, 0.0)
 
 
 def adam_call(narrow, gt, gm, misc, attn, mlp, table, vec, bias):
     width = gm.shape[1]
     share = mlp[0].shape[1]
     gt = gt.reshape(4, width, width)
-    quarter = share // 2
-    gm = gm.reshape(4, quarter, width)
-    mlp = [a.reshape(4, quarter, width) for a in mlp]
-    bias = [a.reshape(1, -1) for a in bias]
-    col = pl.BlockSpec((width, width), lambda j, *_: (0, j))
-    lead = lambda r: pl.BlockSpec((1, r, width), lambda j, *_: (j, 0, 0))
+    cuts = 8
+    quarter = 2 * share // cuts
+    rows = width // cuts
+    gm = gm.reshape(cuts, quarter, width)
+    mlp = [a.reshape(cuts, quarter, width) for a in mlp]
+    line = pl.BlockSpec((rows, attn[0].shape[1]), lambda j, *_: (j, 0))
+    lead = pl.BlockSpec((1, quarter, width), lambda j, *_: (j, 0, 0))
+    split = pl.BlockSpec((4, rows, width), lambda j, *_: (0, j, 0))
     smalls = list(table) + list(vec) + list(bias)
     args = [gt, gm, misc] + list(attn) + mlp + smalls
-    in_specs = [lead(width), lead(quarter), whole(misc)] + [col] * 3 + [lead(quarter)] * 3 + [whole(a) for a in smalls]
+    in_specs = [split, lead, whole(misc)] + [line] * 3 + [lead] * 3 + [whole(a) for a in smalls]
     three = lambda a: [sds(a.shape, f32)] * 3
     outs = [sds((3,), f32), sds(attn[0].shape, f32), sds(attn[0].shape, bf16)] + [sds(attn[0].shape, f32)] * 2
     outs += [sds(mlp[0].shape, f32), sds(mlp[0].shape, bf16)] + [sds(mlp[0].shape, f32)] * 2
     outs += three(table[0]) + three(vec[0]) + three(bias[0])
-    out_specs = [pl.BlockSpec(memory_space=pltpu.SMEM)] + [col] * 4 + [lead(quarter)] * 4
+    out_specs = [pl.BlockSpec(memory_space=pltpu.SMEM)] + [line] * 4 + [lead] * 4
     out_specs += [whole_out(a) for a in smalls]
     r = pl.pallas_call(
         adam_kernel,
-        grid_spec=pltpu.PrefetchScalarGridSpec(num_scalar_prefetch=1, grid=(4,), in_specs=in_specs, out_specs=out_specs),
+        grid_spec=pltpu.PrefetchScalarGridSpec(num_scalar_prefetch=1, grid=(cuts,), in_specs=in_specs, out_specs=out_specs),
         out_shape=outs,
         compiler_params=pltpu.CompilerParams(vmem_limit_bytes=60 * 1024 * 1024),
     )(narrow, *args)
     full = (2, share, width)
-    return [r[0], *r[1:5], *r[9:12], *r[12:15], *[a.reshape(full) for a in r[5:9]], *[a.reshape(-1) for a in r[15:18]]]
+    return [r[0], *r[1:5], *[a.T for a in r[9:12]], *r[12:15], *[a.reshape(full) for a in r[5:9]], *r[15:18]]
 
 
 def bias_layout(rel_table):
@@ -938,7 +943,7 @@
     rows, width = tokens.shape
     wins = rows // WTOK
     steps = wins // CW
-    heads = rel_table.shape[1]
+    heads = rel_table.shape[0]
     groups = heads // HG
     share = mlp_weight.shape[1]
     hidden = share * narrow_n
@@ -963,11 +968,11 @@
     turned = pltpu.VMEM((CW, groups, SLOT, HG * SLOT), bf16)
     qkv, prob, mixed, stream, stats, gw, tails = run(
         functools.partial(attn_forward, wide_n, narrow_n, comm), steps, scal, (tokens,),
-        wholes_of(attn_weight, mlp_weight, mlp_bias.reshape(1, -1), vectors, rel_table, hot, rinfo, kinfo, mask, mask2),
+        wholes_of(attn_weight, mlp_weight, mlp_bias, vectors, rel_table, hot, rinfo, kinfo, mask, mask2),
         [sds((wins, SLOT, 3 * width), bf16), sds((wins, groups, KR, HG * SLOT), f32), sds((rows, width), bf16), sds((rows, width), f32)],
         [sds((3, 8, width), f32), sds((narrow_n, 2 * share, width), bf16), sds((narrow_n, 8, width), f32)],
         [pltpu.VMEM((width, 4 * width), bf16), pltpu.VMEM((pad, 3 * width), f32), pltpu.VMEM((pad, width), f32), turned,
-         table_s, pltpu.VMEM((256, 128), f32), flat, sides,
+         table_s, pltpu.VMEM((16, 256), f32), flat, sides,
          pltpu.VMEM((2 * share, width), bf16), pltpu.VMEM((8, width), f32),
          pltpu.VMEM((narrow_n, 2 * share, width), bf16), pltpu.VMEM((narrow_n, 8, width), f32)] + sem,
         12 * unit, 1 if linked else None)
@@ -1023,10 +1028,10 @@
     width = tokens.shape[1]
     narrow = lax.axis_index("narrow").reshape(1).astype(jnp.int32)
     outputs, input_grad, _, dwq, dwo, misc, mine = block(
-        tokens, grid_sizes, cotangent, attn_weight, rel_table, vectors, mlp_weight, mlp_bias, narrow, wide_n, narrow_n)
+        tokens, grid_sizes, cotangent, attn_weight, rel_table.T, vectors, mlp_weight, mlp_bias, narrow, wide_n, narrow_n)
     gm, gt, misc = reduce_call(wide_n, narrow_n, mlp_weight.shape[1], mine, dwq.reshape(3 * width, width), dwo, misc)
     new = adam_call(narrow, gt, gm, misc, (attn_weight, attn_first, attn_second), (mlp_weight, mlp_first, mlp_second),
-                    (rel_table, table_first, table_second), (vectors, vector_first, vector_second),
+                    (rel_table.T, table_first.T, table_second.T), (vectors, vector_first, vector_second),
                     (mlp_bias, bias_first, bias_second))
     return (outputs, input_grad, *new)
 

time: 205 us -> 188 us (0.917)
  local copies, waits for them, and re-layouts: 15 us -> 4.89 us
  other arithmetic: 3.75 us -> 0 us
  Pallas kernels: 185 us -> 182 us
    unnamed x15 -> x1, local copies, waits for them, and re-layouts: 12.6 us -> 4.89 us
    pallas_call x3, Pallas kernels: 130 us -> 124 us  [run(): pl.pallas_call(body, grid=(steps,), in_specs=[smem] * len(scalars) + [by_...]
    pallas_call x3 -> x0, other arithmetic: 3.75 us -> none  [adam_call(): pl.pallas_call(adam_kernel, grid_spec=pltpu.PrefetchScalarGridSpec(num_sc...]
    reshape x3 -> x0, local copies, waits for them, and re-layouts: 2.37 us -> none  [the longest x1 1.24 us: block(): mlp_bias.reshape(1, -1)]
where the time goes in v4:
time: 188 us
  Pallas kernels  182 us (97%)
  local copies, waits for them, and re-layouts  4.89 us (3%)
    pallas_call x3, Pallas kernels, run(): pl.pallas_call(body, grid=(steps,), in_specs=[smem] * len(scalars) + [by_...  124 us
    pallas_call x1, Pallas kernels, reduce_call(): pl.pallas_call(functools.partial(reduce_all, wide_n, narrow_n, share), ou...  45.3 us
    pallas_call x1, Pallas kernels, adam_call(): pl.pallas_call(adam_kernel, grid_spec=pltpu.PrefetchScalarGridSpec(num_sc...  12.7 us
    unnamed x1, local copies, waits for them, and re-layouts  4.89 us

profile of v4, /device:TPU:0, one launch (start us, length us, event | category | flops | bytes accessed | tf_op | source)
XLA Modules:
  0.0 187.7 jit_solution(4316734505857357700)
XLA Ops:
  0.7 36.3 %shard_map.374 = (bf16[64,64,1152]{2,1,0:T(8,128)(2,1)}, f32[64,3,56,256]{3,2,1,0:T(8,128)}, bf16[3136,384]{1,0:T(8,128)(2,1)}, f32[3136,384]{1,0:T(8,128)}, f32...) custom-call(s32[1]{0:T(128)} %bitcast.narrow_ref, s32[16]{0:T(128)} %sides.3, ...), custom_call_target="tpu_custom_call" | custom-call | flops 5549064192 | bytes 20000000 | tf_op jit(solution)/shard_map/pallas_call | solution.py:639
  37.0 48.7 %shard_map.375 = (bf16[3136,384]{1,0:T(8,128)(2,1)}, f32[3136,384]{1,0:T(8,128)}, bf16[64,64,384]{2,1,0:T(8,128)(2,1)}, f32[4,768,384]{2,1,0:T(8,128)}, f32[384,...) custom-call(s32[1]{0:T(128)} %bitcast.narrow_ref, s32[16]{0:T(128)} %sides.3, bf16[3136,384]{1,0:T(8,128)(2,1)} %cot.1, ...), custom_call_target="tpu_custom_call" | custom-call | flops 24045944832 | bytes 20000000 | tf_op jit(solution)/shard_map/pallas_call | solution.py:639
  85.7 39.1 %shard_map.376 = (f32[3136,384]{1,0:T(8,128)}, f32[3,384,384]{2,1,0:T(8,128)}, f32[32,384]{1,0:T(8,128)}, bf16[96,384]{1,0:T(8,128)(2,1)}) custom-call(bf16[3136,384]{1,0:T(8,128)(2,1)} %tok.3, bf16[64,64,1152]{2,1,0:T(8,128)(2,1)} %get-tuple-element.64.qkv_s, f32[64,3,56,256]{3,2,1,0:T(8,128)} %get-tuple-element.65.prob_in, ...), custom_call_target="tpu_custom_call" | custom-call | flops 9248440320 | bytes 20000000 | tf_op jit(solution)/shard_map/pallas_call | solution.py:639
  124.8 45.3 %shard_map.377 = (bf16[768,384]{1,0:T(8,128)(2,1)}, bf16[4,384,384]{2,1,0:T(8,128)(2,1)}, f32[32,384]{1,0:T(8,128)}) custom-call(bf16[96,384]{1,0:T(8,128)(2,1)} %get-tuple-element.73.mine_ref, f32[1152,384]{1,0:T(8,128)} %bitcast.16, f32[384,384]{1,0:T(8,128)} %get-tuple-element.75.o_ref, f32[32,384]{1,0:T(8,128)} %get-tuple-element.76.s_ref), custom_call_target="tpu_custom_call" | custom-call | tf_op jit(solution)/shard_map/pallas_call | solution.py:863
  170.2 12.7 %shard_map.378 = (f32[3]{0:T(128)}, f32[384,1536]{1,0:T(8,128)}, bf16[384,1536]{1,0:T(8,128)(2,1)}, f32[384,1536]{1,0:T(8,128)}, f32[384,1536]{1,0:T(8,128)}, /*...) custom-call(s32[1]{0:T(128)} %bitcast.narrow_ref, ...), custom_call_target="tpu_custom_call" | custom-call | tf_op jit(solution)/shard_map/pallas_call | solution.py:923
  182.8 4.9 %copy.44 = f32[3136,384]{1,0:T(8,128)} copy(f32[3136,384]{1,0:T(8,128)} %get-tuple-element.119) | data formatting | bytes 9633792

commit v5 on v4

--- a/solution.py
+++ b/solution.py
@@ -491,10 +491,10 @@
     return stages
 
 
-def attn_backward(wide_n, narrow_n, comm, tok, qkv_s, prob_in, gm_s, grad_stream_in, attn_w, vec, hot, hmask, hmask2,
+def attn_backward(wide_n, narrow_n, comm, tok, qkv_s, prob_in, gm_s, vec, hot, hmask, hmask2,
                   dmlp, dhid, dvec2, stats,
-                  input_grad, dwq, misc, mine_out,
-                  wq, pj, gp_s, low_s, turn_s, dext, dvec, dtable, flat, send0, recv0, acc, zsend, zrecv, *rest):
+                  dproj_out, dwq, misc, mine_out,
+                  pj, gp_s, low_s, turn_s, dext, dtable, flat, send0, recv0, acc, zsend, zrecv, *rest):
     step = pl.program_id(0)
     steps = pl.num_programs(0)
     static_steps = comm[1]
@@ -524,8 +524,7 @@
 
     @pl.when(step == 0)
     def _():
-        wq[...] = attn_w[:, : 3 * width].astype(bf16)
-        for ref in (dwq, dext, dvec, dtable):
+        for ref in (dwq, dext, dtable):
             ref[...] = jnp.zeros_like(ref)
 
     def first(b, carry):
@@ -563,25 +562,23 @@
             pj[rows, width + 128 * g : width + 128 * g + 128] = nn(low_s[i, g], q_bd)
             pj[rows, 2 * width + 128 * g : 2 * width + 128 * g + 128] = nn(padded(prob_in[i, g]).astype(bf16), do_bd)
     dproj = pj[:CR, :].astype(bf16)
+    dproj_out[...] = dproj
     x = tok[...].astype(f32)
-    xhat, inverse = norm_stats(x)
+    xhat, _ = norm_stats(x)
     low = (xhat * vec[0:1] + vec[1:2]).astype(bf16)
     low_t = jnp.concatenate([low.T, jnp.ones((16, CR), bf16)], 0)
     for j in range(3):
         outer = nn(low_t, dproj[:, width * j : width * j + width])
         dwq[j] += outer[:width]
         dext[j] += outer[width : width + 8]
-    grad_normed = nt(dproj, wq[...])
-    dvec[0] += fold_rows(grad_normed * xhat)
-    dvec[1] += fold_rows(grad_normed)
-    input_grad[...] = grad_stream_in[...] + norm_grad(grad_normed, xhat, inverse, vec[0:1])
 
     @pl.when(step == steps - 1)
     def _():
-        rows = [dvec[0], dvec[1], None, None, dvec2[3], dvec2[0], dvec2[1], dvec2[2]]
+        rows = [None, None, None, None, dvec2[3], dvec2[0], dvec2[1], dvec2[2]]
         for i, part in enumerate(rows):
             if part is not None:
                 misc[i : i + 1, :] = jnp.sum(part, 0, keepdims=True)
+        misc[0:2, :] = jnp.zeros((2, width), f32)
         misc[2:3, :] = dext[0, 0:1, :]
         misc[3:4, :] = dext[2, 0:1, :]
         for i in range(dhid.shape[1] // width):
@@ -628,7 +625,7 @@
 
 def by_step(a, steps):
     nd = len(a.shape)
-    return pl.BlockSpec((a.shape[0] // steps,) + tuple(a.shape[1:]), lambda c: (c,) + (0,) * (nd - 1))
+    return pl.BlockSpec((a.shape[0] // steps,) + tuple(a.shape[1:]), lambda c, *_: (c,) + (0,) * (nd - 1))
 
 
 def run(body, steps, scalars, stepped, wholes, out_stepped, out_wholes, scratch, flops, collective_id=None):
@@ -655,221 +652,248 @@
     lax.fori_loop(0, total // size, lambda i, c: (body(pl.multiple_of(i * size, size), size), c)[1], 0)
 
 
-def reduce_all(wide_n, narrow_n, share, mine_ref, q_ref, o_ref, s_ref, gm_out, gt_out, s_out,
-               recv0, acct, zsend, zrecv, gm, gt, sbuf, srecv, szrecv, *rest):
-    bufs = rest[:-2]
+def attn_chains(wide_n, half):
+    rest = list(range(1, wide_n.bit_length() - 1))
+    turned = rest[len(rest) // 2 :] + rest[: len(rest) // 2]
+    chains, start = [], 0
+    while start < half:
+        sizes = [min(64, half - start)]
+        for _ in rest:
+            sizes.append(sizes[-1] // 2 if sizes[-1] % 32 == 0 else sizes[-1])
+        chains.append((start, turned if len(chains) % 2 else rest, sizes))
+        start += sizes[0]
+    return chains
+
+
+def reduce_all(wide_n, narrow_n, share, mine_ref, q_ref, o_ref, s_ref, vec, dproj, tok, attn_w, gm_out, gt_out, s_out, part_out,
+               proj_s, tok_s, part_s, wide_w, wq, dvec, own_sem, recv0, acct, gm, gt, sbuf, srecv, szrecv, *rest):
+    bufs = list(rest[:-2])
     links = Links(wide_n, narrow_n, *rest[-2:])
-    bit, me_n, peer, n_bits = links.bit, links.n, links.peer, links.bits
-    plan, m_streams, m_sizes = scatter_sizes(wide_n, share)
+    bit, me_n, peer = links.bit, links.n, links.peer
+    steps = links.bits - 1
+    width = q_ref.shape[1]
+    blocks = proj_s.shape[0]
+    at_block = [pl.ds(CR * b, CR) for b in range(blocks)]
+    from_hbm = [pltpu.make_async_copy(attn_w.at[:, pl.ds(0, 3 * width)], wide_w, own_sem.at[0])]
+    for b in range(blocks):
+        from_hbm.append(pltpu.make_async_copy(dproj.at[at_block[b], :], proj_s.at[b], own_sem.at[1 + 2 * b]))
+        from_hbm.append(pltpu.make_async_copy(tok.at[at_block[b], :], tok_s.at[b], own_sem.at[2 + 2 * b]))
+    to_hbm = [pltpu.make_async_copy(part_s.at[b], part_out.at[at_block[b], :], own_sem.at[1 + 2 * blocks + b]) for b in range(blocks)]
+    for c in from_hbm:
+        c.start()
     links.barrier()
     ht = acct.shape[1]
-    steps = n_bits - 1
-
-    def attn_rows(n, start, size):
-        flat = n * share
-        if flat < q_ref.shape[0]:
-            return q_ref[pl.ds(flat + start, size), :]
-        return o_ref[pl.ds(flat - q_ref.shape[0] + start, size), :]
-
-    m_trail = []
-    m_place = {}
-    for st, (start, _) in m_streams.items():
+    away, keep = (1 - bit[0]) * ht, bit[0] * ht
+
+    def rows_at(at, size):
+        return pl.ds(pl.multiple_of(at, 16), size)
+
+    def go(copies):
+        for c in copies:
+            c.start()
+
+    def come(copies):
+        for c in copies:
+            c.wait_recv()
+
+    def attn_chain(start, order, sizes):
+        copies = []
+        for n in range(narrow_n):
+            flat = n * share
+            src, off = (q_ref, flat) if flat < q_ref.shape[0] else (o_ref, flat - q_ref.shape[0])
+            copies.append(links.copy(src.at[rows_at(off + away + start, sizes[0]), :],
+                                     recv0.at[n, pl.ds(start, sizes[0]), :], links.along(0)))
+        go(copies)
+        yield
+        come(copies)
+        for n in range(narrow_n):
+            flat = n * share
+            src, off = (q_ref, flat) if flat < q_ref.shape[0] else (o_ref, flat - q_ref.shape[0])
+            def add0(i, size):
+                acct[n, pl.ds(start + i, size), :] = (src[rows_at(off + keep + start + i, size), :]
+                                                      + recv0[n, pl.ds(start + i, size), :])
+            loop_rows(sizes[0], add0)
         here = start
+        trail = []
         for s in range(steps):
-            b = plan[st][s]
-            size = m_sizes[st][s + 1]
-            halves = size < m_sizes[st][s]
-            here = here + bit[b] * size if halves else here
-            m_trail.append((st, s, b, here, size, halves))
-        m_place[st] = here
-    base = 0
-    for st in m_streams:
-        size = m_sizes[st][-1]
-        gm[pl.ds(pl.multiple_of(bit[0] * share + m_place[st], 16), size), :] = mine_ref[base : base + size, :]
-        base += size
-    m_back = []
-    for s in reversed(range(steps)):
-        stage = []
-        for st, s2, b, at, size, halves in m_trail:
-            if s2 == s and halves:
-                part = gm.at[pl.ds(pl.multiple_of(bit[0] * share + at, 16), size), :]
-                stage.append(links.copy(part, part, links.along(b)))
-        m_back.append(stage)
-    part = gm.at[pl.ds(pl.multiple_of(bit[0] * share, 16), share), :]
-    m_back.append([links.copy(part, part, links.along(0))])
-    m_back.append([])
-
-    def back(k):
-        if 0 < k <= len(m_back) - 1:
-            for c in m_back[k - 1]:
-                c.wait_recv()
-        if k < len(m_back):
-            for c in m_back[k]:
-                c.start()
-
-    away_t, keep_t = (1 - bit[0]) * ht, bit[0] * ht
-    sbuf[0] = s_ref[...]
-    copies = [links.copy(sbuf.at[0], srecv.at[0], links.along(0))]
-    copies[0].start()
-    for n in range(narrow_n):
-        flat = n * share
-        src, off = (q_ref, flat) if flat < q_ref.shape[0] else (o_ref, flat - q_ref.shape[0])
-        c = links.copy(src.at[pl.ds(pl.multiple_of(off + away_t, 16), ht), :], recv0.at[n], links.along(0))
-        c.start()
-        copies.append(c)
-    back(0)
-    copies[0].wait_recv()
-    sbuf[1] = sbuf[0] + srecv[0]
-    for n in range(narrow_n):
-        copies[n + 1].wait_recv()
-        def add_t(i, size):
-            acct[n, pl.ds(i, size), :] = attn_rows(n, pl.multiple_of(keep_t + i, 16), size) + recv0[n, pl.ds(i, size), :]
-        loop_rows(ht, add_t)
-
-    streams, sizes = t_streams(wide_n, ht)
-    place = {st: streams[st][0] for st in streams}
-    trail = []
-    for s in range(steps):
-        work = []
-        small = links.copy(sbuf.at[1 + s], srecv.at[1 + s], links.along(plan["A"][s]))
-        small.start()
-        for k, st in enumerate(streams):
-            b = plan[st][s]
-            size = sizes[st][s + 1]
-            halves = size < sizes[st][s]
-            send, recv = bufs[2 * (2 * s + k)], bufs[2 * (2 * s + k) + 1]
-            here = place[st]
+            b, size = order[s], sizes[s + 1]
+            halves = size < sizes[s]
+            send, recv = bufs.pop(0), bufs.pop(0)
             out_at, in_at = (here + (1 - bit[b]) * size, here + bit[b] * size) if halves else (here, here)
             for n in range(narrow_n):
-                def pack(i, k2):
-                    send[n, pl.ds(i, k2), :] = acct[n, pl.ds(pl.multiple_of(out_at + i, 16), k2), :].astype(send.dtype)
+                def pack(i, k):
+                    send[n, pl.ds(i, k), :] = acct[n, rows_at(out_at + i, k), :].astype(bf16)
                 loop_rows(size, pack)
             c = links.copy(send, recv, links.along(b))
             c.start()
-            work.append((send, recv, in_at, size, halves, c))
-            trail.append((st, s, b, in_at, size, halves))
-            place[st] = in_at
-        back(1 + s)
-        small.wait_recv()
-        sbuf[2 + s] = sbuf[1 + s] + srecv[1 + s]
-        for send, recv, in_at, size, halves, c in work:
+            yield
             c.wait_recv()
             for n in range(narrow_n):
-                def add(i, k2):
-                    here = pl.ds(pl.multiple_of(in_at + i, 16), k2)
-                    mine = acct[n, here, :] if halves else send[n, pl.ds(i, k2), :].astype(f32)
-                    acct[n, here, :] = mine + recv[n, pl.ds(i, k2), :].astype(f32)
+                def add(i, k):
+                    own = acct[n, rows_at(in_at + i, k), :] if halves else send[n, pl.ds(i, k), :].astype(f32)
+                    acct[n, rows_at(in_at + i, k), :] = own + recv[n, pl.ds(i, k), :].astype(f32)
                 loop_rows(size, add)
-
-    z_base, total = {}, 0
-    for st in streams:
-        z_base[st] = total
-        total += sizes[st][-1]
-    copies = []
-    for i, n in enumerate(peer):
-        c = links.copy(sbuf.at[n_bits], szrecv.at[i], links.over(n))
-        c.start()
-        copies.append(c)
-    for i, n in enumerate(peer):
-        for st in streams:
+            here = in_at
+            trail.append((b, in_at, size, halves))
+        size = sizes[-1]
+        zsend, zrecv = bufs.pop(0), bufs.pop(0)
+        copies = []
+        for i, n in enumerate(peer):
             def pack(r, k):
-                zsend[i, pl.ds(z_base[st] + r, k), :] = acct[n, pl.ds(pl.multiple_of(place[st] + r, 16), k), :].astype(bf16)
-            loop_rows(sizes[st][-1], pack)
-        c = links.copy(zsend.at[i], zrecv.at[i], links.over(n))
-        c.start()
-        copies.append(c)
-    for k in range(1 + steps, len(m_back)):
-        back(k)
-    for c in copies:
-        c.wait_recv()
-    for st in streams:
-        top = keep_t + place[st]
+                zsend[i, pl.ds(r, k), :] = acct[n, rows_at(here + r, k), :].astype(bf16)
+            loop_rows(size, pack)
+            copies.append(links.copy(zsend.at[i], zrecv.at[i], links.over(n)))
+            copies[-1].start()
+        yield
+        come(copies)
         def add(r, k):
-            value = acct[me_n, pl.ds(pl.multiple_of(place[st] + r, 16), k), :]
+            value = acct[me_n, rows_at(here + r, k), :]
             for i in range(narrow_n - 1):
-                value = value + zrecv[i, pl.ds(z_base[st] + r, k), :].astype(f32)
-            gt[me_n, pl.ds(pl.multiple_of(top + r, 16), k), :] = value.astype(bf16)
-        loop_rows(sizes[st][-1], add)
-
-    pending = []
-    for st in streams:
-        where = pl.ds(pl.multiple_of(keep_t + place[st], 16), sizes[st][-1])
-        for n in peer:
-            part = gt.at[me_n, where, :]
-            c = links.copy(part, part, links.over(n))
-            c.start()
-            pending.append(c)
-    zero = sbuf[n_bits]
-    total_s = jnp.zeros_like(zero)
-    for n in range(narrow_n):
-        behind = lax.rem(me_n + narrow_n - n, narrow_n)
-        value = zero
-        for i in range(1, narrow_n):
-            value = jnp.where(behind == i, szrecv[i - 1], value)
-        total_s = total_s + value
-    s_out[...] = total_s
-    gm_out[...] = gm[...]
-    for s in reversed(range(steps)):
-        for c in pending:
-            c.wait_recv()
-        pending = []
-        for st, s2, b, at, size, halves in trail:
-            if s2 == s and halves:
-                part = gt.at[:, pl.ds(pl.multiple_of(keep_t + at, 16), size), :]
+                value = value + zrecv[i, pl.ds(r, k), :].astype(f32)
+            gt[me_n, rows_at(keep + here + r, k), :] = value.astype(bf16)
+        loop_rows(size, add)
+        part = gt.at[me_n, rows_at(keep + here, size), :]
+        copies = [links.copy(part, part, links.over(n)) for n in peer]
+        go(copies)
+        yield
+        come(copies)
+        for b, at, size, halves in reversed(trail):
+            if halves:
+                part = gt.at[:, rows_at(keep + at, size), :]
                 c = links.copy(part, part, links.along(b))
                 c.start()
-                pending.append(c)
-    for c in pending:
+                yield
+                c.wait_recv()
+        part = gt.at[:, rows_at(keep + start, sizes[0]), :]
+        c = links.copy(part, part, links.along(0))
+        c.start()
+        yield
         c.wait_recv()
-    part = gt.at[:, pl.ds(pl.multiple_of(keep_t, 16), ht), :]
-    c = links.copy(part, part, links.along(0))
-    c.start()
-    c.wait_recv()
+
+    def small_chain():
+        yield
+        from_hbm[0].wait()
+        wq[...] = wide_w[...].astype(bf16)
+        dvec[...] = jnp.zeros_like(dvec)
+        for b in range(blocks):
+            from_hbm[1 + 2 * b].wait()
+            from_hbm[2 + 2 * b].wait()
+            xhat, inverse = norm_stats(tok_s[b].astype(f32))
+            grad_normed = nt(proj_s[b], wq[...])
+            dvec[0] += fold_rows(grad_normed * xhat)
+            dvec[1] += fold_rows(grad_normed)
+            part_s[b] = norm_grad(grad_normed, xhat, inverse, vec[0:1]).astype(bf16)
+            to_hbm[b].start()
+            yield
+        sbuf[0] = s_ref[...]
+        for i in range(2):
+            sbuf[0, i : i + 1, :] = jnp.sum(dvec[i], 0, keepdims=True)
+        for b in range(links.bits):
+            c = links.copy(sbuf.at[b], srecv.at[b], links.along(b))
+            c.start()
+            yield
+            c.wait_recv()
+            sbuf[b + 1] = sbuf[b] + srecv[b]
+        copies = [links.copy(sbuf.at[links.bits], szrecv.at[i], links.over(n)) for i, n in enumerate(peer)]
+        go(copies)
+        yield
+        come(copies)
+        own = sbuf[links.bits]
+        total = jnp.zeros_like(own)
+        for n in range(narrow_n):
+            behind = lax.rem(me_n + narrow_n - n, narrow_n)
+            value = own
+            for i in range(1, narrow_n):
+                value = jnp.where(behind == i, szrecv[i - 1], value)
+            total = total + value
+        s_out[...] = total
+
+    def mlp_chain():
+        plan, streams, sizes = scatter_sizes(wide_n, share)
+        trail, base = [], 0
+        for st, (here, _) in streams.items():
+            for s in range(steps):
+                b, size = plan[st][s], sizes[st][s + 1]
+                halves = size < sizes[st][s]
+                here = here + bit[b] * size if halves else here
+                trail.append((s, b, here, size, halves))
+            size = sizes[st][-1]
+            gm[rows_at(bit[0] * share + here, size), :] = mine_ref[base : base + size, :]
+            base += size
+        yield
+        yield
+        for s in reversed(range(steps)):
+            copies = []
+            for s2, b, at, size, halves in trail:
+                if s2 == s and halves:
+                    part = gm.at[rows_at(bit[0] * share + at, size), :]
+                    copies.append(links.copy(part, part, links.along(b)))
+            go(copies)
+            yield
+            come(copies)
+        part = gm.at[rows_at(bit[0] * share, share), :]
+        c = links.copy(part, part, links.along(0))
+        c.start()
+        yield
+        c.wait_recv()
+        gm_out[...] = gm[...]
+
+    going = [attn_chain(*c) for c in attn_chains(wide_n, ht)] + [mlp_chain(), small_chain()]
+    while going:
+        still = []
+        for chain in going:
+            try:
+                next(chain)
+                still.append(chain)
+            except StopIteration:
+                pass
+        going = still
     gt_out[...] = gt[...]
     for c in links.all:
         c.wait_send()
-
-
-def t_streams(wide_n, ht):
-    rest = range(1, wide_n.bit_length() - 1)
-    cut = ht * 2 // 3
-    streams = {"A": (0, cut), "B": (cut, ht - cut)}
-    sizes = {}
-    for st, (_, size) in streams.items():
-        sizes[st] = [size]
-        for _ in rest:
-            sizes[st].append(sizes[st][-1] // 2 if sizes[st][-1] % 32 == 0 else sizes[st][-1])
-    return streams, sizes
-
-
-def reduce_call(wide_n, narrow_n, share, mine, dq, do, misc):
+    for c in to_hbm:
+        c.wait()
+
+
+def reduce_call(wide_n, narrow_n, share, mine, dq, do, misc, vec, dproj, tok, attn_w):
     width = mine.shape[1]
+    rows = tok.shape[0]
+    blocks = rows // CR
     ht = share // 2
     n_bits = wide_n.bit_length() - 1
-    streams, sizes = t_streams(wide_n, ht)
-    last = sum(sizes[st][-1] for st in streams)
     scratch = [
+        pltpu.VMEM((blocks, CR, 3 * width), bf16), pltpu.VMEM((blocks, CR, width), bf16), pltpu.VMEM((blocks, CR, width), bf16),
+        pltpu.VMEM((width, 3 * width), f32), pltpu.VMEM((width, 3 * width), bf16), pltpu.VMEM((2, 8, width), f32),
+        pltpu.SemaphoreType.DMA((1 + 3 * blocks,)),
         pltpu.VMEM((narrow_n, ht, width), f32), pltpu.VMEM((narrow_n, ht, width), f32),
-        pltpu.VMEM((narrow_n - 1, last, width), bf16), pltpu.VMEM((narrow_n - 1, last, width), bf16),
         pltpu.VMEM((2 * share, width), bf16), pltpu.VMEM((narrow_n, share, width), bf16),
         pltpu.VMEM((n_bits + 1,) + misc.shape, f32), pltpu.VMEM((n_bits,) + misc.shape, f32),
         pltpu.VMEM((narrow_n - 1,) + misc.shape, f32)]
-    for s in range(n_bits - 1):
-        for st in streams:
-            scratch += [pltpu.VMEM((narrow_n, sizes[st][s + 1], width), bf16)] * 2
-    copies = 2 + narrow_n + 7 * n_bits + 4 * narrow_n
+    order = order_of_bufs(wide_n, narrow_n, ht)
+    scratch += [pltpu.VMEM((lead, rows, width), bf16) for lead, rows in order for _ in range(2)]
+    chains = len(attn_chains(wide_n, ht))
+    copies = chains * (narrow_n + 2 * n_bits + 2 * narrow_n) + 4 * n_bits + narrow_n
     scratch += [pltpu.SemaphoreType.DMA((copies,)), pltpu.SemaphoreType.DMA((copies,))]
     vmem = pl.BlockSpec(memory_space=pltpu.VMEM)
     return pl.pallas_call(
         functools.partial(reduce_all, wide_n, narrow_n, share),
-        out_shape=[sds((2 * share, width), bf16), sds((narrow_n, share, width), bf16), sds(misc.shape, f32)],
-        in_specs=[vmem] * 4, out_specs=[vmem] * 3, scratch_shapes=scratch,
+        out_shape=[sds((2 * share, width), bf16), sds((narrow_n, share, width), bf16), sds(misc.shape, f32),
+                   sds((rows, width), bf16)],
+        in_specs=[vmem] * 5 + [pl.BlockSpec(memory_space=pl.ANY)] * 3, out_specs=[vmem] * 3 + [pl.BlockSpec(memory_space=pl.ANY)], scratch_shapes=scratch,
         compiler_params=pltpu.CompilerParams(collective_id=0, has_side_effects=True, vmem_limit_bytes=60 * 1024 * 1024),
-    )(mine, dq, do, misc)
-
-
-def adam_kernel(narrow_ref, gt, gm, misc, aw, af, as_, mw, mf, ms, tw, tf, ts, vw, vf, vs, bw, bf, bs,
-                rms, an, al, afn, asn, mn, ml, mfn, msn, tn_, tfn, tsn, vn, vfn, vsn, bn, bfn, bsn):
+    )(mine, dq, do, misc, vec, dproj, tok, attn_w)
+
+
+def order_of_bufs(wide_n, narrow_n, ht):
+    chains = attn_chains(wide_n, ht)
+    out = []
+    for s in range(wide_n.bit_length() - 2):
+        out += [(narrow_n, sizes[s + 1]) for _, _, sizes in chains]
+    return out + [(narrow_n - 1, sizes[-1]) for _, _, sizes in chains]
+
+
+def adam_kernel(narrow_ref, grad_stream, part, gt, gm, misc, aw, af, as_, mw, mf, ms, tw, tf, ts, vw, vf, vs, bw, bf, bs,
+                input_grad, rms, an, al, afn, asn, mn, ml, mfn, msn, tn_, tfn, tsn, vn, vfn, vsn, bn, bfn, bsn):
     def put(new, w, g, m, v, rate, decay, low=None):
         out = adam_step(w, g, m, v, rate, decay)
         for ref, value in zip(new, out):
@@ -877,6 +901,7 @@
         if low is not None:
             low[...] = out[0].astype(bf16).reshape(low.shape)
 
+    input_grad[...] = grad_stream[...] + part[...].astype(f32)
     put((an, afn, asn), aw[...], jnp.concatenate([gt[j].astype(f32) for j in range(4)], 1), af[...], as_[...], 0.02, 0.05, al)
     put((mn, mfn, msn), mw[0], gm[0].astype(f32), mf[0], ms[0], 0.02, 0.05, ml)
 
@@ -899,11 +924,12 @@
         put((tn_, tfn, tsn), tw[...], misc[16 : 16 + heads, :count], tf[...], ts[...], 0.3, 0.0)
 
 
-def adam_call(narrow, gt, gm, misc, attn, mlp, table, vec, bias):
+def adam_call(narrow, grad_stream, part, gt, gm, misc, attn, mlp, table, vec, bias):
     width = gm.shape[1]
     share = mlp[0].shape[1]
     gt = gt.reshape(4, width, width)
-    cuts = 8
+    cuts = 4 if grad_stream.shape[0] % 64 == 0 else 2
+    some = by_step(grad_stream, cuts)
     quarter = 2 * share // cuts
     rows = width // cuts
     gm = gm.reshape(cuts, quarter, width)
@@ -912,13 +938,13 @@
     lead = pl.BlockSpec((1, quarter, width), lambda j, *_: (j, 0, 0))
     split = pl.BlockSpec((4, rows, width), lambda j, *_: (0, j, 0))
     smalls = list(table) + list(vec) + list(bias)
-    args = [gt, gm, misc] + list(attn) + mlp + smalls
-    in_specs = [split, lead, whole(misc)] + [line] * 3 + [lead] * 3 + [whole(a) for a in smalls]
+    args = [grad_stream, part, gt, gm, misc] + list(attn) + mlp + smalls
+    in_specs = [some, some, split, lead, whole(misc)] + [line] * 3 + [lead] * 3 + [whole(a) for a in smalls]
     three = lambda a: [sds(a.shape, f32)] * 3
-    outs = [sds((3,), f32), sds(attn[0].shape, f32), sds(attn[0].shape, bf16)] + [sds(attn[0].shape, f32)] * 2
+    outs = [sds(grad_stream.shape, f32), sds((3,), f32), sds(attn[0].shape, f32), sds(attn[0].shape, bf16)] + [sds(attn[0].shape, f32)] * 2
     outs += [sds(mlp[0].shape, f32), sds(mlp[0].shape, bf16)] + [sds(mlp[0].shape, f32)] * 2
     outs += three(table[0]) + three(vec[0]) + three(bias[0])
-    out_specs = [pl.BlockSpec(memory_space=pltpu.SMEM)] + [line] * 4 + [lead] * 4
+    out_specs = [some, pl.BlockSpec(memory_space=pltpu.SMEM)] + [line] * 4 + [lead] * 4
     out_specs += [whole_out(a) for a in smalls]
     r = pl.pallas_call(
         adam_kernel,
@@ -927,7 +953,8 @@
         compiler_params=pltpu.CompilerParams(vmem_limit_bytes=60 * 1024 * 1024),
     )(narrow, *args)
     full = (2, share, width)
-    return [r[0], *r[1:5], *[a.T for a in r[9:12]], *r[12:15], *[a.reshape(full) for a in r[5:9]], *r[15:18]]
+    grad, r = r[0], r[1:]
+    return [grad, r[0], *r[1:5], *[a.T for a in r[9:12]], *r[12:15], *[a.reshape(full) for a in r[5:9]], *r[15:18]]
 
 
 def bias_layout(rel_table):
@@ -995,19 +1022,18 @@
             bufs += [pltpu.VMEM((narrow_n, sizes[st][s + 1], width), bf16)] * 2
     copies = 1 + 2 * n_bits + narrow_n
     sem = [pltpu.SemaphoreType.DMA((copies,)), pltpu.SemaphoreType.DMA((copies,))] if linked else []
-    input_grad, dwq, misc, mine = run(
-        functools.partial(attn_backward, wide_n, narrow_n, comm), steps, (), (tokens, qkv, prob, gm, grad_stream),
-        wholes_of(attn_weight, vectors, hot, mask, mask2, dmlp, dhid, dvec2, stats),
-        [sds((rows, width), f32)],
+    dproj, dwq, misc, mine = run(
+        functools.partial(attn_backward, wide_n, narrow_n, comm), steps, (), (tokens, qkv, prob, gm),
+        wholes_of(vectors, hot, mask, mask2, dmlp, dhid, dvec2, stats),
+        [sds((rows, 3 * width), bf16)],
         [sds((3, width, width), f32), sds((32, width), f32), sds((last, width), bf16)],
-        [pltpu.VMEM((width, 3 * width), bf16), pltpu.VMEM((pad, 3 * width), f32),
-         pltpu.VMEM((CW, groups, KR, HG * SLOT), f32), turned, turned, pltpu.VMEM((3, 8, width), f32),
-         pltpu.VMEM((2, 8, width), f32), table_s, flat,
+        [pltpu.VMEM((pad, 3 * width), f32),
+         pltpu.VMEM((CW, groups, KR, HG * SLOT), f32), turned, turned, pltpu.VMEM((3, 8, width), f32), table_s, flat,
          pltpu.VMEM((narrow_n, share, width), bf16), pltpu.VMEM((narrow_n, share, width), bf16),
          pltpu.VMEM((narrow_n, share, width), f32), pltpu.VMEM((narrow_n - 1, last, width), bf16),
          pltpu.VMEM((narrow_n - 1, last, width), bf16)] + bufs + sem,
         20 * unit, 2 if linked else None)
-    return outputs, input_grad, dmlp, dwq, dwo, misc, mine
+    return outputs, grad_stream, dmlp, dwq, dwo, misc, mine, dproj
 
 
 TILE = 768
@@ -1027,13 +1053,14 @@
            bias_second):
     width = tokens.shape[1]
     narrow = lax.axis_index("narrow").reshape(1).astype(jnp.int32)
-    outputs, input_grad, _, dwq, dwo, misc, mine = block(
+    outputs, grad_stream, _, dwq, dwo, misc, mine, dproj = block(
         tokens, grid_sizes, cotangent, attn_weight, rel_table.T, vectors, mlp_weight, mlp_bias, narrow, wide_n, narrow_n)
-    gm, gt, misc = reduce_call(wide_n, narrow_n, mlp_weight.shape[1], mine, dwq.reshape(3 * width, width), dwo, misc)
-    new = adam_call(narrow, gt, gm, misc, (attn_weight, attn_first, attn_second), (mlp_weight, mlp_first, mlp_second),
+    gm, gt, misc, part = reduce_call(wide_n, narrow_n, mlp_weight.shape[1], mine, dwq.reshape(3 * width, width), dwo, misc,
+                                     vectors, dproj, tokens, attn_weight)
+    new = adam_call(narrow, grad_stream, part, gt, gm, misc, (attn_weight, attn_first, attn_second), (mlp_weight, mlp_first, mlp_second),
                     (rel_table.T, table_first.T, table_second.T), (vectors, vector_first, vector_second),
                     (mlp_bias, bias_first, bias_second))
-    return (outputs, input_grad, *new)
+    return (outputs, *new)
 
 
 def solution(mesh):

time: 188 us -> 174 us (0.926)
  Pallas kernels: 182 us -> 173 us
  local copies, waits for them, and re-layouts: 4.89 us -> 0 us
    pallas_call x1, Pallas kernels: 45.3 us -> 39.8 us  [reduce_call(): pl.pallas_call(functools.partial(reduce_all, wide_n, narrow_n, share), ou...]
    unnamed x1 -> x0, local copies, waits for them, and re-layouts: 4.89 us -> none
    pallas_call x3, Pallas kernels: 124 us -> 120 us  [run(): pl.pallas_call(body, grid=(steps,), in_specs=[smem] * len(scalars) + [by_...]
where the time goes in v5:
time: 174 us
  Pallas kernels  173 us (99%)
    pallas_call x3, Pallas kernels, run(): pl.pallas_call(body, grid=(steps,), in_specs=[smem] * len(scalars) + [by_...  120 us
    pallas_call x1, Pallas kernels, reduce_call(): pl.pallas_call(functools.partial(reduce_all, wide_n, narrow_n, share), ou...  39.8 us
    pallas_call x1, Pallas kernels, adam_call(): pl.pallas_call(adam_kernel, grid_spec=pltpu.PrefetchScalarGridSpec(num_sc...  13.5 us

profile of v5, /device:TPU:0, one launch (start us, length us, event | category | flops | bytes accessed | tf_op | source)
XLA Modules:
  0.0 174.3 jit_solution(18407245008442962389)
XLA Ops:
  0.7 36.2 %shard_map.374 = (bf16[64,64,1152]{2,1,0:T(8,128)(2,1)}, f32[64,3,56,256]{3,2,1,0:T(8,128)}, bf16[3136,384]{1,0:T(8,128)(2,1)}, f32[3136,384]{1,0:T(8,128)}, f32...) custom-call(s32[1]{0:T(128)} %bitcast.narrow_ref, s32[16]{0:T(128)} %sides.3, ...), custom_call_target="tpu_custom_call" | custom-call | flops 5549064192 | bytes 20000000 | tf_op jit(solution)/shard_map/pallas_call | solution.py:636
  36.9 48.7 %shard_map.375 = (bf16[3136,384]{1,0:T(8,128)(2,1)}, f32[3136,384]{1,0:T(8,128)}, bf16[64,64,384]{2,1,0:T(8,128)(2,1)}, f32[4,768,384]{2,1,0:T(8,128)}, f32[384,...) custom-call(s32[1]{0:T(128)} %bitcast.narrow_ref, s32[16]{0:T(128)} %sides.3, bf16[3136,384]{1,0:T(8,128)(2,1)} %cot.1, ...), custom_call_target="tpu_custom_call" | custom-call | flops 24045944832 | bytes 20000000 | tf_op jit(solution)/shard_map/pallas_call | solution.py:636
  85.6 35.2 %shard_map.376 = (bf16[3136,1152]{1,0:T(8,128)(2,1)}, f32[3,384,384]{2,1,0:T(8,128)}, f32[32,384]{1,0:T(8,128)}, bf16[96,384]{1,0:T(8,128)(2,1)}) custom-call(bf16[3136,384]{1,0:T(8,128)(2,1)} %tok.5, bf16[64,64,1152]{2,1,0:T(8,128)(2,1)} %get-tuple-element.67.qkv_s, f32[64,3,56,256]{3,2,1,0:T(8,128)} %get-tuple-element.68.prob_in, ...), custom_call_target="tpu_custom_call" | custom-call | flops 9248440320 | bytes 20000000 | tf_op jit(solution)/shard_map/pallas_call | solution.py:636
  120.8 39.8 %shard_map.377 = (bf16[768,384]{1,0:T(8,128)(2,1)}, bf16[4,384,384]{2,1,0:T(8,128)(2,1)}, f32[32,384]{1,0:T(8,128)}, bf16[3136,384]{1,0:T(8,128)(2,1)}) custom-call(bf16[96,384]{1,0:T(8,128)(2,1)} %get-tuple-element.74.mine_ref, f32[1152,384]{1,0:T(8,128)} %bitcast.16, f32[384,384]{1,0:T(8,128)} %get-tuple-element.76.o_ref, ...), custom_call_target="tpu_custom_call" | custom-call | tf_op jit(solution)/shard_map/pallas_call | solution.py:878
  160.6 13.5 %shard_map.378 = (f32[3136,384]{1,0:T(8,128)}, f32[3]{0:T(128)}, f32[384,1536]{1,0:T(8,128)}, bf16[384,1536]{1,0:T(8,128)(2,1)}, f32[384,1536]{1,0:T(8,128)}, /*...) custom-call(s32[1]{0:T(128)} %bitcast.narrow_ref, ...), custom_call_target="tpu_custom_call" | custom-call | tf_op jit(solution)/shard_map/pallas_call | solution.py:949

commit v6 on v5

--- a/solution.py
+++ b/solution.py
@@ -15,6 +15,8 @@
 STEP = 5
 CW = 16
 CR = CW * WTOK
+EVEN = CR // 256 * 256
+ODD = 128
 SLOT = 64
 KR = 56
 HG = 4
@@ -221,7 +223,7 @@
 
 def attn_forward(wide_n, narrow_n, comm, narrow_ref, sides, tok, attn_w, mlp_w, mlp_b, vec, table, hot, rinfo, kinfo, hmask, hmask2,
                  qkv_s, prob_out, mixed_out, stream_out, stats, gw_out, tail_out,
-                 wq, pj, mx, turn_s, bias, wide_t, flat, side_s, own, tail_own, gw, tails, *sems):
+                 wq, pj, mx, turn_s, bias, wide_t, flat, side_s, own, tail_own, gw, tails, wide_w, hot_s, load_sem, *sems):
     step = pl.program_id(0)
     steps = pl.num_programs(0)
     static_steps = comm[1]
@@ -231,8 +233,12 @@
     narrow = narrow_ref[0]
     share = mlp_w.shape[1]
 
+    loads = [pltpu.make_async_copy(attn_w, wide_w, load_sem.at[0]), pltpu.make_async_copy(hot, hot_s, load_sem.at[1])]
+
     @pl.when(step == 0)
     def _():
+        for c in loads:
+            c.start()
         for j in range(2):
             own[share * j : share * j + share, :] = mlp_w[j].astype(bf16)
         tail_own[...] = jnp.zeros_like(tail_own)
@@ -261,9 +267,11 @@
 
     @pl.when(step == 0)
     def _():
-        wq[...] = attn_w[...].astype(bf16)
         fill_sides(sides, rinfo, side_s)
-        expand_table(table, hot, wide_t, flat, bias)
+        for c in loads:
+            c.wait()
+        wq[...] = wide_w[...].astype(bf16)
+        expand_table(table, hot_s, wide_t, flat, bias)
         for ref in (pj, mx, stats):
             ref[...] = jnp.zeros_like(ref)
 
@@ -326,7 +334,7 @@
 
 def feed_forward(tile, narrow_ref, sides, cot, mixed_in, stream_in, attn_w, gw, tails, vec, rinfo,
                  out_ref, grad_stream_out, gm_s, dmlp, dwo, dhid, dvec,
-                 wo, w1, w2, hb, dw1, dw2, mx, side_s):
+                 wo, w1, w2, hb, dw1, dw2, mx, side_s, second_r, grad_r, pre_r, active_r, load_sem):
     step = pl.program_id(0)
     steps = pl.num_programs(0)
     width = cot.shape[1]
@@ -334,17 +342,22 @@
     hidden = w1.shape[0]
     shards_n, twice, _ = gw.shape
     share = twice // 2
+    loads = []
+    for n in range(shards_n):
+        for j, ref in enumerate((w1, w2)):
+            loads.append(pltpu.make_async_copy(gw.at[n, pl.ds(share * j, share), :], ref.at[pl.ds(share * n, share), :],
+                                               load_sem.at[2 * n + j]))
 
     @pl.when(step == 0)
     def _():
+        for c in loads:
+            c.start()
         wo[...] = attn_w[...].astype(bf16)
         for n in range(shards_n):
-            w1[share * n : share * n + share, :] = gw[n, :share, :]
-            w2[share * n : share * n + share, :] = gw[n, share:, :]
             three = tails[n]
             hb[:, share * n : share * n + share] = (three[0:1] + three[1:2] + three[2:3])[:, :share]
         fill_sides(sides, rinfo, side_s)
-        for ref in (mx, dw1, dw2, dwo, dhid, dvec):
+        for ref in (mx, dw1, dw2, dwo, dhid, dvec, second_r, grad_r, pre_r, active_r):
             ref[...] = jnp.zeros_like(ref)
 
     top, left = corner(narrow_ref[0], step, steps)
@@ -355,8 +368,17 @@
     second = (xhat2 * vec[5:6] + vec[6:7]).astype(bf16)
     kept_cot = cotan * keep
     grad_low = kept_cot.astype(bf16)
-    second_t = jnp.concatenate([second.T, jnp.ones((16, CR), bf16)], 0)
-    grad_t = grad_low.T
+    second_t = jnp.concatenate([second[:EVEN].T, jnp.ones((16, EVEN), bf16)], 0)
+    grad_t = grad_low[:EVEN].T
+    odd = pl.ds(pl.multiple_of(step * (CR - EVEN), CR - EVEN), CR - EVEN)
+    second_r[odd, :] = second[EVEN:]
+    grad_r[odd, :] = grad_low[EVEN:]
+
+    @pl.when(step == 0)
+    def _():
+        for c in loads:
+            c.wait()
+
     mlp_out = jnp.zeros((CR, width), f32)
     grad_second = jnp.zeros((CR, width), f32)
     for t in range(hidden // tile):
@@ -369,10 +391,12 @@
         grad_pre = (nt(grad_low, w2[cols, :]) * slope).astype(bf16)
         mlp_out += nn(active, w2[cols, :])
         grad_second += nn(grad_pre, w1[cols, :])
-        outer = nn(second_t, grad_pre)
+        pre_r[odd, cols] = grad_pre[EVEN:]
+        active_r[odd, cols] = active[EVEN:]
+        outer = nn(second_t, grad_pre[:EVEN])
         dw1[:, cols] += outer[:width]
         dhid[:, cols] += outer[width : width + 8]
-        dw2[:, cols] += nn(grad_t, active)
+        dw2[:, cols] += nn(grad_t, active[:EVEN])
     branch = (mlp_out + vec[7:8]) * keep
     out_ref[...] = (stream + branch).astype(bf16)
     dvec[4] += fold_rows(branch * branch)
@@ -391,6 +415,14 @@
 
     @pl.when(step == steps - 1)
     def _():
+        rest_t = jnp.concatenate([second_r[...].T, jnp.ones((16, second_r.shape[0]), bf16)], 0)
+        rest_g = grad_r[...].T
+        for t in range(hidden // width):
+            cols = slice(width * t, width * t + width)
+            outer = nn(rest_t, pre_r[:, cols])
+            dw1[:, cols] += outer[:width]
+            dhid[:, cols] += outer[width : width + 8]
+            dw2[:, cols] += nn(rest_g, active_r[:, cols])
         for j, ref in enumerate((dw1, dw2)):
             for t in range(hidden // width):
                 turned = ref[:, width * t : width * t + width].T
@@ -494,7 +526,7 @@
 def attn_backward(wide_n, narrow_n, comm, tok, qkv_s, prob_in, gm_s, vec, hot, hmask, hmask2,
                   dmlp, dhid, dvec2, stats,
                   dproj_out, dwq, misc, mine_out,
-                  pj, gp_s, low_s, turn_s, dext, dtable, flat, send0, recv0, acc, zsend, zrecv, *rest):
+                  pj, gp_s, low_s, turn_s, dext, dtable, flat, low_r, proj_r, dmlp_s, load_sem, send0, recv0, acc, zsend, zrecv, *rest):
     step = pl.program_id(0)
     steps = pl.num_programs(0)
     static_steps = comm[1]
@@ -502,6 +534,7 @@
     groups = width // 128
     scale = 32 ** (-0.5)
     share = dmlp.shape[1] // 2
+    load = pltpu.make_async_copy(dmlp, dmlp_s, load_sem.at[0])
 
     if comm[0]:
         links = Links(wide_n, narrow_n, *rest[-2:])
@@ -510,21 +543,13 @@
         def _():
             links.barrier()
 
-        stages = scatter_stages(links, wide_n, narrow_n, share, dmlp, mine_out, send0, recv0, acc, zsend, zrecv, rest[:-2])
-        for k, (pack, copies, add) in enumerate(stages):
-            @pl.when(step == min(k, static_steps - 1))
-            def _():
-                if k:
-                    for c in stages[k - 1][1]:
-                        c.wait()
-                    stages[k - 1][2]()
-                pack()
-                for c in copies:
-                    c.start()
+        @pl.when(step == 0)
+        def _():
+            load.start()
 
     @pl.when(step == 0)
     def _():
-        for ref in (dwq, dext, dtable):
+        for ref in (dwq, dext, dtable, low_r, proj_r):
             ref[...] = jnp.zeros_like(ref)
 
     def first(b, carry):
@@ -551,6 +576,21 @@
         return carry
 
     lax.fori_loop(0, CW // BATCH, first, 0)
+    if comm[0]:
+        stages = scatter_stages(links, wide_n, narrow_n, share, dmlp_s, mine_out, send0, recv0, acc, zsend, zrecv, rest[:-2])
+        for k, (pack, copies, add) in enumerate(stages):
+            @pl.when(step == min(k, static_steps - 1))
+            def _():
+                if not k:
+                    load.wait()
+                if k:
+                    for c in stages[k - 1][1]:
+                        c.wait()
+                    stages[k - 1][2]()
+                pack()
+                for c in copies:
+                    c.start()
+
     lax.fori_loop(0, CW // BATCH, second, 0)
     for i in range(CW):
         rows = slice(WTOK * i, WTOK * i + SLOT)
@@ -566,14 +606,22 @@
     x = tok[...].astype(f32)
     xhat, _ = norm_stats(x)
     low = (xhat * vec[0:1] + vec[1:2]).astype(bf16)
-    low_t = jnp.concatenate([low.T, jnp.ones((16, CR), bf16)], 0)
+    low_t = jnp.concatenate([low[:EVEN].T, jnp.ones((16, EVEN), bf16)], 0)
+    odd = pl.ds(pl.multiple_of(step * (CR - EVEN), CR - EVEN), CR - EVEN)
+    low_r[odd, :] = low[EVEN:]
+    proj_r[odd, :] = dproj[EVEN:]
     for j in range(3):
-        outer = nn(low_t, dproj[:, width * j : width * j + width])
+        outer = nn(low_t, dproj[:EVEN, width * j : width * j + width])
         dwq[j] += outer[:width]
         dext[j] += outer[width : width + 8]
 
     @pl.when(step == steps - 1)
     def _():
+        rest_t = jnp.concatenate([low_r[...].T, jnp.ones((16, low_r.shape[0]), bf16)], 0)
+        for j in range(3):
+            outer = nn(rest_t, proj_r[:, width * j : width * j + width])
+            dwq[j] += outer[:width]
+            dext[j] += outer[width : width + 8]
         rows = [None, None, None, None, dvec2[3], dvec2[0], dvec2[1], dvec2[2]]
         for i, part in enumerate(rows):
             if part is not None:
@@ -643,8 +691,8 @@
     )(*scalars, *stepped, *wholes[0])
 
 
-def wholes_of(*arrays):
-    return (arrays, [whole(a) for a in arrays])
+def wholes_of(*arrays, far=()):
+    return (arrays, [pl.BlockSpec(memory_space=pl.ANY) if i in far else whole(a) for i, a in enumerate(arrays)])
 
 
 def loop_rows(total, body):
@@ -995,24 +1043,26 @@
     turned = pltpu.VMEM((CW, groups, SLOT, HG * SLOT), bf16)
     qkv, prob, mixed, stream, stats, gw, tails = run(
         functools.partial(attn_forward, wide_n, narrow_n, comm), steps, scal, (tokens,),
-        wholes_of(attn_weight, mlp_weight, mlp_bias, vectors, rel_table, hot, rinfo, kinfo, mask, mask2),
+        wholes_of(attn_weight, mlp_weight, mlp_bias, vectors, rel_table, hot, rinfo, kinfo, mask, mask2, far=(0, 5)),
         [sds((wins, SLOT, 3 * width), bf16), sds((wins, groups, KR, HG * SLOT), f32), sds((rows, width), bf16), sds((rows, width), f32)],
         [sds((3, 8, width), f32), sds((narrow_n, 2 * share, width), bf16), sds((narrow_n, 8, width), f32)],
         [pltpu.VMEM((width, 4 * width), bf16), pltpu.VMEM((pad, 3 * width), f32), pltpu.VMEM((pad, width), f32), turned,
          table_s, pltpu.VMEM((16, 256), f32), flat, sides,
          pltpu.VMEM((2 * share, width), bf16), pltpu.VMEM((8, width), f32),
-         pltpu.VMEM((narrow_n, 2 * share, width), bf16), pltpu.VMEM((narrow_n, 8, width), f32)] + sem,
+         pltpu.VMEM((narrow_n, 2 * share, width), bf16), pltpu.VMEM((narrow_n, 8, width), f32),
+         pltpu.VMEM((width, 4 * width), f32), pltpu.VMEM(hot.shape, bf16), pltpu.SemaphoreType.DMA((2,))] + sem,
         12 * unit, 1 if linked else None)
     out_proj = pl.BlockSpec((width, width), lambda *_: (0, 3), pipeline_mode=pl.Buffered(1))
     fixed = (attn_weight, gw, tails, vectors, rinfo)
     outputs, grad_stream, gm, dmlp, dwo, dhid, dvec2 = run(
         functools.partial(feed_forward, TILE), steps, scal, (cotangent, mixed, stream),
-        (fixed, [out_proj] + [whole(a) for a in fixed[1:]]),
+        (fixed, [out_proj, pl.BlockSpec(memory_space=pl.ANY)] + [whole(a) for a in fixed[2:]]),
         [sds((rows, width), bf16), sds((rows, width), f32), sds((wins, SLOT, width), bf16)],
         [sds((narrow_n, 2 * share, width), f32), sds((width, width), f32), sds((8, hidden), f32), sds((5, 8, width), f32)],
         [pltpu.VMEM((width, width), bf16), pltpu.VMEM((hidden, width), bf16), pltpu.VMEM((hidden, width), bf16),
          pltpu.VMEM((1, hidden), f32), pltpu.VMEM((width, hidden), f32), pltpu.VMEM((width, hidden), f32),
-         pltpu.VMEM((pad, width), f32), sides],
+         pltpu.VMEM((pad, width), f32), sides, pltpu.VMEM((ODD, width), bf16), pltpu.VMEM((ODD, width), bf16),
+         pltpu.VMEM((ODD, hidden), bf16), pltpu.VMEM((ODD, hidden), bf16), pltpu.SemaphoreType.DMA((2 * narrow_n,))],
         52 * unit)
     _, streams, sizes = scatter_sizes(wide_n, share)
     last = sum(sizes[st][-1] for st in streams)
@@ -1024,11 +1074,12 @@
     sem = [pltpu.SemaphoreType.DMA((copies,)), pltpu.SemaphoreType.DMA((copies,))] if linked else []
     dproj, dwq, misc, mine = run(
         functools.partial(attn_backward, wide_n, narrow_n, comm), steps, (), (tokens, qkv, prob, gm),
-        wholes_of(vectors, hot, mask, mask2, dmlp, dhid, dvec2, stats),
+        wholes_of(vectors, hot, mask, mask2, dmlp, dhid, dvec2, stats, far=(4,)),
         [sds((rows, 3 * width), bf16)],
         [sds((3, width, width), f32), sds((32, width), f32), sds((last, width), bf16)],
         [pltpu.VMEM((pad, 3 * width), f32),
          pltpu.VMEM((CW, groups, KR, HG * SLOT), f32), turned, turned, pltpu.VMEM((3, 8, width), f32), table_s, flat,
+         pltpu.VMEM((ODD, width), bf16), pltpu.VMEM((ODD, 3 * width), bf16), pltpu.VMEM(dmlp.shape, f32), pltpu.SemaphoreType.DMA((1,)),
          pltpu.VMEM((narrow_n, share, width), bf16), pltpu.VMEM((narrow_n, share, width), bf16),
          pltpu.VMEM((narrow_n, share, width), f32), pltpu.VMEM((narrow_n - 1, last, width), bf16),
          pltpu.VMEM((narrow_n - 1, last, width), bf16)] + bufs + sem,

time: 174 us -> 172 us (0.989)
  Pallas kernels: 173 us -> 171 us
    pallas_call x3, Pallas kernels: 120 us -> 117 us  [run(): pl.pallas_call(body, grid=(steps,), in_specs=[smem] * len(scalars) + [by_...]
where the time goes in v6:
time: 172 us
  Pallas kernels  171 us (99%)
    pallas_call x3, Pallas kernels, run(): pl.pallas_call(body, grid=(steps,), in_specs=[smem] * len(scalars) + [by_...  117 us
    pallas_call x1, Pallas kernels, reduce_call(): pl.pallas_call(functools.partial(reduce_all, wide_n, narrow_n, share), ou...  40.5 us
    pallas_call x1, Pallas kernels, adam_call(): pl.pallas_call(adam_kernel, grid_spec=pltpu.PrefetchScalarGridSpec(num_sc...  13.5 us

profile of v6, /device:TPU:0, one launch (start us, length us, event | category | flops | bytes accessed | tf_op | source)
XLA Modules:
  0.0 171.8 jit_solution(17152120582123300269)
XLA Ops:
  0.7 34.8 %shard_map.374 = (bf16[64,64,1152]{2,1,0:T(8,128)(2,1)}, f32[64,3,56,256]{3,2,1,0:T(8,128)}, bf16[3136,384]{1,0:T(8,128)(2,1)}, f32[3136,384]{1,0:T(8,128)}, f32...) custom-call(s32[1]{0:T(128)} %bitcast.narrow_ref, s32[16]{0:T(128)} %sides.3, ...), custom_call_target="tpu_custom_call" | custom-call | flops 5549064192 | bytes 20000000 | tf_op jit(solution)/shard_map/pallas_call | solution.py:684
  35.5 46.6 %shard_map.375 = (bf16[3136,384]{1,0:T(8,128)(2,1)}, f32[3136,384]{1,0:T(8,128)}, bf16[64,64,384]{2,1,0:T(8,128)(2,1)}, f32[4,768,384]{2,1,0:T(8,128)}, f32[384,...) custom-call(s32[1]{0:T(128)} %bitcast.narrow_ref, s32[16]{0:T(128)} %sides.3, bf16[3136,384]{1,0:T(8,128)(2,1)} %cot.1, ...), custom_call_target="tpu_custom_call" | custom-call | flops 24045944832 | bytes 20000000 | tf_op jit(solution)/shard_map/pallas_call | solution.py:684
  82.0 35.6 %shard_map.376 = (bf16[3136,1152]{1,0:T(8,128)(2,1)}, f32[3,384,384]{2,1,0:T(8,128)}, f32[32,384]{1,0:T(8,128)}, bf16[96,384]{1,0:T(8,128)(2,1)}) custom-call(bf16[3136,384]{1,0:T(8,128)(2,1)} %tok.5, bf16[64,64,1152]{2,1,0:T(8,128)(2,1)} %get-tuple-element.67.qkv_s, f32[64,3,56,256]{3,2,1,0:T(8,128)} %get-tuple-element.68.prob_in, ...), custom_call_target="tpu_custom_call" | custom-call | flops 9248440320 | bytes 20000000 | tf_op jit(solution)/shard_map/pallas_call | solution.py:684
  117.6 40.5 %shard_map.377 = (bf16[768,384]{1,0:T(8,128)(2,1)}, bf16[4,384,384]{2,1,0:T(8,128)(2,1)}, f32[32,384]{1,0:T(8,128)}, bf16[3136,384]{1,0:T(8,128)(2,1)}) custom-call(bf16[96,384]{1,0:T(8,128)(2,1)} %get-tuple-element.74.mine_ref, f32[1152,384]{1,0:T(8,128)} %bitcast.16, f32[384,384]{1,0:T(8,128)} %get-tuple-element.76.o_ref, ...), custom_call_target="tpu_custom_call" | custom-call | tf_op jit(solution)/shard_map/pallas_call | solution.py:926
  158.1 13.5 %shard_map.378 = (f32[3136,384]{1,0:T(8,128)}, f32[3]{0:T(128)}, f32[384,1536]{1,0:T(8,128)}, bf16[384,1536]{1,0:T(8,128)(2,1)}, f32[384,1536]{1,0:T(8,128)}, /*...) custom-call(s32[1]{0:T(128)} %bitcast.narrow_ref, ...), custom_call_target="tpu_custom_call" | custom-call | tf_op jit(solution)/shard_map/pallas_call | solution.py:997

commit v7 on v6

--- a/solution.py
+++ b/solution.py
@@ -832,7 +832,8 @@
             dvec[1] += fold_rows(grad_normed)
             part_s[b] = norm_grad(grad_normed, xhat, inverse, vec[0:1]).astype(bf16)
             to_hbm[b].start()
-            yield
+            if b % 2:
+                yield
         sbuf[0] = s_ref[...]
         for i in range(2):
             sbuf[0, i : i + 1, :] = jnp.sum(dvec[i], 0, keepdims=True)

time: 172 us -> 166 us (0.965)
  Pallas kernels: 171 us -> 165 us
    pallas_call x1, Pallas kernels: 40.5 us -> 34.8 us  [reduce_call(): pl.pallas_call(functools.partial(reduce_all, wide_n, narrow_n, share), ou...]
where the time goes in v7:
time: 166 us
  Pallas kernels  165 us (99%)
    pallas_call x3, Pallas kernels, run(): pl.pallas_call(body, grid=(steps,), in_specs=[smem] * len(scalars) + [by_...  117 us
    pallas_call x1, Pallas kernels, reduce_call(): pl.pallas_call(functools.partial(reduce_all, wide_n, narrow_n, share), ou...  34.8 us
    pallas_call x1, Pallas kernels, adam_call(): pl.pallas_call(adam_kernel, grid_spec=pltpu.PrefetchScalarGridSpec(num_sc...  13.5 us

profile of v7, /device:TPU:0, one launch (start us, length us, event | category | flops | bytes accessed | tf_op | source)
XLA Modules:
  0.0 166.2 jit_solution(4638823311312746535)
XLA Ops:
  0.7 34.8 %shard_map.374 = (bf16[64,64,1152]{2,1,0:T(8,128)(2,1)}, f32[64,3,56,256]{3,2,1,0:T(8,128)}, bf16[3136,384]{1,0:T(8,128)(2,1)}, f32[3136,384]{1,0:T(8,128)}, f32...) custom-call(s32[1]{0:T(128)} %bitcast.narrow_ref, s32[16]{0:T(128)} %sides.3, ...), custom_call_target="tpu_custom_call" | custom-call | flops 5549064192 | bytes 20000000 | tf_op jit(solution)/shard_map/pallas_call | solution.py:684
  35.5 46.6 %shard_map.375 = (bf16[3136,384]{1,0:T(8,128)(2,1)}, f32[3136,384]{1,0:T(8,128)}, bf16[64,64,384]{2,1,0:T(8,128)(2,1)}, f32[4,768,384]{2,1,0:T(8,128)}, f32[384,...) custom-call(s32[1]{0:T(128)} %bitcast.narrow_ref, s32[16]{0:T(128)} %sides.3, bf16[3136,384]{1,0:T(8,128)(2,1)} %cot.1, ...), custom_call_target="tpu_custom_call" | custom-call | flops 24045944832 | bytes 20000000 | tf_op jit(solution)/shard_map/pallas_call | solution.py:684
  82.0 35.6 %shard_map.376 = (bf16[3136,1152]{1,0:T(8,128)(2,1)}, f32[3,384,384]{2,1,0:T(8,128)}, f32[32,384]{1,0:T(8,128)}, bf16[96,384]{1,0:T(8,128)(2,1)}) custom-call(bf16[3136,384]{1,0:T(8,128)(2,1)} %tok.5, bf16[64,64,1152]{2,1,0:T(8,128)(2,1)} %get-tuple-element.67.qkv_s, f32[64,3,56,256]{3,2,1,0:T(8,128)} %get-tuple-element.68.prob_in, ...), custom_call_target="tpu_custom_call" | custom-call | flops 9248440320 | bytes 20000000 | tf_op jit(solution)/shard_map/pallas_call | solution.py:684
  117.6 34.8 %shard_map.377 = (bf16[768,384]{1,0:T(8,128)(2,1)}, bf16[4,384,384]{2,1,0:T(8,128)(2,1)}, f32[32,384]{1,0:T(8,128)}, bf16[3136,384]{1,0:T(8,128)(2,1)}) custom-call(bf16[96,384]{1,0:T(8,128)(2,1)} %get-tuple-element.74.mine_ref, f32[1152,384]{1,0:T(8,128)} %bitcast.16, f32[384,384]{1,0:T(8,128)} %get-tuple-element.76.o_ref, ...), custom_call_target="tpu_custom_call" | custom-call | tf_op jit(solution)/shard_map/pallas_call | solution.py:927
  152.5 13.5 %shard_map.378 = (f32[3136,384]{1,0:T(8,128)}, f32[3]{0:T(128)}, f32[384,1536]{1,0:T(8,128)}, bf16[384,1536]{1,0:T(8,128)(2,1)}, f32[384,1536]{1,0:T(8,128)}, /*...) custom-call(s32[1]{0:T(128)} %bitcast.narrow_ref, ...), custom_call_target="tpu_custom_call" | custom-call | tf_op jit(solution)/shard_map/pallas_call | solution.py:998

commit v8 on v7

--- a/solution.py
+++ b/solution.py
@@ -888,8 +888,12 @@
         gm_out[...] = gm[...]
 
     going = [attn_chain(*c) for c in attn_chains(wide_n, ht)] + [mlp_chain(), small_chain()]
+    rounds = 0
     while going:
         still = []
+        if rounds == 3:
+            going = going[-1:] + going[:-1]
+        rounds += 1
         for chain in going:
             try:
                 next(chain)

time: 166 us -> 165 us (level)
  no operation moved by 1% of the time
where the time goes in v8:
time: 165 us
  Pallas kernels  164 us (99%)
    pallas_call x3, Pallas kernels, run(): pl.pallas_call(body, grid=(steps,), in_specs=[smem] * len(scalars) + [by_...  117 us
    pallas_call x1, Pallas kernels, reduce_call(): pl.pallas_call(functools.partial(reduce_all, wide_n, narrow_n, share), ou...  33.6 us
    pallas_call x1, Pallas kernels, adam_call(): pl.pallas_call(adam_kernel, grid_spec=pltpu.PrefetchScalarGridSpec(num_sc...  13.5 us

profile of v8, /device:TPU:0, one launch (start us, length us, event | category | flops | bytes accessed | tf_op | source)
XLA Modules:
  0.0 164.9 jit_solution(12100210800345615981)
XLA Ops:
  0.7 34.8 %shard_map.374 = (bf16[64,64,1152]{2,1,0:T(8,128)(2,1)}, f32[64,3,56,256]{3,2,1,0:T(8,128)}, bf16[3136,384]{1,0:T(8,128)(2,1)}, f32[3136,384]{1,0:T(8,128)}, f32...) custom-call(s32[1]{0:T(128)} %bitcast.narrow_ref, s32[16]{0:T(128)} %sides.3, ...), custom_call_target="tpu_custom_call" | custom-call | flops 5549064192 | bytes 20000000 | tf_op jit(solution)/shard_map/pallas_call | solution.py:684
  35.5 46.6 %shard_map.375 = (bf16[3136,384]{1,0:T(8,128)(2,1)}, f32[3136,384]{1,0:T(8,128)}, bf16[64,64,384]{2,1,0:T(8,128)(2,1)}, f32[4,768,384]{2,1,0:T(8,128)}, f32[384,...) custom-call(s32[1]{0:T(128)} %bitcast.narrow_ref, s32[16]{0:T(128)} %sides.3, bf16[3136,384]{1,0:T(8,128)(2,1)} %cot.1, ...), custom_call_target="tpu_custom_call" | custom-call | flops 24045944832 | bytes 20000000 | tf_op jit(solution)/shard_map/pallas_call | solution.py:684
  82.0 35.6 %shard_map.376 = (bf16[3136,1152]{1,0:T(8,128)(2,1)}, f32[3,384,384]{2,1,0:T(8,128)}, f32[32,384]{1,0:T(8,128)}, bf16[96,384]{1,0:T(8,128)(2,1)}) custom-call(bf16[3136,384]{1,0:T(8,128)(2,1)} %tok.5, bf16[64,64,1152]{2,1,0:T(8,128)(2,1)} %get-tuple-element.67.qkv_s, f32[64,3,56,256]{3,2,1,0:T(8,128)} %get-tuple-element.68.prob_in, ...), custom_call_target="tpu_custom_call" | custom-call | flops 9248440320 | bytes 20000000 | tf_op jit(solution)/shard_map/pallas_call | solution.py:684
  117.6 33.6 %shard_map.377 = (bf16[768,384]{1,0:T(8,128)(2,1)}, bf16[4,384,384]{2,1,0:T(8,128)(2,1)}, f32[32,384]{1,0:T(8,128)}, bf16[3136,384]{1,0:T(8,128)(2,1)}) custom-call(bf16[96,384]{1,0:T(8,128)(2,1)} %get-tuple-element.74.mine_ref, f32[1152,384]{1,0:T(8,128)} %bitcast.16, f32[384,384]{1,0:T(8,128)} %get-tuple-element.76.o_ref, ...), custom_call_target="tpu_custom_call" | custom-call | tf_op jit(solution)/shard_map/pallas_call | solution.py:931
  151.3 13.5 %shard_map.378 = (f32[3136,384]{1,0:T(8,128)}, f32[3]{0:T(128)}, f32[384,1536]{1,0:T(8,128)}, bf16[384,1536]{1,0:T(8,128)(2,1)}, f32[384,1536]{1,0:T(8,128)}, /*...) custom-call(s32[1]{0:T(128)} %bitcast.narrow_ref, ...), custom_call_target="tpu_custom_call" | custom-call | tf_op jit(solution)/shard_map/pallas_call | solution.py:1002

commit v9 on v8

--- a/solution.py
+++ b/solution.py
@@ -832,7 +832,7 @@
             dvec[1] += fold_rows(grad_normed)
             part_s[b] = norm_grad(grad_normed, xhat, inverse, vec[0:1]).astype(bf16)
             to_hbm[b].start()
-            if b % 2:
+            if b % 2 and b + 1 < blocks:
                 yield
         sbuf[0] = s_ref[...]
         for i in range(2):

time: 165 us -> 168 us (1.018)
  Pallas kernels: 164 us -> 167 us
    pallas_call x1, Pallas kernels: 33.6 us -> 36.1 us  [reduce_call(): pl.pallas_call(functools.partial(reduce_all, wide_n, narrow_n, share), ou...]
where the time goes in v9:
time: 168 us; the launch traced here: 167 us
  Pallas kernels  167 us (99%)
    pallas_call x3, Pallas kernels, run(): pl.pallas_call(body, grid=(steps,), in_specs=[smem] * len(scalars) + [by_...  117 us
    pallas_call x1, Pallas kernels, reduce_call(): pl.pallas_call(functools.partial(reduce_all, wide_n, narrow_n, share), ou...  36.1 us
    pallas_call x1, Pallas kernels, adam_call(): pl.pallas_call(adam_kernel, grid_spec=pltpu.PrefetchScalarGridSpec(num_sc...  13.5 us

profile of v9, /device:TPU:0, one launch (start us, length us, event | category | flops | bytes accessed | tf_op | source)
XLA Modules:
  0.0 167.4 jit_solution(98794873191144135)
XLA Ops:
  0.7 34.8 %shard_map.374 = (bf16[64,64,1152]{2,1,0:T(8,128)(2,1)}, f32[64,3,56,256]{3,2,1,0:T(8,128)}, bf16[3136,384]{1,0:T(8,128)(2,1)}, f32[3136,384]{1,0:T(8,128)}, f32...) custom-call(s32[1]{0:T(128)} %bitcast.narrow_ref, s32[16]{0:T(128)} %sides.3, ...), custom_call_target="tpu_custom_call" | custom-call | flops 5549064192 | bytes 20000000 | tf_op jit(solution)/shard_map/pallas_call | solution.py:684
  35.5 46.6 %shard_map.375 = (bf16[3136,384]{1,0:T(8,128)(2,1)}, f32[3136,384]{1,0:T(8,128)}, bf16[64,64,384]{2,1,0:T(8,128)(2,1)}, f32[4,768,384]{2,1,0:T(8,128)}, f32[384,...) custom-call(s32[1]{0:T(128)} %bitcast.narrow_ref, s32[16]{0:T(128)} %sides.3, bf16[3136,384]{1,0:T(8,128)(2,1)} %cot.1, ...), custom_call_target="tpu_custom_call" | custom-call | flops 24045944832 | bytes 20000000 | tf_op jit(solution)/shard_map/pallas_call | solution.py:684
  82.0 35.6 %shard_map.376 = (bf16[3136,1152]{1,0:T(8,128)(2,1)}, f32[3,384,384]{2,1,0:T(8,128)}, f32[32,384]{1,0:T(8,128)}, bf16[96,384]{1,0:T(8,128)(2,1)}) custom-call(bf16[3136,384]{1,0:T(8,128)(2,1)} %tok.5, bf16[64,64,1152]{2,1,0:T(8,128)(2,1)} %get-tuple-element.67.qkv_s, f32[64,3,56,256]{3,2,1,0:T(8,128)} %get-tuple-element.68.prob_in, ...), custom_call_target="tpu_custom_call" | custom-call | flops 9248440320 | bytes 20000000 | tf_op jit(solution)/shard_map/pallas_call | solution.py:684
  117.6 36.1 %shard_map.377 = (bf16[768,384]{1,0:T(8,128)(2,1)}, bf16[4,384,384]{2,1,0:T(8,128)(2,1)}, f32[32,384]{1,0:T(8,128)}, bf16[3136,384]{1,0:T(8,128)(2,1)}) custom-call(bf16[96,384]{1,0:T(8,128)(2,1)} %get-tuple-element.74.mine_ref, f32[1152,384]{1,0:T(8,128)} %bitcast.16, f32[384,384]{1,0:T(8,128)} %get-tuple-element.76.o_ref, ...), custom_call_target="tpu_custom_call" | custom-call | tf_op jit(solution)/shard_map/pallas_call | solution.py:931
  153.7 13.5 %shard_map.378 = (f32[3136,384]{1,0:T(8,128)}, f32[3]{0:T(128)}, f32[384,1536]{1,0:T(8,128)}, bf16[384,1536]{1,0:T(8,128)(2,1)}, f32[384,1536]{1,0:T(8,128)}, /*...) custom-call(s32[1]{0:T(128)} %bitcast.narrow_ref, ...), custom_call_target="tpu_custom_call" | custom-call | tf_op jit(solution)/shard_map/pallas_call | solution.py:1002
